TPU v7x, 32 devices: a whole 2x2x4 slice. The times are simulated.
32 devices in a mesh: section: 2 (over core), ctx: 4 (over z), fsdp: 4 (over y, x).
Axes of the slice: x: 2, y: 2, z: 4, core: 2. Of those that a mesh axis runs over, the one named last changes fastest.
Arguments:
- tokens: bfloat16 [2, 4, 512, 1024], P(None, 'fsdp', 'ctx'), may hold values from -6 to 6
- lengths: int32 [2, 4, 2], P(None, 'fsdp'), may hold values from 0 to 512, as said below
- cotangent: bfloat16 [2, 4, 512, 1024], P(None, 'fsdp', 'ctx'), may hold values from -6 to 6
- norm_one: bfloat16 [2, 1024], P('section', 'fsdp'), may hold values from 0.5 to 1.5
- qkv_weight: bfloat16 [2, 1024, 3072], P('section', 'fsdp'), may hold values from -0.1875 to 0.1875
- decay_weight: bfloat16 [2, 1024, 8], P('section', 'fsdp'), may hold values from -0.08984375 to 0.08984375
- decay_bias: bfloat16 [2, 8], P('section', 'fsdp'), may hold values from 3 to 9
- persistent: bfloat16 [2, 16, 2048], P('section', None, 'fsdp'), may hold values from -6 to 6
- out_weight: bfloat16 [2, 1024, 1024], P('section', 'fsdp'), may hold values from -0.375 to 0.375
- norm_two: bfloat16 [2, 1024], P('section', 'fsdp'), may hold values from 0.5 to 1.5
- gate_up: bfloat16 [2, 1024, 5632], P('section', 'fsdp'), may hold values from -0.1875 to 0.1875
- down_weight: bfloat16 [2, 2816, 1024], P('section', 'fsdp'), may hold values from -0.109375 to 0.109375
Outputs:
- output: bfloat16 [2, 4, 512, 1024], P('section', 'fsdp', 'ctx')
- input_grad: bfloat16 [2, 4, 512, 1024], P('section', 'fsdp', 'ctx')
- grad_norm_one: float32 [2, 1024], P('section', 'fsdp')
- grad_qkv_weight: float32 [2, 1024, 3072], P('section', 'fsdp')
- grad_decay_weight: float32 [2, 1024, 8], P('section', 'fsdp')
- grad_decay_bias: float32 [2, 8], P('section', 'fsdp')
- grad_persistent: float32 [2, 16, 2048], P('section', None, 'fsdp')
- grad_out_weight: float32 [2, 1024, 1024], P('section', 'fsdp')
- grad_norm_two: float32 [2, 1024], P('section', 'fsdp')
- grad_gate_up: float32 [2, 1024, 5632], P('section', 'fsdp')
- grad_down_weight: float32 [2, 2816, 1024], P('section', 'fsdp')
Inputs may be any that keep to these rules, and one draw needn't show every extreme that they name: `lengths`: each group's two entries sum to 512; the first is at least 128, the second is 0 or at least 128; in every group one micro-batch holds a single sequence of all 512 positions.
All inputs are finite; a program needn't handle non-finite values.
Results may differ from a plain program's by a relative error of at most 0.025.
Values may be sent and summed in bfloat16 or wider, within the bound.
No kernel may reach another device: no remote copies, remote signals or barrier semaphores. Data moves between devices by JAX's collectives and lax.ppermute only.
A program may use at most 384 MiB of HBM per device.

v0:
```python
import jax
import jax.numpy as jnp
from jax import lax
from jax.sharding import PartitionSpec as P

epsilon = 1e-05
negative = -1e30
wide = jnp.float32
half = jnp.bfloat16


def exchange(value, axis, distance):
    count = lax.axis_size(axis)
    return lax.ppermute(value, axis, [(i, i ^ distance) for i in range(count)])


def gather_parts(block, axis):
    count = lax.axis_size(axis)
    return [block] + [exchange(block, axis, r) for r in range(1, count)]


def scatter_sum(blocks, axis):
    total = blocks[0].astype(wide)
    for r in range(1, len(blocks)):
        total = total + exchange(blocks[r].astype(half), axis, r).astype(wide)
    return total


def in_order(parts, index, dim):
    count = len(parts)
    shape = list(parts[0].shape)
    size = shape[dim]
    shape[dim] = size * count
    whole = jnp.zeros(shape, parts[0].dtype)
    for r, part in enumerate(parts):
        whole = lax.dynamic_update_slice_in_dim(whole, part, (index ^ r) * size, dim)
    return whole


def columns_here(shard, kinds, axis):
    count, index = lax.axis_size(axis), lax.axis_index(axis)
    rows, width = shard.shape[0], shard.shape[1] // (kinds * count)
    blocks = shard.reshape(rows, kinds, count, width)
    parts = []
    for r in range(count):
        block = lax.dynamic_index_in_dim(blocks, index ^ r, 2, False).reshape(rows, kinds * width)
        parts.append(block if r == 0 else exchange(block, axis, r))
    return in_order(parts, index, 0)


def rows_here(columns, kinds, axis):
    count, index = lax.axis_size(axis), lax.axis_index(axis)
    rows, width = columns.shape[0] // count, columns.shape[1] // kinds
    parts = []
    for r in range(count):
        block = lax.dynamic_slice_in_dim(columns, (index ^ r) * rows, rows, 0)
        block = block if r == 0 else exchange(block, axis, r)
        parts.append(block.reshape(rows, kinds, 1, width))
    return in_order(parts, index, 2).reshape(rows, kinds * count * width)


def line_sum(value, axis):
    count, index = lax.axis_size(axis), lax.axis_index(axis)
    if count != 4:
        return lax.psum(value, axis)

    def plus(a, b):
        return (a.astype(wide) + b.astype(wide)).astype(value.dtype)

    pair = plus(value, lax.ppermute(value, axis, [(0, 1), (3, 2)]))
    total = plus(pair, lax.ppermute(pair, axis, [(1, 2), (2, 1)]))
    outer = lax.ppermute(total, axis, [(1, 0), (2, 3)])
    return jnp.where((index == 0) | (index == 3), outer, total)


def dot(a, b, contract=(1, 0)):
    return lax.dot_general(a, b, (((contract[0],), (contract[1],)), ((), ())), preferred_element_type=wide)


def normalise(values, gain):
    scale = lax.rsqrt(jnp.mean(values * values, axis=-1, keepdims=True) + epsilon)
    return (values * scale * gain).astype(half)


def normalise_back(values, gain, grad):
    scale = lax.rsqrt(jnp.mean(values * values, axis=-1, keepdims=True) + epsilon)
    unit = values * scale
    grad_gain = jnp.sum(grad * unit, axis=0)
    scaled = grad * gain
    return scale * (scaled - unit * jnp.mean(scaled * unit, axis=-1, keepdims=True)), grad_gain


def heads_first(rows, size):
    return rows.reshape(rows.shape[0], rows.shape[1] // size, size).transpose(1, 0, 2)


def rows_first(heads):
    return heads.transpose(1, 0, 2).reshape(heads.shape[1], heads.shape[0] * heads.shape[2])


def batched(a, b, contract):
    return lax.dot_general(a, b, (((contract[0],), (contract[1],)), ((0,), (0,))), preferred_element_type=wide)


def cumulative(values, positions):
    earlier = (positions[None, :] <= positions[:, None]).astype(wide)
    return jnp.dot(earlier, values, precision=lax.Precision.HIGHEST)


def mixer_parts(projected, logits, fixed, length, positions, size):
    width = projected.shape[1] // 3
    q, k, v = (heads_first(projected[:, i * width : (i + 1) * width], size) for i in range(3))
    fixed_k, fixed_v = (heads_first(fixed[:, i * width : (i + 1) * width], size) for i in range(2))
    scale = size ** (-0.5)
    documents = positions >= length
    starts = (positions == 0) | (positions == length)
    allowed = ((positions[None, :] <= positions[:, None]) & (documents[:, None] == documents[None, :]))[None]
    log_keep = jax.nn.log_sigmoid(logits)
    total_log = cumulative(log_keep, positions).T
    keep = jnp.where(starts[:, None], 0.0, jax.nn.sigmoid(logits)).T
    lose = jnp.where(starts[:, None], 1.0, jax.nn.sigmoid(-logits)).T
    inflow = jnp.sqrt(lose * (1.0 + keep))
    scores = batched(q, k, (2, 2)) * scale
    fixed_scores = batched(q, fixed_k, (2, 2)) * scale
    masked = jnp.where(allowed, scores, negative)
    top = jnp.maximum(jnp.max(masked, axis=2), jnp.max(fixed_scores, axis=2))[:, :, None]
    weights, fixed_weights = jnp.exp(masked - top), jnp.exp(fixed_scores - top)
    mass = 1.0 / (jnp.sum(weights, axis=2) + jnp.sum(fixed_weights, axis=2))[:, :, None]
    weights, fixed_weights = weights * mass, fixed_weights * mass
    fall = jnp.exp(jnp.where(allowed, total_log[:, :, None] - total_log[:, None, :], negative))
    reach = scores * fall
    both = (weights + reach * inflow[:, None, :]).astype(half)
    return q, k, v, fixed_k, fixed_v, weights, fixed_weights, fall, reach, both, keep, lose, inflow


def mixer(projected, logits, fixed, length, positions, size):
    parts = mixer_parts(projected, logits, fixed, length, positions, size)
    q, k, v, fixed_k, fixed_v, weights, fixed_weights, fall, reach, both, keep, lose, inflow = parts
    mixed = batched(both, v, (2, 1)) + batched(fixed_weights.astype(half), fixed_v, (2, 1))
    return rows_first(mixed.astype(half))


def mixer_back(projected, logits, fixed, length, positions, size, grad):
    parts = mixer_parts(projected, logits, fixed, length, positions, size)
    q, k, v, fixed_k, fixed_v, weights, fixed_weights, fall, reach, both, keep, lose, inflow = parts
    scale = size ** (-0.5)
    grad = heads_first(grad, size)
    grad_both = batched(grad, v, (2, 2))
    grad_fixed = batched(grad, fixed_v, (2, 2))
    delta = (jnp.sum(weights * grad_both, axis=2) + jnp.sum(fixed_weights * grad_fixed, axis=2))[:, :, None]
    grad_scores = (weights * (grad_both - delta) + grad_both * fall * inflow[:, None, :]).astype(half)
    grad_fixed_scores = (fixed_weights * (grad_fixed - delta)).astype(half)
    grad_q = (batched(grad_scores, k, (2, 1)) + batched(grad_fixed_scores, fixed_k, (2, 1))) * scale
    grad_k = batched(grad_scores, q, (1, 1)) * scale
    grad_v = batched(both, grad, (1, 1))
    grad_fixed_k = batched(grad_fixed_scores, q, (1, 1)) * scale
    grad_fixed_v = batched(fixed_weights.astype(half), grad, (1, 1))
    pull = grad_both * reach
    grad_inflow = jnp.sum(pull, axis=1)
    grad_total = jnp.sum(pull * inflow[:, None, :], axis=2) - inflow * grad_inflow
    later = (positions[None, :] >= positions[:, None]).astype(wide)
    grad_log = jnp.dot(grad_total, later.T, precision=lax.Precision.HIGHEST)
    lose_all = jax.nn.sigmoid(-logits).T
    grad_logits = grad_log * lose_all - grad_inflow * keep * keep * lose / inflow
    grad_projected = jnp.concatenate([rows_first(grad_q), rows_first(grad_k), rows_first(grad_v)], axis=1)
    grad_persistent = jnp.concatenate([rows_first(grad_fixed_k), rows_first(grad_fixed_v)], axis=1)
    return grad_projected.astype(half), grad_logits.T, grad_persistent


def per_device(
    tokens,
    lengths,
    cotangent,
    norm_one,
    qkv_weight,
    decay_weight,
    decay_bias,
    persistent,
    out_weight,
    norm_two,
    gate_up,
    down_weight,
):
    sections, ctx_count, fsdp_count = (lax.axis_size(a) for a in ("section", "ctx", "fsdp"))
    section, ctx, fsdp = (lax.axis_index(a) for a in ("section", "ctx", "fsdp"))
    spread = ctx_count // fsdp_count
    rows, width = tokens.shape[2:]
    heads_here = decay_bias.shape[1]
    size = width // (heads_here * fsdp_count)
    inner = heads_here * size
    first = section == 0

    def own_batch(value):
        return lax.dynamic_index_in_dim(value, section, 0, False)[0]

    pairs = [(c * fsdp_count + f, f * ctx_count + c) for c in range(ctx_count) for f in range(fsdp_count)]

    def to_plane(value):
        return lax.ppermute(value, ("ctx", "fsdp"), pairs)

    def from_plane(value):
        return lax.ppermute(value, ("ctx", "fsdp"), [(b, a) for a, b in pairs])

    x_in = to_plane(own_batch(tokens))
    g_in = to_plane(own_batch(cotangent))
    length = to_plane(own_batch(lengths))[0]

    def both_layers(own):
        other = exchange(own, "section", 1)
        return jnp.where(first, own, other), jnp.where(first, other, own)

    small = jnp.concatenate(
        [
            norm_one[0],
            norm_two[0],
            decay_weight[0].reshape(-1),
            persistent[0].reshape(-1),
        ]
    )
    small = jnp.stack(both_layers(in_order([p[None] for p in gather_parts(small, "fsdp")], fsdp, 0)))
    cut = width // fsdp_count
    sizes = [cut, cut, decay_weight[0].size, persistent[0].size]
    edges = [0]
    for piece in sizes:
        edges.append(edges[-1] + piece)
    gains_one, gains_two, decays, fixeds = (small[:, :, a:b] for a, b in zip(edges[:-1], edges[1:]))
    gains_one = gains_one.reshape(2, width).astype(wide)
    gains_two = gains_two.reshape(2, width).astype(wide)
    head_count = heads_here * fsdp_count
    decays = lax.dynamic_slice_in_dim(decays.reshape(2, width, head_count), fsdp * heads_here, heads_here, 2)
    slots = persistent.shape[1]
    fixeds = fixeds.reshape(2, fsdp_count, slots, 2 * cut).transpose(0, 2, 1, 3).reshape(2, slots, 2, fsdp_count, inner)
    fixeds = lax.dynamic_index_in_dim(fixeds, fsdp, 3, False).reshape(2, slots, 2 * inner)
    biases = jnp.stack(both_layers(decay_bias[0])).astype(wide)
    qkvs = both_layers(columns_here(qkv_weight[0], 3, "fsdp"))
    outs = both_layers(out_weight[0])
    gate_ups = both_layers(columns_here(gate_up[0], 2, "fsdp"))
    downs = both_layers(down_weight[0])
    hidden = downs[0].shape[0]

    pieces = [(k * fsdp_count + (fsdp ^ r)) * rows + jnp.arange(rows) for k in range(spread) for r in range(fsdp_count)]
    all_positions = jnp.concatenate(pieces)
    groups = [[g * spread + k for k in range(spread)] for g in range(ctx_count // spread)]

    def whole(value):
        if spread == 1:
            return value
        return lax.all_gather(value, "ctx", axis_index_groups=groups, axis=0, tiled=True)

    def own_rows(value):
        if spread == 1:
            return value
        count = value.shape[0] // spread
        return lax.dynamic_slice_in_dim(value, (ctx % spread) * count, count, 0)

    def blocks_of(value):
        return list(value.reshape(fsdp_count, rows, value.shape[1]))

    def forward(layer, x, last):
        normed = jnp.concatenate(gather_parts(normalise(x, gains_one[layer]), "fsdp"))
        projected = dot(normed, qkvs[layer]).astype(half)
        logits = dot(normed, decays[layer]) + biases[layer]
        seen, seen_logits = whole(projected), whole(logits)
        combined = own_rows(mixer(seen, seen_logits, fixeds[layer], length, all_positions, size))
        middle = x + scatter_sum(blocks_of(dot(combined, outs[layer])), "fsdp")
        normed_two = jnp.concatenate(gather_parts(normalise(middle, gains_two[layer]), "fsdp"))
        gates = dot(normed_two, gate_ups[layer])
        activated = (jax.nn.silu(gates[:, :hidden]) * gates[:, hidden:]).astype(half)
        out = middle + scatter_sum(blocks_of(dot(activated, downs[layer])), "fsdp")
        return out.astype(half), (x, normed, seen, seen_logits, combined, middle, normed_two, gates, activated)

    def backward(layer, g_out, saved):
        x, normed, seen, seen_logits, combined, middle, normed_two, gates, activated = saved
        g_rows = jnp.concatenate(gather_parts(g_out, "fsdp"))
        grad_down = dot(activated, g_rows, (0, 0))
        g_activated = dot(g_rows, downs[layer], (1, 1))
        gate, up = gates[:, :hidden], gates[:, hidden:]
        sig = jax.nn.sigmoid(gate)
        g_up = g_activated * gate * sig
        g_gate = g_activated * up * sig * (1.0 + gate * (1.0 - sig))
        g_gates = jnp.concatenate([g_gate, g_up], axis=1).astype(half)
        grad_gate_up = dot(normed_two, g_gates, (0, 0))
        g_normed_two = scatter_sum(blocks_of(dot(g_gates, gate_ups[layer], (1, 1))), "fsdp")
        g_middle, grad_norm_two = normalise_back(middle, gains_two[layer], g_normed_two)
        g_middle = g_middle + g_out.astype(wide)
        g_branch = jnp.concatenate(gather_parts(g_middle.astype(half), "fsdp"))
        grad_out = dot(combined, g_branch, (0, 0))
        g_combined = whole(dot(g_branch, outs[layer], (1, 1)).astype(half))
        g_projected, g_logits, grad_fixed = mixer_back(
            seen, seen_logits, fixeds[layer], length, all_positions, size, g_combined
        )
        g_projected, g_logits = own_rows(g_projected), own_rows(g_logits)
        grad_fixed = jnp.where(ctx % spread == 0, grad_fixed, 0.0)
        grad_qkv = dot(normed, g_projected, (0, 0))
        grad_decay = dot(normed.astype(wide), g_logits, (0, 0))
        grad_bias = jnp.sum(g_logits, axis=0)
        g_normed = dot(g_projected, qkvs[layer], (1, 1)) + dot(g_logits, decays[layer].astype(wide), (1, 1))
        g_normed = scatter_sum(blocks_of(g_normed), "fsdp")
        g_x, grad_norm_one = normalise_back(x, gains_one[layer], g_normed)
        g_x = (g_x + g_middle).astype(half)
        large = (grad_qkv, grad_out, grad_gate_up, grad_down)
        return g_x, tuple(g.astype(half) for g in large), (grad_norm_one, grad_norm_two, grad_decay, grad_bias, grad_fixed)

    between, saved_first = forward(0, x_in.astype(wide), False)
    out, saved_second = forward(1, between.astype(wide), True)
    g_between, large_second, small_second = backward(1, g_in, saved_second)
    g_input, large_first, small_first = backward(0, g_between, saved_first)

    def reduced(from_first, from_second):
        received = exchange(jnp.where(first, from_second, from_first), "section", 1)
        own = jnp.where(first, from_first, from_second)
        own = (own.astype(wide) + received.astype(wide)).astype(half)
        return line_sum(own, "ctx")

    grad_qkv, grad_out, grad_gate_up, grad_down = (reduced(a, b) for a, b in zip(large_first, large_second))
    grad_qkv = rows_here(grad_qkv, 3, "fsdp")
    grad_gate_up = rows_here(grad_gate_up, 2, "fsdp")

    def small_whole(pieces):
        n_one, n_two, decay, bias, fixed = pieces
        decay_all = lax.dynamic_update_slice_in_dim(jnp.zeros((width, head_count), wide), decay, fsdp * heads_here, 1)
        bias_all = lax.dynamic_update_slice_in_dim(jnp.zeros((head_count,), wide), bias, fsdp * heads_here, 0)
        fixed_all = jnp.zeros((slots, 2, fsdp_count, inner), wide)
        fixed_all = lax.dynamic_update_slice_in_dim(fixed_all, fixed.reshape(slots, 2, 1, inner), fsdp, 2)
        return jnp.concatenate([n_one, n_two, decay_all.reshape(-1), fixed_all.reshape(-1), bias_all])

    tiny_first, tiny_second = small_whole(small_first), small_whole(small_second)
    tiny = lax.psum(jnp.stack([tiny_first, tiny_second]), ("section", "ctx", "fsdp"))
    tiny = lax.dynamic_index_in_dim(tiny, section, 0, False)
    grad_norm_one = lax.dynamic_slice_in_dim(tiny[:width], fsdp * cut, cut, 0)
    grad_norm_two = lax.dynamic_slice_in_dim(tiny[width : 2 * width], fsdp * cut, cut, 0)
    at = 2 * width
    grad_decay = lax.dynamic_slice_in_dim(tiny[at : at + width * head_count].reshape(width, head_count), fsdp * cut, cut, 0)
    at += width * head_count
    grad_fixed = tiny[at : at + slots * 2 * width].reshape(slots, 2 * width)
    grad_fixed = lax.dynamic_slice_in_dim(grad_fixed, fsdp * 2 * cut, 2 * cut, 1)
    at += slots * 2 * width
    grad_bias = lax.dynamic_slice_in_dim(tiny[at:], fsdp * heads_here, heads_here, 0)

    return (
        from_plane(out)[None, None],
        from_plane(g_input)[None, None],
        grad_norm_one[None],
        grad_qkv.astype(wide)[None],
        grad_decay[None],
        grad_bias[None],
        grad_fixed[None],
        grad_out.astype(wide)[None],
        grad_norm_two[None],
        grad_gate_up.astype(wide)[None],
        grad_down.astype(wide)[None],
    )


def solution(mesh):
    by_row = P("section", "fsdp", None)
    by_gain = P("section", "fsdp")
    by_token = P(None, "fsdp", "ctx", None)
    by_output = P("section", "fsdp", "ctx", None)
    by_slot = P("section", None, "fsdp")
    return jax.shard_map(
        per_device,
        mesh=mesh,
        in_specs=(
            by_token,
            P(None, "fsdp", None),
            by_token,
            by_gain,
            by_row,
            by_row,
            by_gain,
            by_slot,
            by_row,
            by_gain,
            by_row,
            by_row,
        ),
        out_specs=(
            by_output,
            by_output,
            by_gain,
            by_row,
            by_row,
            by_gain,
            by_slot,
            by_row,
            by_gain,
            by_row,
            by_row,
        ),
        check_vma=False,
    )
```

profile of v0, /device:TPU:2, one launch (start us, length us, event | category | flops | bytes accessed | tf_op | source)
XLA Modules:
  0.0 833.2 jit_solution(12970916462072042730)
XLA Ops:
  56.7 6.3 collective-permute-start.10
  75.1 6.2 collective-permute-done.10
  87.8 10.4 %collective-permute-done.6 = bf16[128,1024]{1,0:T(8,128)(2,1)} collective-permute-done((bf16[128,1024]{1,0:T(8,128)(2,1)}, bf16[128,1024]{1,0:T(8,128)(2,1)}, u32[]{:S(2)}, u32[]{:S(2)}) %collective-permute-start.6) | collective-permute-done | bytes 262176 | tf_op jit(solution)/shard_map/ppermute | solution.py:14
  98.2 6.5 collective-permute-start.22
  112.4 25.8 %collective-permute-done.22 = bf16[256,1408]{1,0:T(8,128)(2,1)} collective-permute-done((bf16[256,1408]{1,0:T(8,128)(2,1)}, bf16[256,1408]{1,0:T(8,128)(2,1)}, u32[]{:S(2)}, u32[]{:S(2)}) %collective-permute-start.22) | collective-permute-done | bytes 720928 | tf_op jit(solution)/shard_map/ppermute | solution.py:14
  160.2 6.6 collective-permute-done.16
  170.8 5.6 collective-permute-done.18
  176.4 6.5 collective-permute-done.19
  192.8 5.7 collective-permute-done.26
  275.7 5.6 fusion.243
  347.1 7.0 collective-permute-done.40
  360.4 10.7 %collective-permute-start.41 = (bf16[128,1024]{1,0:T(8,128)(2,1)S(1)}, bf16[128,1024]{1,0:T(8,128)(2,1)S(1)}, u32[]{:S(2)}, u32[]{:S(2)}) collective-permute-start(bf16[128,1024]{1,0:T(8,128)(2,1)S(1)} %get-tuple-element.113), channel_id=1, source_target_pairs={{0,0},{4,1},{8,2},{12,3},{1,4},{5,5},{9,6},{13,7},{2,8},{6,9},{10,... | collective-permute-start | bytes 786440 | tf_op jit(solution)/shard_map/ppermute | solution.py:202
  437.4 7.2 collective-permute-start.80
  478.3 27.7 %collective-permute-done.80 = bf16[1024,1408]{1,0:T(8,128)(2,1)} collective-permute-done((bf16[1024,1408]{1,0:T(8,128)(2,1)}, bf16[1024,1408]{1,0:T(8,128)(2,1)}, u32[]{:S(2)}, u32[]{:S(2)}) %collective-permute-start.80) | collective-permute-done | bytes 2883616 | tf_op jit(solution)/shard_map/ppermute | solution.py:70
  519.7 21.7 %collective-permute-done.69 = bf16[1024,768]{0,1:T(8,128)(2,1)} collective-permute-done((bf16[1024,768]{0,1:T(8,128)(2,1)}, bf16[1024,768]{0,1:T(8,128)(2,1)}, u32[]{:S(2)}, u32[]{:S(2)}) %collective-permute-start.69) | collective-permute-done | bytes 1572896 | tf_op jit(solution)/shard_map/ppermute | solution.py:70
  550.1 40.8 %collective-permute-start.76 = (bf16[256,1024]{1,0:T(8,128)(2,1)S(1)}, bf16[256,1024]{1,0:T(8,128)(2,1)S(1)}, u32[]{:S(2)}, u32[]{:S(2)}) collective-permute-start(bf16[256,1024]{1,0:T(8,128)(2,1)S(1)} %add_convert_fusion.15), channel_id=1, source_target_pairs={{0,4},{12,8},{1,5},{13,9},{2,6},{14,10},{3,7},{15,11},{16,20},{28,... | collective-permute-start | bytes 1572872 | tf_op jit(solution)/shard_map/ppermute | solution.py:70
  602.6 31.0 %collective-permute-start.67 = (bf16[128,1024]{1,0:T(8,128)(2,1)}, bf16[128,1024]{1,0:T(8,128)(2,1)}, u32[]{:S(2)}, u32[]{:S(2)}) collective-permute-start(bf16[128,1024]{1,0:T(8,128)(2,1)} %fusion.57), channel_id=1, source_target_pairs={{0,0},{4,1},{8,2},{12,3},{1,4},{5,5},{9,6},{13,7},{2,8},{6,9},{10,... | collective-permute-start | bytes 786440 | tf_op jit(solution)/shard_map/ppermute | solution.py:202
  633.6 13.1 %all-reduce.2.cloned.1.call-done = f32[2,43016]{1,0:T(2,128)} async-done(((f32[2,43016]{1,0:T(2,128)}), f32[2,43016]{1,0:T(2,128)}) %all-reduce.2.cloned.1.call-update) | async-done | bytes 344144 | tf_op jit(solution)/shard_map/psum | solution.py:328
  653.3 46.7 %collective-permute-done.67 = bf16[128,1024]{1,0:T(8,128)(2,1)} collective-permute-done((bf16[128,1024]{1,0:T(8,128)(2,1)}, bf16[128,1024]{1,0:T(8,128)(2,1)}, u32[]{:S(2)}, u32[]{:S(2)}) %collective-permute-start.67) | collective-permute-done | bytes 262176 | tf_op jit(solution)/shard_map/ppermute | solution.py:202
  718.2 25.2 %collective-permute-done.89 = bf16[704,1024]{1,0:T(8,128)(2,1)S(1)} collective-permute-done((bf16[704,1024]{1,0:T(8,128)(2,1)S(1)}, bf16[704,1024]{1,0:T(8,128)(2,1)S(1)}, u32[]{:S(2)}, u32[]{:S(2)}) %collective-permute-start.89) | collective-permute-done | bytes 1441824 | tf_op jit(solution)/shard_map/ppermute | solution.py:72
  747.6 11.7 %dynamic_update_slice.96 = bf16[256,3,4,256]{3,2,1,0:T(4,128)(2,1)S(1)} dynamic-update-slice(bf16[256,3,4,256]{3,2,1,0:T(4,128)(2,1)S(1)} %broadcast_in_dim.227, bf16[256,3,1,256]{3,2,1,0:T(2,128)(2,1)S(1)} %copy.179, s32[]{:T(128)} %constant.116.clone.1, s32[]{:T(128)} %constant.116.clone.1, s32[]{:T(128)S(6)} %select_n.274, s32[]{:T(128)} %constant.116.clone.1) | dynamic-update-slice | bytes 786436 | tf_op jit(solution)/shard_map/dynamic_update_slice | solution.py:36
  766.0 11.6 %dynamic_update_slice.97 = bf16[256,3,4,256]{3,2,1,0:T(4,128)(2,1)S(1)} dynamic-update-slice(bf16[256,3,4,256]{3,2,1,0:T(4,128)(2,1)S(1)} %dynamic_update_slice.96, bf16[256,3,1,256]{3,2,1,0:T(2,128)(2,1)S(1)} %copy.180, s32[]{:T(128)} %constant.116.clone.1, s32[]{:T(128)} %constant.116.clone.1, s32[]{:T(128)S(6)} %select_n.275, s32[]{:T(128)} %constant.116.clone.1) | dynamic-update-slice | bytes 786436 | tf_op jit(solution)/shard_map/dynamic_update_slice | solution.py:36
  777.6 15.0 %dynamic_update_slice.98 = bf16[256,3,4,256]{3,2,1,0:T(4,128)(2,1)S(1)} dynamic-update-slice(bf16[256,3,4,256]{3,2,1,0:T(4,128)(2,1)S(1)} %dynamic_update_slice.97, bf16[256,3,1,256]{3,2,1,0:T(2,128)(2,1)} %copy.181, s32[]{:T(128)} %constant.116.clone.1, s32[]{:T(128)} %constant.116.clone.1, s32[]{:T(128)S(6)} %select_n.276, s32[]{:T(128)} %constant.116.clone.1) | dynamic-update-slice | bytes 786436 | tf_op jit(solution)/shard_map/dynamic_update_slice | solution.py:36
  792.6 11.7 %dynamic_update_slice.99 = bf16[256,3,4,256]{3,2,1,0:T(4,128)(2,1)S(1)} dynamic-update-slice(bf16[256,3,4,256]{3,2,1,0:T(4,128)(2,1)S(1)} %dynamic_update_slice.98, bf16[256,3,1,256]{3,2,1,0:T(2,128)(2,1)S(1)} %copy-done.36, s32[]{:T(128)} %constant.116.clone.1, s32[]{:T(128)} %constant.116.clone.1, s32[]{:T(128)S(6)} %select_n.277, s32[]{:T(128)} %constant.116.clone.1) | dynamic-update-slice | bytes 786436 | tf_op jit(solution)/shard_map/dynamic_update_slice | solution.py:36
  (844 shorter events, 449.1 us)
Async XLA Ops:
  7.2 639.5 %all-reduce.2.cloned.1.call-start = ((), (), s32[]{:S(2)}) async-start(), calls=%async_computation | async-start | bytes 690176 | tf_op jit(solution)/shard_map/psum | solution.py:328
  10.4 46.4 %collective-permute-start.2 = (bf16[10752]{0:T(1024)(128)(2,1)S(1)}, bf16[10752]{0:T(1024)(128)(2,1)S(1)}, u32[]{:S(2)}, u32[]{:S(2)}) collective-permute-start(bf16[10752]{0:T(1024)(128)(2,1)S(1)} %pad_maximum_fusion.32), channel_id=1, source_target_pairs={{0,1},{1,0},{2,3},{3,2},{4,5},{5,4},{6,7},{7,6},{8,9},{9,8},{10,11... | collective-permute-start | bytes 64520 | tf_op jit(solution)/shard_map/ppermute | solution.py:14
  10.4 53.4 %collective-permute-start.3 = (bf16[10752]{0:T(1024)(128)(2,1)S(1)}, bf16[10752]{0:T(1024)(128)(2,1)S(1)}, u32[]{:S(2)}, u32[]{:S(2)}) collective-permute-start(bf16[10752]{0:T(1024)(128)(2,1)S(1)} %pad_maximum_fusion.32), channel_id=1, source_target_pairs={{0,2},{1,3},{2,0},{3,1},{4,6},{5,7},{6,4},{7,5},{8,10},{9,11},{10,... | collective-permute-start | bytes 64520 | tf_op jit(solution)/shard_map/ppermute | solution.py:14
  12.5 53.7 %collective-permute-start.4 = (bf16[10752]{0:T(1024)(128)(2,1)S(1)}, bf16[10752]{0:T(1024)(128)(2,1)S(1)}, u32[]{:S(2)}, u32[]{:S(2)}) collective-permute-start(bf16[10752]{0:T(1024)(128)(2,1)S(1)} %pad_maximum_fusion.32), channel_id=1, source_target_pairs={{0,3},{1,2},{2,1},{3,0},{4,7},{5,6},{6,5},{7,4},{8,11},{9,10},{10,... | collective-permute-start | bytes 64520 | tf_op jit(solution)/shard_map/ppermute | solution.py:14
  14.6 55.6 %collective-permute-start = (bf16[128,1024]{1,0:T(8,128)(2,1)}, bf16[128,1024]{1,0:T(8,128)(2,1)S(1)}, u32[]{:S(2)}, u32[]{:S(2)}) collective-permute-start(bf16[128,1024]{1,0:T(8,128)(2,1)} %dynamic-slice_bitcast_fusion.3), channel_id=1, source_target_pairs={{0,0},{1,4},{2,8},{3,12},{4,1},{5,5},{6,9},{7,13},{8,2},{9,6},{10,... | collective-permute-start | bytes 786440 | tf_op jit(solution)/shard_map/ppermute | solution.py:199
  87.4 53.8 %collective-permute-start.12 = (bf16[1024,768]{0,1:T(8,128)(2,1)S(1)}, bf16[1024,768]{0,1:T(8,128)(2,1)}, u32[]{:S(2)}, u32[]{:S(2)}) collective-permute-start(bf16[1024,768]{0,1:T(8,128)(2,1)S(1)} %constant_dynamic-update-slice_fusion.14), channel_id=1, source_target_pairs={{0,16},{16,0},{1,17},{17,1},{2,18},{18,2},{3,19},{19,3},{4,20},{20... | collective-permute-start | bytes 4718600 | tf_op jit(solution)/shard_map/ppermute | solution.py:14
  379.3 53.6 %collective-permute-start.79 = (bf16[1024,1408]{1,0:T(8,128)(2,1)}, bf16[1024,1408]{1,0:T(8,128)(2,1)}, u32[]{:S(2)}, u32[]{:S(2)}) collective-permute-start(bf16[1024,1408]{1,0:T(8,128)(2,1)} %get-tuple-element.174), channel_id=1, source_target_pairs={{0,16},{16,0},{1,17},{17,1},{2,18},{18,2},{3,19},{19,3},{4,20},{20... | collective-permute-start | bytes 8650760 | tf_op jit(solution)/shard_map/ppermute | solution.py:14
  437.4 68.6 %collective-permute-start.80 = (bf16[1024,1408]{1,0:T(8,128)(2,1)}, bf16[1024,1408]{1,0:T(8,128)(2,1)}, u32[]{:S(2)}, u32[]{:S(2)}) collective-permute-start(bf16[1024,1408]{1,0:T(8,128)(2,1)} %add_convert_fusion.2), channel_id=1, source_target_pairs={{0,4},{12,8},{1,5},{13,9},{2,6},{14,10},{3,7},{15,11},{16,20},{28,... | collective-permute-start | bytes 8650760 | tf_op jit(solution)/shard_map/ppermute | solution.py:70
  463.8 49.2 %collective-permute-start.86 = (bf16[704,1024]{1,0:T(8,128)(2,1)}, bf16[704,1024]{1,0:T(8,128)(2,1)}, u32[]{:S(2)}, u32[]{:S(2)}) collective-permute-start(bf16[704,1024]{1,0:T(8,128)(2,1)} %get-tuple-element.176), channel_id=1, source_target_pairs={{0,16},{16,0},{1,17},{17,1},{2,18},{18,2},{3,19},{19,3},{4,20},{20... | collective-permute-start | bytes 4325384 | tf_op jit(solution)/shard_map/ppermute | solution.py:14
  464.4 84.3 %collective-permute-start.75 = (bf16[256,1024]{1,0:T(8,128)(2,1)}, bf16[256,1024]{1,0:T(8,128)(2,1)}, u32[]{:S(2)}, u32[]{:S(2)}) collective-permute-start(bf16[256,1024]{1,0:T(8,128)(2,1)} %get-tuple-element.172), channel_id=1, source_target_pairs={{0,16},{16,0},{1,17},{17,1},{2,18},{18,2},{3,19},{19,3},{4,20},{20... | collective-permute-start | bytes 1572872 | tf_op jit(solution)/shard_map/ppermute | solution.py:14
  475.7 65.7 %collective-permute-start.69 = (bf16[1024,768]{0,1:T(8,128)(2,1)}, bf16[1024,768]{0,1:T(8,128)(2,1)}, u32[]{:S(2)}, u32[]{:S(2)}) collective-permute-start(bf16[1024,768]{0,1:T(8,128)(2,1)} %add_convert_fusion.5), channel_id=1, source_target_pairs={{0,4},{12,8},{1,5},{13,9},{2,6},{14,10},{3,7},{15,11},{16,20},{28,... | collective-permute-start | bytes 4718600 | tf_op jit(solution)/shard_map/ppermute | solution.py:70
  515.7 75.2 %collective-permute-start.87 = (bf16[704,1024]{1,0:T(8,128)(2,1)S(1)}, bf16[704,1024]{1,0:T(8,128)(2,1)S(1)}, u32[]{:S(2)}, u32[]{:S(2)}) collective-permute-start(bf16[704,1024]{1,0:T(8,128)(2,1)S(1)} %add_convert_fusion.8), channel_id=1, source_target_pairs={{0,4},{12,8},{1,5},{13,9},{2,6},{14,10},{3,7},{15,11},{16,20},{28,... | collective-permute-start | bytes 4325384 | tf_op jit(solution)/shard_map/ppermute | solution.py:70
  544.0 50.6 %collective-permute-start.70 = (bf16[1024,768]{0,1:T(8,128)(2,1)S(1)}, bf16[1024,768]{0,1:T(8,128)(2,1)S(1)}, u32[]{:S(2)}, u32[]{:S(2)}) collective-permute-start(bf16[1024,768]{0,1:T(8,128)(2,1)S(1)} %add_convert_fusion.4), channel_id=1, source_target_pairs={{4,8},{8,4},{5,9},{9,5},{6,10},{10,6},{7,11},{11,7},{20,24},{24,20... | collective-permute-start | bytes 4718600 | tf_op jit(solution)/shard_map/ppermute | solution.py:71
  547.5 161.7 %collective-permute-start.82 = (bf16[1024,1408]{1,0:T(8,128)(2,1)S(1)}, bf16[1024,1408]{1,0:T(8,128)(2,1)}, u32[]{:S(2)}, u32[]{:S(2)}) collective-permute-start(bf16[1024,1408]{1,0:T(8,128)(2,1)S(1)} %add_convert_fusion), channel_id=1, source_target_pairs={{4,0},{8,12},{5,1},{9,13},{6,2},{10,14},{7,3},{11,15},{20,16},{24,... | collective-permute-start | bytes 8650760 | tf_op jit(solution)/shard_map/ppermute | solution.py:72
  550.1 49.0 %collective-permute-start.76 = (bf16[256,1024]{1,0:T(8,128)(2,1)S(1)}, bf16[256,1024]{1,0:T(8,128)(2,1)S(1)}, u32[]{:S(2)}, u32[]{:S(2)}) collective-permute-start(bf16[256,1024]{1,0:T(8,128)(2,1)S(1)} %add_convert_fusion.15), channel_id=1, source_target_pairs={{0,4},{12,8},{1,5},{13,9},{2,6},{14,10},{3,7},{15,11},{16,20},{28,... | collective-permute-start | bytes 1572872 | tf_op jit(solution)/shard_map/ppermute | solution.py:70
  592.7 110.0 %collective-permute-start.88 = (bf16[704,1024]{1,0:T(8,128)(2,1)}, bf16[704,1024]{1,0:T(8,128)(2,1)}, u32[]{:S(2)}, u32[]{:S(2)}) collective-permute-start(bf16[704,1024]{1,0:T(8,128)(2,1)} %add_convert_fusion.7), channel_id=1, source_target_pairs={{4,8},{8,4},{5,9},{9,5},{6,10},{10,6},{7,11},{11,7},{20,24},{24,20... | collective-permute-start | bytes 4325384 | tf_op jit(solution)/shard_map/ppermute | solution.py:71
  596.5 110.0 %collective-permute-start.71 = (bf16[1024,768]{0,1:T(8,128)(2,1)}, bf16[1024,768]{0,1:T(8,128)(2,1)}, u32[]{:S(2)}, u32[]{:S(2)}) collective-permute-start(bf16[1024,768]{0,1:T(8,128)(2,1)} %add_convert_fusion.3), channel_id=1, source_target_pairs={{4,0},{8,12},{5,1},{9,13},{6,2},{10,14},{7,3},{11,15},{20,16},{24,... | collective-permute-start | bytes 4718600 | tf_op jit(solution)/shard_map/ppermute | solution.py:72
  600.1 100.0 %collective-permute-start.77 = (bf16[256,1024]{1,0:T(8,128)(2,1)}, bf16[256,1024]{1,0:T(8,128)(2,1)}, u32[]{:S(2)}, u32[]{:S(2)}) collective-permute-start(bf16[256,1024]{1,0:T(8,128)(2,1)} %add_convert_fusion.14), channel_id=1, source_target_pairs={{4,8},{8,4},{5,9},{9,5},{6,10},{10,6},{7,11},{11,7},{20,24},{24,20... | collective-permute-start | bytes 1572872 | tf_op jit(solution)/shard_map/ppermute | solution.py:71
  602.6 97.4 %collective-permute-start.67 = (bf16[128,1024]{1,0:T(8,128)(2,1)}, bf16[128,1024]{1,0:T(8,128)(2,1)}, u32[]{:S(2)}, u32[]{:S(2)}) collective-permute-start(bf16[128,1024]{1,0:T(8,128)(2,1)} %fusion.57), channel_id=1, source_target_pairs={{0,0},{4,1},{8,2},{12,3},{1,4},{5,5},{9,6},{13,7},{2,8},{6,9},{10,... | collective-permute-start | bytes 786440 | tf_op jit(solution)/shard_map/ppermute | solution.py:202
  709.1 51.0 %collective-permute-start.73 = (bf16[256,768]{0,1:T(8,128)(2,1)}, bf16[256,768]{0,1:T(8,128)(2,1)}, u32[]{:S(2)}, u32[]{:S(2)}) collective-permute-start(bf16[256,768]{0,1:T(8,128)(2,1)} %get-tuple-element.75), channel_id=1, source_target_pairs={{0,2},{1,3},{2,0},{3,1},{4,6},{5,7},{6,4},{7,5},{8,10},{9,11},{10,... | collective-permute-start | bytes 1179656 | tf_op jit(solution)/shard_map/ppermute | solution.py:14
  709.1 53.9 %collective-permute-start.74 = (bf16[256,768]{0,1:T(8,128)(2,1)}, bf16[256,768]{0,1:T(8,128)(2,1)}, u32[]{:S(2)}, u32[]{:S(2)}) collective-permute-start(bf16[256,768]{0,1:T(8,128)(2,1)} %get-tuple-element.74), channel_id=1, source_target_pairs={{0,3},{1,2},{2,1},{3,0},{4,7},{5,6},{6,5},{7,4},{8,11},{9,10},{10,... | collective-permute-start | bytes 1179656 | tf_op jit(solution)/shard_map/ppermute | solution.py:14
  718.2 90.5 %collective-permute-start.83 = (bf16[256,1408]{1,0:T(8,128)(2,1)}, bf16[256,1408]{1,0:T(8,128)(2,1)}, u32[]{:S(2)}, u32[]{:S(2)}) collective-permute-start(bf16[256,1408]{1,0:T(8,128)(2,1)} %get-tuple-element.67), channel_id=1, source_target_pairs={{0,1},{1,0},{2,3},{3,2},{4,5},{5,4},{6,7},{7,6},{8,9},{9,8},{10,11... | collective-permute-start | bytes 2162696 | tf_op jit(solution)/shard_map/ppermute | solution.py:14
  743.4 67.5 %collective-permute-start.84 = (bf16[256,1408]{1,0:T(8,128)(2,1)}, bf16[256,1408]{1,0:T(8,128)(2,1)}, u32[]{:S(2)}, u32[]{:S(2)}) collective-permute-start(bf16[256,1408]{1,0:T(8,128)(2,1)} %get-tuple-element.66), channel_id=1, source_target_pairs={{0,2},{1,3},{2,0},{3,1},{4,6},{5,7},{6,4},{7,5},{8,10},{9,11},{10,... | collective-permute-start | bytes 2162696 | tf_op jit(solution)/shard_map/ppermute | solution.py:14
  744.5 71.0 %collective-permute-start.85 = (bf16[256,1408]{1,0:T(8,128)(2,1)}, bf16[256,1408]{1,0:T(8,128)(2,1)}, u32[]{:S(2)}, u32[]{:S(2)}) collective-permute-start(bf16[256,1408]{1,0:T(8,128)(2,1)} %get-tuple-element.65), channel_id=1, source_target_pairs={{0,3},{1,2},{2,1},{3,0},{4,7},{5,6},{6,5},{7,4},{8,11},{9,10},{10,... | collective-permute-start | bytes 2162696 | tf_op jit(solution)/shard_map/ppermute | solution.py:14
  (273 other events, 3335.2 us)
Sparse Core Ops, SparseCore 0:
  513.1 133.6 all-reduce.1
where the time goes:
time: 848 us; the launch traced here: 833 us
  waiting for transfers between devices  284 us (33%)
  starting transfers between devices  210 us (25%)
  local copies, waits for them, and re-layouts  168 us (20%)
  matrix products  90.6 us (11%)
  other arithmetic  62.4 us (7%)
  between operations  17.9 us (2%)
    ppermute x73, waiting for transfers between devices, exchange(): return lax.ppermute(value, axis, [(i, i ^ distance) for i in range(count)])  144 us
    ppermute x73, starting transfers between devices, exchange(): return lax.ppermute(value, axis, [(i, i ^ distance) for i in range(count)])  93.3 us
    dot_general x30, matrix products, dot(): lax.dot_general(a, b, (((contract[0],), (contract[1],)), ((), ())), prefe...  70.4 us
    dynamic_update_slice x20, local copies, waits for them, and re-layouts, in_order(): lax.dynamic_update_slice_in_dim(whole, part, (index ^ r) * size, dim)  65.1 us
    ppermute x4, starting transfers between devices, line_sum(): pair = plus(value, lax.ppermute(value, axis, [(0, 1), (3, 2)]))  54.5 us
    ppermute x4, waiting for transfers between devices, line_sum(): pair = plus(value, lax.ppermute(value, axis, [(0, 1), (3, 2)]))  50.8 us
    ppermute x2, waiting for transfers between devices, from_plane(): return lax.ppermute(value, ('ctx', 'fsdp'), [(b, a) for a, b in pairs])  46.7 us
    ppermute x2, starting transfers between devices, from_plane(): return lax.ppermute(value, ('ctx', 'fsdp'), [(b, a) for a, b in pairs])  41.8 us
  transfers between devices with their start and end apart: 91, of which 40 were waited for; matrix products, arithmetic and copies ran while one was open for 34% of the time, Pallas kernels for 0%

commit v1 on v0

--- a/solution.py
+++ b/solution.py
@@ -1,12 +1,925 @@
 import jax
 import jax.numpy as jnp
 from jax import lax
+from jax.experimental import pallas as pl
+from jax.experimental.pallas import tpu as pltpu
 from jax.sharding import PartitionSpec as P
 
 epsilon = 1e-05
 negative = -1e30
 wide = jnp.float32
 half = jnp.bfloat16
+LANES = 128
+PAIR = 64
+vmem = pl.BlockSpec(memory_space=pltpu.VMEM)
+smem = pl.BlockSpec(memory_space=pltpu.SMEM)
+anywhere = pl.BlockSpec(memory_space=pltpu.HBM)
+
+
+def outside(*arrays):
+    return [pltpu.with_memory_space_constraint(array, pltpu.HBM) for array in arrays]
+
+
+def mm(a, b):
+    return lax.dot_general(a, b, (((1,), (0,)), ((), ())), preferred_element_type=wide)
+
+
+def mm_nt(a, b):
+    return lax.dot_general(a, b, (((1,), (1,)), ((), ())), preferred_element_type=wide)
+
+
+def mm_tn(a, b):
+    return lax.dot_general(a, b, (((0,), (0,)), ((), ())), preferred_element_type=wide)
+
+
+def sig(v):
+    return 1.0 / (1.0 + jnp.exp(-v))
+
+
+def call(body, out_shape, in_specs, scratch, flops, moved, name):
+    return pl.pallas_call(
+        body,
+        out_shape=out_shape,
+        in_specs=in_specs,
+        out_specs=jax.tree.map(lambda _: vmem, out_shape),
+        scratch_shapes=scratch,
+        compiler_params=pltpu.CompilerParams(vmem_limit_bytes=26 * 1024 * 1024),
+        cost_estimate=pl.CostEstimate(flops=flops, bytes_accessed=moved, transcendentals=0),
+        name=name,
+    )
+
+
+def shape(dims, kind=half):
+    return jax.ShapeDtypeStruct(tuple(dims), kind)
+
+
+def pack_heads(count, shard, place):
+    rows, columns = shard.shape
+    inner = columns // (3 * count)
+
+    def body(place_ref, shard_ref, *outs):
+        for r in range(count):
+            target = place_ref[0] ^ r
+            for kind in range(3):
+                at = pl.multiple_of(kind * count * inner + target * inner, inner)
+                outs[r][:, kind * inner : (kind + 1) * inner] = shard_ref[:, pl.ds(at, inner)]
+
+    outs = [shape((rows, 3 * inner))] * count
+    return call(body, outs, [smem, vmem], [], 0, 2 * shard.size * 2, "pack_heads")(place, shard)
+
+
+def pack_gates(count, shard, place):
+    rows, columns = shard.shape
+    hidden = columns // 2
+    mine = columns // count
+
+    def body(place_ref, shard_ref, *rest):
+        outs, mixed = rest[:count], rest[count]
+        low = lax.broadcasted_iota(jnp.int32, (rows, LANES), 1) < PAIR
+        for m in range(hidden // LANES):
+            gate = shard_ref[:, m * LANES : (m + 1) * LANES].astype(wide)
+            up = shard_ref[:, hidden + m * LANES : hidden + (m + 1) * LANES].astype(wide)
+            even = jnp.where(low, gate, pltpu.roll(up, PAIR, 1))
+            odd = jnp.where(low, pltpu.roll(gate, PAIR, 1), up)
+            mixed[:, 2 * m * LANES : (2 * m + 1) * LANES] = even.astype(half)
+            mixed[:, (2 * m + 1) * LANES : (2 * m + 2) * LANES] = odd.astype(half)
+        for r in range(count):
+            at = pl.multiple_of((place_ref[0] ^ r) * mine, LANES)
+            outs[r][...] = mixed[:, pl.ds(at, mine)]
+
+    outs = [shape((rows, mine))] * count
+    scratch = [pltpu.VMEM((rows, columns), half)]
+    return call(body, outs, [smem, vmem], scratch, 0, 2 * shard.size * 2, "pack_gates")(place, shard)
+
+
+class Loader:
+    def __init__(self, place_ref, layer, sems):
+        self.place, self.layer, self.sems, self.used, self.waits = place_ref, layer, sems, 0, []
+
+    def start(self, mine, other, target, relative=False):
+        handles = []
+        rows = mine[0].shape[0]
+        for r in range(len(mine)):
+            at = r * rows if relative else pl.multiple_of((self.place[0] ^ r) * rows, rows)
+            where = target.at[pl.ds(at, rows)]
+            sem = self.sems.at[self.used]
+            self.used += 1
+
+            @pl.when(self.place[1] == self.layer)
+            def _(r=r, where=where, sem=sem):
+                pltpu.make_async_copy(mine[r], where, sem).start()
+
+            @pl.when(self.place[1] != self.layer)
+            def _(r=r, where=where, sem=sem):
+                pltpu.make_async_copy(other[r], where, sem).start()
+
+            handles.append(pltpu.make_async_copy(mine[r], where, sem))
+        return handles
+
+
+def finish(handles):
+    for handle in handles:
+        handle.wait()
+
+
+def put_rows(parts, target, place_ref):
+    rows = parts[0].shape[0]
+    for r, part in enumerate(parts):
+        target[pl.ds(pl.multiple_of((place_ref[0] ^ r) * rows, rows), rows), :] = part[...]
+
+
+def take_rows(source, outs, place_ref):
+    rows = outs[0].shape[0]
+    for r, out in enumerate(outs):
+        out[...] = source[pl.ds(pl.multiple_of((place_ref[0] ^ r) * rows, rows), rows), :].astype(out.dtype)
+
+
+def three_way(v):
+    high = v.astype(half)
+    rest = v - high.astype(wide)
+    middle = rest.astype(half)
+    return high, middle, (rest - middle.astype(wide)).astype(half)
+
+
+def exact_sum(mask, values):
+    return sum(mm(mask, piece) for piece in three_way(values))
+
+
+def gate_rows(logits, length, rows):
+    at = lax.broadcasted_iota(jnp.int32, (rows, LANES), 0)
+    starts = (at == 0) | (at == length)
+    spill = jnp.log(1.0 + jnp.exp(-jnp.abs(logits)))
+    log_keep = jnp.minimum(logits, 0.0) - spill
+    keep = jnp.where(starts, 0.0, sig(logits))
+    lose = jnp.where(starts, 1.0, sig(-logits))
+    return log_keep, keep, lose
+
+
+def totals(log_keep, rows):
+    below = lax.broadcasted_iota(jnp.int32, (rows, rows), 1) <= lax.broadcasted_iota(jnp.int32, (rows, rows), 0)
+    return exact_sum(below.astype(wide).astype(half), log_keep)
+
+
+def block_scores(i, block, head, size, inner, projected, fixed, total, total_t, inflow_t, length, scale):
+    n = (i + 1) * block
+    rows = slice(i * block, n)
+    lanes = slice(head * size, (head + 1) * size)
+    q = projected[rows, lanes]
+    k = projected[0:n, inner + head * size : inner + (head + 1) * size]
+    v = projected[0:n, 2 * inner + head * size : 2 * inner + (head + 1) * size]
+    fixed_k = fixed[:, lanes]
+    fixed_v = fixed[:, inner + head * size : inner + (head + 1) * size]
+    scores = mm_nt(q, k) * scale
+    fixed_scores = mm_nt(q, fixed_k) * scale
+    at = i * block + lax.broadcasted_iota(jnp.int32, (block, 1), 0)
+    begin = jnp.where(at >= length, length, 0)
+    column = lax.broadcasted_iota(jnp.int32, (block, n), 1)
+    allowed = (column <= at) & (column >= begin)
+    masked = jnp.where(allowed, scores, negative)
+    top = jnp.maximum(jnp.max(masked, axis=1, keepdims=True), jnp.max(fixed_scores, axis=1, keepdims=True))
+    weights, fixed_weights = jnp.exp(masked - top), jnp.exp(fixed_scores - top)
+    mass = 1.0 / (jnp.sum(weights, axis=1, keepdims=True) + jnp.sum(fixed_weights, axis=1, keepdims=True))
+    weights, fixed_weights = weights * mass, fixed_weights * mass
+    fall = jnp.exp(jnp.where(allowed, total[rows, head : head + 1] - total_t[head : head + 1, 0:n], negative))
+    reach = scores * fall
+    both = (weights + reach * inflow_t[head : head + 1, 0:n]).astype(half)
+    return q, k, v, fixed_k, fixed_v, weights, fixed_weights, fall, reach, both
+
+
+def mix_forward(layer, heads, size, place, parts, qkv_mine, qkv_other, out_mine, out_other, decay, bias, fixed):
+    count = len(parts)
+    rows, width = parts[0].shape
+    total_rows, inner = rows * count, heads * size
+    scale = size ** (-0.5)
+    block = rows
+
+    def body(place_ref, *refs):
+        parts_in, mine, other = refs[:count], refs[count : 2 * count], refs[2 * count : 3 * count]
+        o_mine, o_other, refs = refs[3 * count : 3 * count + 1], refs[3 * count + 1 : 3 * count + 2], refs[3 * count + 2 :]
+        decay_ref, bias_ref, fixed_ref, refs = refs[0], refs[1], refs[2], refs[3:]
+        terms, refs = refs[:count], refs[count:]
+        combined, normed, projected, logits_out, weight, out_weight, whole, sems = refs
+        loader = Loader(place_ref, layer, sems)
+        handles = loader.start(mine, other, weight)
+        out_handles = loader.start(o_mine, o_other, out_weight, relative=True)
+        put_rows(parts_in, normed, place_ref)
+        length = place_ref[2]
+        logits = mm(normed[...], decay_ref[...]) + bias_ref[...]
+        logits_out[...] = logits
+        log_keep, keep, lose = gate_rows(logits, length, total_rows)
+        total = totals(log_keep, total_rows)
+        total_t = total.T
+        inflow_t = jnp.sqrt(lose * (1.0 + keep)).T
+        finish(handles)
+        for kind in range(3):
+            lanes = slice(kind * inner, (kind + 1) * inner)
+            projected[:, lanes] = mm(normed[...], weight[:, lanes]).astype(half)
+        for head in range(heads):
+            for i in range(count):
+                q, k, v, fixed_k, fixed_v, weights, fixed_weights, fall, reach, both = block_scores(
+                    i, block, head, size, inner, projected, fixed_ref, total, total_t, inflow_t, length, scale
+                )
+                mixed = mm(both, v) + mm(fixed_weights.astype(half), fixed_v)
+                combined[i * block : (i + 1) * block, head * size : (head + 1) * size] = mixed.astype(half)
+        finish(out_handles)
+        whole[...] = mm(combined[...], out_weight[...])
+        take_rows(whole, terms, place_ref)
+
+    outs = [shape((rows, width), wide if r == 0 else half) for r in range(count)] + [
+        shape((total_rows, inner)),
+        shape((total_rows, width)),
+        shape((total_rows, 3 * inner)),
+        shape((total_rows, LANES), wide),
+    ]
+    scratch = [
+        pltpu.VMEM((width, 3 * inner), half),
+        pltpu.VMEM((inner, width), half),
+        pltpu.VMEM((total_rows, width), wide),
+        pltpu.SemaphoreType.DMA((count + 1,)),
+    ]
+    specs = [smem] + [vmem] * count + [anywhere] * (2 * count + 2) + [vmem] * 3
+    flops = 2 * total_rows * (width * 4 * inner + inner * total_rows * 2)
+    moved = 2 * (width * 3 * inner + total_rows * (2 * width + 4 * inner))
+    return call(body, outs, specs, scratch, flops, moved, "mix_forward")(
+        place, *parts, *outside(*qkv_mine, *qkv_other, out_mine, out_other), decay, bias, fixed
+    )
+
+
+def mix_backward(layer, heads, size, place, parts, out_mine, out_other, qkv_mine, qkv_other, decay, fixed, projected, logits, normed, gain):
+    count = len(parts)
+    rows, width = parts[0].shape
+    total_rows, inner = rows * count, heads * size
+    scale = size ** (-0.5)
+    block = rows
+
+    def body(place_ref, *refs):
+        parts_in, refs = refs[:count], refs[count:]
+        o_mine, o_other, refs = refs[:1], refs[1:2], refs[2:]
+        mine, other, refs = refs[:count], refs[count : 2 * count], refs[2 * count :]
+        decay_ref, fixed_ref, projected, logits_ref, normed_ref, gain_ref = refs[:6]
+        refs = refs[6:]
+        terms, refs = refs[:count], refs[count:]
+        branch, g_projected, g_logits_out, g_fixed, g_gain, refs = refs[0], refs[1], refs[2], refs[3], refs[4], refs[5:]
+        weight, out_weight, combined, g_k, g_v, pulled, pushed, whole, sems = refs
+        loader = Loader(place_ref, layer, sems)
+        out_handles = loader.start(o_mine, o_other, out_weight, relative=True)
+        handles = loader.start(mine, other, weight)
+        put_rows(parts_in, branch, place_ref)
+        length = place_ref[2]
+        logits = logits_ref[...]
+        log_keep, keep, lose = gate_rows(logits, length, total_rows)
+        total = totals(log_keep, total_rows)
+        total_t = total.T
+        inflow = jnp.sqrt(lose * (1.0 + keep))
+        inflow_t = inflow.T
+        finish(out_handles)
+        combined[...] = mm_nt(branch[...], out_weight[...]).astype(half)
+        g_k[...] = jnp.zeros_like(g_k)
+        g_v[...] = jnp.zeros_like(g_v)
+        pulled[...] = jnp.zeros_like(pulled)
+        pushed[...] = jnp.zeros_like(pushed)
+        g_fixed[...] = jnp.zeros_like(g_fixed)
+        for head in range(heads):
+            lanes = slice(head * size, (head + 1) * size)
+            for i in range(count):
+                n = (i + 1) * block
+                here = slice(i * block, n)
+                q, k, v, fixed_k, fixed_v, weights, fixed_weights, fall, reach, both = block_scores(
+                    i, block, head, size, inner, projected, fixed_ref, total, total_t, inflow_t, length, scale
+                )
+                grad = combined[here, lanes]
+                g_both = mm_nt(grad, v)
+                g_few = mm_nt(grad, fixed_v)
+                delta = jnp.sum(weights * g_both, axis=1, keepdims=True) + jnp.sum(
+                    fixed_weights * g_few, axis=1, keepdims=True
+                )
+                inflow_row = inflow_t[head : head + 1, 0:n]
+                g_scores = (weights * (g_both - delta) + g_both * fall * inflow_row).astype(half)
+                g_few_scores = (fixed_weights * (g_few - delta)).astype(half)
+                g_projected[here, lanes] = ((mm(g_scores, k) + mm(g_few_scores, fixed_k)) * scale).astype(half)
+                g_k[0:n, lanes] += mm_tn(g_scores, q)
+                g_v[0:n, lanes] += mm_tn(both, grad)
+                g_fixed[:, lanes] += mm_tn(g_few_scores, q) * scale
+                g_fixed[:, inner + head * size : inner + (head + 1) * size] += mm_tn(fixed_weights.astype(half), grad)
+                pull = g_both * reach
+                pulled[head : head + 1, 0:n] += jnp.sum(pull, axis=0, keepdims=True)
+                pushed[here, head : head + 1] = jnp.sum(pull * inflow_row, axis=1, keepdims=True)
+        g_projected[:, inner : 2 * inner] = (g_k[...] * scale).astype(half)
+        g_projected[:, 2 * inner : 3 * inner] = g_v[...].astype(half)
+        g_inflow = jnp.concatenate([pulled[...], jnp.zeros((LANES - 8, total_rows), wide)], axis=0).T
+        g_total = pushed[...] - inflow * g_inflow
+        above = lax.broadcasted_iota(jnp.int32, (total_rows, total_rows), 1) >= lax.broadcasted_iota(
+            jnp.int32, (total_rows, total_rows), 0
+        )
+        g_log = exact_sum(above.astype(wide).astype(half), g_total)
+        g_logits = g_log * sig(-logits) - g_inflow * keep * keep * lose / inflow
+        lane = lax.broadcasted_iota(jnp.int32, (total_rows, LANES), 1)
+        g_logits = jnp.where(lane < heads, g_logits, 0.0)
+        g_logits_out[...] = g_logits
+        finish(handles)
+        high, middle, low = three_way(g_logits)
+        whole[...] = (
+            mm_nt(g_projected[...], weight[...]) + mm_nt(high, decay_ref[...]) + mm_nt(middle, decay_ref[...])
+        )
+        pulls = jnp.sum(whole[...] * normed_ref[...].astype(wide), axis=0, keepdims=True) / gain_ref[...]
+        g_gain[...] = jnp.broadcast_to(pulls, g_gain.shape)
+        take_rows(whole, terms, place_ref)
+
+    outs = [shape((rows, width), wide if r == 0 else half) for r in range(count)] + [
+        shape((total_rows, width)),
+        shape((total_rows, 3 * inner)),
+        shape((total_rows, LANES), wide),
+        shape((fixed.shape[0], 2 * inner), wide),
+        shape((8, width), wide),
+    ]
+    scratch = [
+        pltpu.VMEM((width, 3 * inner), half),
+        pltpu.VMEM((inner, width), half),
+        pltpu.VMEM((total_rows, inner), half),
+        pltpu.VMEM((total_rows, inner), wide),
+        pltpu.VMEM((total_rows, inner), wide),
+        pltpu.VMEM((8, total_rows), wide),
+        pltpu.VMEM((total_rows, LANES), wide),
+        pltpu.VMEM((total_rows, width), wide),
+        pltpu.SemaphoreType.DMA((count + 1,)),
+    ]
+    specs = [smem] + [vmem] * count + [anywhere] * 2 + [anywhere] * (2 * count) + [vmem] * 6
+    flops = 2 * total_rows * (width * 4 * inner + inner * total_rows * 5)
+    moved = 2 * (width * 4 * inner + total_rows * (5 * width + 6 * inner))
+    return call(body, outs, specs, scratch, flops, moved, "mix_backward")(
+        place, *parts, *outside(out_mine, out_other, *qkv_mine, *qkv_other), decay, fixed, projected, logits, normed, gain
+    )
+
+
+def gates_of(tile_pair):
+    rows, columns = tile_pair.shape
+    if columns == LANES:
+        return tile_pair[:, :PAIR], pltpu.roll(tile_pair, PAIR, 1)[:, :PAIR]
+    first, second = tile_pair[:, :LANES], tile_pair[:, LANES:]
+    low = lax.broadcasted_iota(jnp.int32, (rows, LANES), 1) < PAIR
+    gate = jnp.where(low, first, pltpu.roll(second, PAIR, 1))
+    up = jnp.where(low, pltpu.roll(first, PAIR, 1), second)
+    return gate, up
+
+
+def tiles_of(gate, up):
+    rows, columns = gate.shape
+    if columns == PAIR:
+        return jnp.concatenate([gate, up], axis=1)
+    low = lax.broadcasted_iota(jnp.int32, (rows, LANES), 1) < PAIR
+    first = jnp.where(low, gate, pltpu.roll(up, PAIR, 1))
+    second = jnp.where(low, pltpu.roll(gate, PAIR, 1), up)
+    return jnp.concatenate([first, second], axis=1)
+
+
+def tile_ranges(columns):
+    return [(at, min(2 * LANES, columns - at)) for at in range(0, columns, 2 * LANES)]
+
+
+def feed_forward(layer, place, parts, gu_mine, gu_other, down_mine, down_other):
+    count = len(parts)
+    rows, width = parts[0].shape
+    total_rows = rows * count
+    columns, hidden = gu_mine[0].shape[1], down_mine.shape[0]
+    padded = -(-hidden // LANES) * LANES
+
+    def body(place_ref, *refs):
+        parts_in, refs = refs[:count], refs[count:]
+        mine, other, refs = refs[:count], refs[count : 2 * count], refs[2 * count :]
+        d_mine, d_other, refs = refs[:1], refs[1:2], refs[2:]
+        terms, normed, refs = refs[:count], refs[count], refs[count + 1 :]
+        weight, down, active, whole, sems = refs
+        loader = Loader(place_ref, layer, sems)
+        handles = loader.start(mine, other, weight)
+        down_handles = loader.start(d_mine, d_other, down, relative=True)
+        put_rows(parts_in, normed, place_ref)
+        if padded != hidden:
+            down[hidden:, :] = jnp.zeros((padded - hidden, width), half)
+            active[:, padded - LANES :] = jnp.zeros((total_rows, LANES), half)
+        finish(handles)
+        for at, size in tile_ranges(columns):
+            gate, up = gates_of(mm(normed[...], weight[:, at : at + size]))
+            active[:, at // 2 : (at + size) // 2] = (gate * sig(gate) * up).astype(half)
+        finish(down_handles)
+        whole[...] = mm(active[...], down[...])
+        take_rows(whole, terms, place_ref)
+
+    outs = [shape((rows, width), wide if r == 0 else half) for r in range(count)] + [shape((total_rows, width))]
+    scratch = [
+        pltpu.VMEM((width, columns), half),
+        pltpu.VMEM((padded, width), half),
+        pltpu.VMEM((total_rows, padded), half),
+        pltpu.VMEM((total_rows, width), wide),
+        pltpu.SemaphoreType.DMA((count + 1,)),
+    ]
+    specs = [smem] + [vmem] * count + [anywhere] * (2 * count + 2)
+    flops = 2 * total_rows * width * (columns + hidden)
+    moved = 2 * (width * (columns + hidden) + total_rows * 4 * width)
+    return call(body, outs, specs, scratch, flops, moved, "feed_forward")(
+        place, *parts, *outside(*gu_mine, *gu_other, down_mine, down_other)
+    )
+
+
+def feed_backward(layer, place, parts, normed_two, gain, gu_mine, gu_other, down_mine, down_other):
+    count = len(parts)
+    rows, width = parts[0].shape
+    total_rows = rows * count
+    columns, hidden = gu_mine[0].shape[1], down_mine.shape[0]
+    padded = -(-hidden // LANES) * LANES
+
+    def body(place_ref, *refs):
+        parts_in, refs = refs[:count], refs[count:]
+        normed, gain_ref, refs = refs[0], refs[1], refs[2:]
+        mine, other, refs = refs[:count], refs[count : 2 * count], refs[2 * count :]
+        d_mine, d_other, refs = refs[:1], refs[1:2], refs[2:]
+        terms, refs = refs[:count], refs[count:]
+        g_out, g_gates, active, g_gain, refs = refs[0], refs[1], refs[2], refs[3], refs[4:]
+        weight, down, whole, sems = refs
+        loader = Loader(place_ref, layer, sems)
+        handles = loader.start(mine, other, weight)
+        down_handles = loader.start(d_mine, d_other, down, relative=True)
+        put_rows(parts_in, g_out, place_ref)
+        finish(handles)
+        finish(down_handles)
+        for at, size in tile_ranges(columns):
+            inside = slice(at // 2, (at + size) // 2)
+            gate, up = gates_of(mm(normed[...], weight[:, at : at + size]))
+            g_active = mm_nt(g_out[...], down[inside, :])
+            open_ = sig(gate)
+            lit = gate * open_
+            active[:, inside] = (lit * up).astype(half)
+            g_up = g_active * lit
+            g_gate = g_active * up * (open_ * (1.0 + gate - lit))
+            g_gates[:, at : at + size] = tiles_of(g_gate, g_up).astype(half)
+        whole[...] = mm_nt(g_gates[...], weight[...])
+        pulls = jnp.sum(whole[...] * normed[...].astype(wide), axis=0, keepdims=True) / gain_ref[...]
+        g_gain[...] = jnp.broadcast_to(pulls, g_gain.shape)
+        take_rows(whole, terms, place_ref)
+
+    outs = [shape((rows, width), wide if r == 0 else half) for r in range(count)] + [
+        shape((total_rows, width)),
+        shape((total_rows, columns)),
+        shape((total_rows, hidden)),
+        shape((8, width), wide),
+    ]
+    scratch = [
+        pltpu.VMEM((width, columns), half),
+        pltpu.VMEM((hidden, width), half),
+        pltpu.VMEM((total_rows, width), wide),
+        pltpu.SemaphoreType.DMA((count + 1,)),
+    ]
+    specs = [smem] + [vmem] * (count + 2) + [anywhere] * (2 * count + 2)
+    flops = 2 * total_rows * width * (2 * columns + hidden)
+    moved = 2 * (width * (columns + hidden) + total_rows * (6 * width + columns + hidden))
+    return call(body, outs, specs, scratch, flops, moved, "feed_backward")(
+        place, *parts, normed_two, gain, *outside(*gu_mine, *gu_other, down_mine, down_other)
+    )
+
+
+def pack_small(norm_one, norm_two, decay, bias, persistent, lengths):
+    cut, heads_all = decay.shape
+    slots, columns = persistent.shape
+    heads = bias.shape[1]
+    lanes = cut // LANES
+    total = 16 * (1 + lanes + columns // LANES)
+
+    batches = lengths.shape[0]
+
+    def body(lengths_ref, one_ref, two_ref, decay_ref, bias_ref, fixed_ref, out):
+        rows = [ref[0:1, b * LANES : (b + 1) * LANES].astype(wide) for ref in (one_ref, two_ref) for b in range(lanes)]
+        rows.append(jnp.concatenate([bias_ref[...].astype(wide), jnp.zeros((1, LANES - heads), wide)], axis=1))
+        for m in range(batches):
+            for part in (lengths_ref[m] // 64, lengths_ref[m] % 64):
+                rows.append(jnp.full((1, LANES), part.astype(wide)))
+        rows.append(jnp.zeros((16 - len(rows), LANES), wide))
+        out[0:16, :] = jnp.concatenate(rows, axis=0).astype(half)
+        padded = jnp.concatenate([decay_ref[...].astype(wide), jnp.zeros((cut, LANES - heads_all), wide)], axis=1).T
+        for b in range(lanes):
+            out[16 * (1 + b) : 16 * (2 + b), :] = padded[0:16, b * LANES : (b + 1) * LANES].astype(half)
+        for c in range(columns // LANES):
+            at = 16 * (1 + lanes + c)
+            out[at : at + slots, :] = fixed_ref[:, c * LANES : (c + 1) * LANES]
+
+    return call(body, [shape((total, LANES))], [smem] + [vmem] * 5, [], 0, 1 << 17, "pack_small")(
+        lengths, norm_one, norm_two, decay, bias, persistent
+    )[0]
+
+
+def unpack_small(heads, slots, width, place, parts):
+    count = len(parts)
+    rows = parts[0].shape[0] // 2
+    cut = width // count
+    lanes = cut // LANES
+    inner = heads * LANES
+
+    def body(place_ref, *refs):
+        ins, outs, length, held = refs[:count], refs[count:-2], refs[-2], refs[-1]
+        f = place_ref[0]
+        for r, part in enumerate(ins):
+            for k in range(2):
+                layer = place_ref[1] if k == 0 else 1 - place_ref[1]
+                held[layer, f ^ r] = part[k * rows : (k + 1) * rows, :].astype(wide)
+        at = 2 * lanes + 1 + 2 * place_ref[1]
+        found = held[place_ref[1], place_ref[2], pl.ds(at, 2), :]
+        length[...] = jnp.broadcast_to(found[0:1] * 64.0 + found[1:2], length.shape).astype(jnp.int32)
+        for layer in range(2):
+            one, two, decay, bias, fixed = outs[5 * layer : 5 * layer + 5]
+            for t in range(count):
+                for b in range(lanes):
+                    at = t * cut + b * LANES
+                    one[0:1, at : at + LANES] = held[layer, t, b : b + 1, :]
+                    two[0:1, at : at + LANES] = held[layer, t, lanes + b : lanes + b + 1, :]
+                    group = held[layer, t, 16 * (1 + b) : 16 * (2 + b), :]
+                    row = lax.broadcasted_iota(jnp.int32, (16, LANES), 0)
+                    mine = [
+                        jnp.sum(jnp.where(row == f * heads + h, group, 0.0), axis=0, keepdims=True) for h in range(heads)
+                    ]
+                    mine.append(jnp.zeros((LANES - heads, LANES), wide))
+                    decay[at : at + LANES, :] = jnp.concatenate(mine, axis=0).T.astype(half)
+            bias[...] = held[layer, f, 2 * lanes : 2 * lanes + 1, :]
+            for kind in range(2):
+                source = kind * (count // 2) + f // 2
+                for h in range(heads):
+                    at = pl.multiple_of(16 * (1 + lanes + (f % 2) * heads + h), 16)
+                    lane = kind * inner + h * LANES
+                    fixed[:, lane : lane + LANES] = held[layer, source, pl.ds(at, slots), :].astype(half)
+
+    outs = [
+        shape((1, width), wide),
+        shape((1, width), wide),
+        shape((width, LANES)),
+        shape((1, LANES), wide),
+        shape((slots, 2 * inner)),
+    ] * 2 + [shape((8, LANES), jnp.int32)]
+    scratch = [pltpu.VMEM((2, count, rows, LANES), wide)]
+    made = call(body, outs, [smem] + [vmem] * count, scratch, 0, 1 << 20, "unpack_small")(place, *parts)
+    return [list(pair) for pair in zip(made[:5], made[5:10])], made[10][0, 0]
+
+
+def join_forward(rounded, terms, residual, gain):
+    dims = terms[0].shape
+
+    def body(*refs):
+        count = len(terms)
+        residual_ref, refs_in = refs[count], refs[:count]
+        total = residual_ref[...].astype(wide)
+        for ref in refs_in:
+            total = total + ref[...].astype(wide)
+        if gain is None:
+            refs[count + 1][...] = total.astype(half)
+            return
+        gain_ref, out, normed = refs[count + 1 :]
+        if rounded:
+            total = total.astype(half).astype(wide)
+        out[...] = total.astype(out.dtype)
+        scale = lax.rsqrt(jnp.mean(total * total, axis=1, keepdims=True) + epsilon)
+        normed[...] = (total * scale * gain_ref[...]).astype(half)
+
+    outs = [shape(dims, half if rounded else wide), shape(dims)]
+    inputs = [*terms, residual, gain]
+    if gain is None:
+        outs, inputs = [shape(dims)], inputs[:-1]
+    return call(body, outs, [vmem] * len(inputs), [], 0, dims[0] * dims[1] * 20, "join_forward")(*inputs)
+
+
+def norm_rows(values, gain):
+    def body(values_ref, gain_ref, normed):
+        total = values_ref[...].astype(wide)
+        scale = lax.rsqrt(jnp.mean(total * total, axis=1, keepdims=True) + epsilon)
+        normed[...] = (total * scale * gain_ref[...]).astype(half)
+
+    return call(body, [shape(values.shape)], [vmem, vmem], [], 0, values.size * 4, "norm_rows")(values, gain)[0]
+
+
+def join_backward(terms, values, gain, onward):
+    dims = terms[0].shape
+
+    def body(*refs):
+        count = len(terms)
+        values_ref, gain_ref, onward_ref, out, rounded = refs[count:]
+        grad = refs[0][...].astype(wide)
+        for ref in refs[1:count]:
+            grad = grad + ref[...].astype(wide)
+        v = values_ref[...].astype(wide)
+        scale = lax.rsqrt(jnp.mean(v * v, axis=1, keepdims=True) + epsilon)
+        unit = v * scale
+        scaled = grad * gain_ref[...]
+        through = scale * (scaled - unit * jnp.mean(scaled * unit, axis=1, keepdims=True))
+        total = onward_ref[...].astype(wide) + through
+        out[...] = total
+        rounded[...] = total.astype(half)
+
+    outs = [shape(dims, wide), shape(dims)]
+    inputs = [*terms, values, gain, onward]
+    return call(body, outs, [vmem] * len(inputs), [], 0, dims[0] * dims[1] * 24, "join_backward")(*inputs)
+
+
+SMALL = 16
+
+
+def lane_half(source, target, which, count):
+    for t in range(count):
+        at = pl.multiple_of(t * 2 * LANES + which * LANES, LANES)
+        target[:, t * LANES : (t + 1) * LANES] = source[:, pl.ds(at, LANES)]
+
+
+def packer(packed, received):
+    def put(at, value):
+        rows = value.shape[0]
+        if received is not None:
+            value = value + received[at : at + rows, :].astype(wide)
+        packed[at : at + rows, :] = value.astype(half)
+
+    return put
+
+
+def small_rows(rows):
+    found = jnp.concatenate(rows, axis=0)
+    return jnp.concatenate([found, jnp.zeros((SMALL - found.shape[0], LANES), wide)], axis=0)
+
+
+def grad_call(body, chunks, total, inputs, received, scratch, flops, name):
+    outs = [shape((b - a, LANES)) for a, b in split_rows(total, chunks)]
+    if received is not None:
+        inputs = inputs + [received]
+    scratch = scratch + [pltpu.VMEM((total, LANES), half)]
+    moved = sum(v.size * v.dtype.itemsize for v in inputs) + total * LANES * 2
+    return call(body, outs, [smem] + [vmem] * (len(inputs) - 1), scratch, flops, moved, name)(*inputs)
+
+
+def grad_feed(chunks, count, place, normed, g_gates, active, g_out, g_gain, received=None):
+    total_rows, width = normed.shape
+    columns, hidden = g_gates.shape[1], active.shape[1]
+    tiles = columns // LANES
+    block = columns + SMALL
+    side = width // 2
+
+    def body(place_ref, normed_ref, gates_ref, active_ref, g_out_ref, gain_ref, *refs):
+        left, packed = refs[-2:]
+        got, outs = (None, refs[:-2]) if received is None else (refs[0], refs[1:-2])
+        which = 1 - place_ref[1] if received is None else place_ref[1]
+        put = packer(packed, got)
+        lane_half(normed_ref, left, which, count)
+        turned = left[...].T
+        for at in range(0, columns, 2 * LANES):
+            size = min(2 * LANES, columns - at)
+            tile = mm(turned, gates_ref[:, at : at + size])
+            for t in range(count):
+                for c in range(size // LANES):
+                    put(t * block + at + c * LANES, tile[t * LANES : (t + 1) * LANES, c * LANES : (c + 1) * LANES])
+        for t in range(count):
+            at = pl.multiple_of(t * 2 * LANES + which * LANES, LANES)
+            put(t * block + columns, small_rows([gain_ref[0:1, pl.ds(at, LANES)]]))
+        active_t = active_ref[...].T
+        for c in range(0, side // LANES, 2):
+            at = pl.multiple_of(which * side + c * LANES, LANES)
+            tile = mm(active_t, g_out_ref[:, pl.ds(at, 2 * LANES)])
+            put(count * block + c * hidden, tile[:, :LANES])
+            put(count * block + (c + 1) * hidden, tile[:, LANES:])
+        chunk_out(packed, outs)
+
+    local = (side // LANES) * hidden
+    inputs = [place, normed, g_gates, active, g_out, g_gain]
+    scratch = [pltpu.VMEM((total_rows, side), half)]
+    flops = total_rows * width * (columns + hidden)
+    return grad_call(body, chunks, count * block + local, inputs, received, scratch, flops, "grad_feed")
+
+
+def grad_mix(chunks, count, place, normed, g_projected, combined, branch, g_logits, g_gain, g_fixed, received=None):
+    total_rows, width = normed.shape
+    columns, inner = g_projected.shape[1], combined.shape[1]
+    heads = inner // LANES
+    slots = g_fixed.shape[0]
+    block = columns + SMALL + slots
+    side = width // 2
+
+    def body(place_ref, normed_ref, proj_ref, comb_ref, branch_ref, logits_ref, gain_ref, fixed_ref, *refs):
+        left, packed = refs[-2:]
+        got, outs = (None, refs[:-2]) if received is None else (refs[0], refs[1:-2])
+        which = 1 - place_ref[1] if received is None else place_ref[1]
+        put = packer(packed, got)
+        lane_half(normed_ref, left, which, count)
+        turned = left[...].T
+        for at in range(0, columns, 2 * LANES):
+            tile = mm(turned, proj_ref[:, at : at + 2 * LANES])
+            for t in range(count):
+                for c in range(2):
+                    put(t * block + at + c * LANES, tile[t * LANES : (t + 1) * LANES, c * LANES : (c + 1) * LANES])
+        logits = logits_ref[...]
+        logits_t = logits.T
+        decay = sum(mm(piece, left[...]) for piece in three_way(logits_t)[:2])
+        near = pl.multiple_of(which * LANES, LANES)
+        for t in range(count):
+            at = pl.multiple_of(t * 2 * LANES + which * LANES, LANES)
+            rows = [decay[0:heads, t * LANES : (t + 1) * LANES], gain_ref[0:1, pl.ds(at, LANES)]]
+            put(t * block + columns, small_rows(rows))
+            keys_here = (place_ref[0] // 2 == t).astype(wide)
+            values_here = (place_ref[0] // 2 + 2 == t).astype(wide)
+            fixed = fixed_ref[:, pl.ds(near, LANES)] * keys_here
+            fixed = fixed + fixed_ref[:, pl.ds(pl.multiple_of(inner + near, LANES), LANES)] * values_here
+            put(t * block + columns + SMALL, fixed)
+        comb_t = comb_ref[:, pl.ds(near, LANES)].T
+        for c in range(0, width // LANES, 2):
+            tile = mm(comb_t, branch_ref[:, c * LANES : (c + 2) * LANES])
+            put(count * block + c * LANES, tile[:, :LANES])
+            put(count * block + (c + 1) * LANES, tile[:, LANES:])
+        put(count * block + width, small_rows([jnp.sum(logits, axis=0, keepdims=True)]))
+        packed[count * block + width + SMALL :, :] = jnp.zeros((SMALL, LANES), half)
+        chunk_out(packed, outs)
+
+    local = width + 2 * SMALL
+    inputs = [place, normed, g_projected, combined, branch, g_logits, g_gain, g_fixed]
+    scratch = [pltpu.VMEM((total_rows, side), half)]
+    flops = total_rows * width * (columns + inner)
+    return grad_call(body, chunks, count * block + local, inputs, received, scratch, flops, "grad_mix")
+
+
+def split_rows(total, chunks):
+    units = total // SMALL
+    edges = [SMALL * (units * k // chunks) for k in range(chunks)] + [total]
+    return list(zip(edges[:-1], edges[1:]))
+
+
+def chunk_out(whole, outs):
+    at = 0
+    for out in outs:
+        out[...] = whole[at : at + out.shape[0], :]
+        at += out.shape[0]
+
+
+def spread(count, block, place, chunks):
+    total = sum(chunk.shape[0] for chunk, _ in chunks)
+
+    def body(place_ref, *refs):
+        ins, outs, whole = refs[: 2 * len(chunks)], refs[2 * len(chunks) : -1], refs[-1]
+        for inner in range(2):
+
+            @pl.when(place_ref[3] == inner)
+            def _(inner=inner):
+                at = 0
+                for chunk in ins[1 - inner :: 2]:
+                    whole[at : at + chunk.shape[0], :] = chunk[...]
+                    at += chunk.shape[0]
+
+        take_rows(whole, outs[:count], place_ref)
+        outs[count][...] = whole[count * block :, :]
+
+    outs = [shape((block, LANES))] * count + [shape((total - count * block, LANES))]
+    scratch = [pltpu.VMEM((total, LANES), half)]
+    flat = [piece for pair in chunks for piece in pair]
+    return call(body, outs, [smem] + [vmem] * len(flat), scratch, 0, total * 768, "spread")(place, *flat)
+
+
+def collect_feed(chunks, place, parts, local):
+    count = len(parts)
+    columns = parts[0].shape[0] - SMALL
+    total = count * columns + SMALL + local.shape[0]
+
+    def body(place_ref, *refs):
+        parts_in, local_ref, outs, whole = refs[:count], refs[count], refs[count + 1 : -1], refs[-1]
+        for r, part in enumerate(parts_in):
+            at = pl.multiple_of((place_ref[0] ^ r) * columns, columns)
+            whole[pl.ds(at, columns), :] = part[0:columns, :]
+        small = sum(part[columns:, :].astype(wide) for part in parts_in)
+        whole[count * columns : count * columns + SMALL, :] = small.astype(half)
+        whole[count * columns + SMALL :, :] = local_ref[...]
+        chunk_out(whole, outs)
+
+    outs = [shape((b - a, LANES)) for a, b in split_rows(total, chunks)]
+    return call(body, outs, [smem] + [vmem] * (count + 1), [pltpu.VMEM((total, LANES), half)], 0, total * 512, "collect_feed")(
+        place, *parts, local
+    )
+
+
+def collect_mix(chunks, heads, place, parts, local):
+    count = len(parts)
+    slots = parts[0].shape[0] % (3 * heads * LANES) - SMALL
+    columns = parts[0].shape[0] - SMALL - slots
+    total = count * columns + SMALL + 2 * slots + local.shape[0]
+
+    def body(place_ref, *refs):
+        parts_in, local_ref, outs, whole, few = refs[:count], refs[count], refs[count + 1 : -2], refs[-2], refs[-1]
+        for r, part in enumerate(parts_in):
+            source = place_ref[0] ^ r
+            at = pl.multiple_of(source * columns, columns)
+            whole[pl.ds(at, columns), :] = part[0:columns, :]
+            few[pl.ds(source, 1)] = part[columns:, :].astype(wide)[None]
+        base = count * columns
+        decay = [few[t, 0:heads, :] for t in range(count)]
+        gain = sum(few[t, heads : heads + 1, :] for t in range(count))
+        whole[base : base + SMALL, :] = small_rows(decay + [gain]).astype(half)
+        near = (place_ref[0] % 2) * 2
+        for k in range(2):
+            at = base + SMALL + k * slots
+            whole[at : at + slots, :] = few[near + k, SMALL:, :].astype(half)
+        whole[base + SMALL + 2 * slots :, :] = local_ref[...]
+        chunk_out(whole, outs)
+
+    outs = [shape((b - a, LANES)) for a, b in split_rows(total, chunks)]
+    scratch = [pltpu.VMEM((total, LANES), half), pltpu.VMEM((count, SMALL + slots, LANES), wide)]
+    return call(body, outs, [smem] + [vmem] * (count + 1), scratch, 0, total * 512, "collect_mix")(place, *parts, local)
+
+
+def unpack(body, totals, out_shape, place, name):
+    chunks = len(totals[0][0])
+    edges = [0]
+    for chunk in totals[0][0]:
+        edges.append(edges[-1] + chunk.shape[0])
+
+    def whole_body(place_ref, *refs):
+        ins, outs, halves, sems = refs[: 4 * chunks], refs[4 * chunks : -2], refs[-2], refs[-1]
+        handles = []
+        for side in range(2):
+            for c in range(chunks):
+                spot = place_ref[1] if side == 0 else 1 - place_ref[1]
+                where = halves.at[spot, pl.ds(edges[c], edges[c + 1] - edges[c])]
+                sem = sems.at[side * chunks + c]
+                for layer in range(2):
+                    source = ins[layer * 2 * chunks + side * chunks + c]
+
+                    @pl.when(place_ref[1] == layer)
+                    def _(source=source, where=where, sem=sem):
+                        pltpu.make_async_copy(source, where, sem).start()
+
+                handles.append(pltpu.make_async_copy(ins[side * chunks + c], where, sem))
+        finish(handles)
+        body(place_ref, halves, *outs)
+
+    inputs = [piece for layer in totals for side in layer for piece in side]
+    scratch = [pltpu.VMEM((2, edges[-1], LANES), half), pltpu.SemaphoreType.DMA((2 * chunks,))]
+    moved = sum(o.size * 4 for o in out_shape) + 4 * edges[-1] * LANES
+    return call(whole_body, out_shape, [smem] + [anywhere] * len(inputs), scratch, 0, moved, name)(place, *inputs)
+
+
+def unpack_feed(count, columns, hidden, width, totals, place):
+    part = width // count
+    side = width // 2
+    tiles = columns // LANES
+
+    def body(place_ref, halves, gate_up, down, gain):
+        low = lax.broadcasted_iota(jnp.int32, (LANES, LANES), 1) < PAIR
+        middle = gate_up.shape[1] // 2
+        for h in range(2):
+            rows = slice(h * LANES, (h + 1) * LANES)
+            for m in range(middle // LANES):
+                even = halves[h, 2 * m * LANES : (2 * m + 1) * LANES, :].astype(wide)
+                odd = halves[h, (2 * m + 1) * LANES : (2 * m + 2) * LANES, :].astype(wide)
+                gate_up[rows, m * LANES : (m + 1) * LANES] = jnp.where(low, even, pltpu.roll(odd, PAIR, 1))
+                gate_up[rows, middle + m * LANES : middle + (m + 1) * LANES] = jnp.where(low, pltpu.roll(even, PAIR, 1), odd)
+            base = count * columns
+            gain[0:1, h * LANES : (h + 1) * LANES] = halves[h, base : base + SMALL, :].astype(wide)[0:1]
+            base += SMALL
+            for c in range(side // LANES):
+                at = h * side + c * LANES
+                down[:, at : at + LANES] = halves[h, base + c * hidden : base + (c + 1) * hidden, :].astype(wide)
+
+    outs = [shape((part, count * columns), wide), shape((hidden, width), wide), shape((1, part), wide)]
+    return unpack(body, totals, outs, place, "unpack_feed")
+
+
+def unpack_mix(count, heads, slots, width, totals, place):
+    part = width // count
+    inner = heads * LANES
+    columns = 3 * inner
+
+    def body(place_ref, halves, qkv, out, gain, decay, bias, fixed):
+        for h in range(2):
+            rows = slice(h * LANES, (h + 1) * LANES)
+            for t in range(count):
+                for kind in range(3):
+                    for head in range(heads):
+                        source = t * columns + kind * inner + head * LANES
+                        at = kind * count * inner + t * inner + head * LANES
+                        qkv[rows, at : at + LANES] = halves[h, source : source + LANES, :].astype(wide)
+            base = count * columns
+            small = halves[h, base : base + SMALL, :].astype(wide)
+            padded = jnp.concatenate([small, jnp.zeros((LANES - SMALL, LANES), wide)], axis=0).T
+            decay[rows, :] = padded[:, 0 : count * heads]
+            gain[0:1, rows] = small[count * heads : count * heads + 1]
+            for k in range(2):
+                at = base + SMALL + k * slots
+                lanes = slice(k * inner + h * LANES, k * inner + (h + 1) * LANES)
+                fixed[:, lanes] = halves[h, at : at + slots, :].astype(wide)
+            base += SMALL + 2 * slots
+            for c in range(width // LANES):
+                source = base + c * LANES
+                out[rows, c * LANES : (c + 1) * LANES] = halves[h, source : source + LANES, :].astype(wide)
+            if h == 0:
+                bias[...] = halves[h, base + width : base + width + SMALL, :].astype(wide)[0:1, 0:heads]
+
+    outs = [
+        shape((part, count * columns), wide),
+        shape((inner, width), wide),
+        shape((1, part), wide),
+        shape((part, count * heads), wide),
+        shape((1, heads), wide),
+        shape((slots, 2 * inner), wide),
+    ]
+    return unpack(body, totals, outs, place, "unpack_mix")
+
+
+def tie(*values):
+    return lax.optimization_barrier(values)
 
 
 def exchange(value, axis, distance):
@@ -16,7 +929,240 @@
 
 def gather_parts(block, axis):
     count = lax.axis_size(axis)
-    return [block] + [exchange(block, axis, r) for r in range(1, count)]
+    far = {r: exchange(block, axis, r) for r in reversed(range(1, count))}
+    return [block] + [far[r] for r in range(1, count)]
+
+
+def trade_parts(blocks, axis):
+    far = {r: exchange(blocks[r], axis, r) for r in reversed(range(1, len(blocks)))}
+    return [blocks[0]] + [far[r] for r in range(1, len(blocks))]
+
+
+def plane_device(
+    tokens,
+    lengths,
+    cotangent,
+    norm_one,
+    qkv_weight,
+    decay_weight,
+    decay_bias,
+    persistent,
+    out_weight,
+    norm_two,
+    gate_up,
+    down_weight,
+):
+    ctx_count, count = lax.axis_size("ctx"), lax.axis_size("fsdp")
+    section, ctx, fsdp = (lax.axis_index(a) for a in ("section", "ctx", "fsdp"))
+    rows, width = tokens.shape[2:]
+    heads = decay_bias.shape[1]
+    size = width // (heads * count)
+    inner = heads * size
+
+    def own_batch(value):
+        return lax.dynamic_index_in_dim(value, section, 0, False)[0]
+
+    pairs = [(c * count + f, f * ctx_count + c) for c in range(ctx_count) for f in range(count)]
+
+    def turn_plane(value):
+        return lax.ppermute(value, ("ctx", "fsdp"), pairs)
+
+    def swap(value):
+        return exchange(value, "section", 1)
+
+    slots = persistent.shape[1]
+    spot = jnp.stack([fsdp, section, ctx]).astype(jnp.int32)
+    x_own, qkv_shard = tie(own_batch(tokens), qkv_weight[0])
+    x_in = turn_plane(x_own)
+    qkv_packed = pack_heads(count, qkv_shard, spot)
+    qkv_mine = trade_parts(qkv_packed, "fsdp")
+    small = pack_small(norm_one, norm_two, decay_weight[0], decay_bias, persistent[0], lengths[:, 0, 0])
+    small, qkv_packed = tie(small, qkv_packed)
+    smalls = gather_parts(jnp.concatenate([small, swap(small)]), "fsdp")
+    (gains_one, gains_two, decays, biases, fixeds), length = unpack_small(heads, slots, width, spot, smalls)
+    place = jnp.stack([fsdp, section, length, (ctx == 1) | (ctx == 2)]).astype(jnp.int32)
+    out_mine = out_weight[0]
+    out_other = swap(out_mine)
+    gu_packed = pack_gates(count, gate_up[0], spot)
+    x_parts = gather_parts(norm_rows(x_in, gains_one[0]), "fsdp")
+    qkv_mine, x_parts, gu_packed, g_own = tie(qkv_mine, x_parts, gu_packed, own_batch(cotangent))
+    qkv_other = [swap(piece) for piece in qkv_mine]
+    gu_mine = trade_parts(gu_packed, "fsdp")
+    down_mine = down_weight[0]
+    down_other = swap(down_mine)
+    g_in = turn_plane(g_own)
+    hidden = down_mine.shape[0]
+    columns = gu_mine[0].shape[1]
+
+    def mix_first_half(layer, parts):
+        *terms, combined, seen, projected, logits = mix_forward(
+            layer, heads, size, place, parts, qkv_mine, qkv_other, out_mine, out_other, decays[layer], biases[layer], fixeds[layer]
+        )
+        return terms, (seen, projected, logits, combined)
+
+    def mix_second_half(layer, terms, x):
+        middle, normed_two = join_forward(False, trade_parts(terms, "fsdp"), x, gains_two[layer])
+        return middle, gather_parts(normed_two, "fsdp")
+
+    def feed_step(layer, parts, saved):
+        *terms, g_rows, g_gates, active, g_gain = feed_backward(
+            layer, place, parts, saved[6], gains_two[layer], gu_mine, gu_other, down_mine, down_other
+        )
+        return terms, (saved[6], g_gates, active, g_rows, g_gain)
+
+    def mix_step(layer, parts, saved):
+        x, seen, projected, logits, combined, middle, seen_two = saved
+        *terms, branch, g_projected, g_logits, g_fixed, g_gain = mix_backward(
+            layer, heads, size, place, parts, out_mine, out_other, qkv_mine, qkv_other,
+            decays[layer], fixeds[layer], projected, logits, seen, gains_one[layer],
+        )
+        return terms, (seen, g_projected, combined, branch, g_logits, g_gain, g_fixed)
+
+    inside = (ctx == 1) | (ctx == 2)
+    line = {"queue": [], "inward": None, "across": None, "total": None, "flight": (None, None), "sums": []}
+
+    def begin():
+        own = line["queue"].pop(0) if line["queue"] else None
+        total = line["total"]
+        if own is not None and total is not None:
+            sent = jnp.where(inside, total, own)
+            route = [(0, 1), (3, 2), (1, 0), (2, 3)]
+        else:
+            sent = own if total is None else total
+            route = [(0, 1), (3, 2)] if total is None else [(1, 0), (2, 3)]
+        pair = line["across"]
+        line["sent"] = (sent, pair, own, total is not None)
+        return [v for v in (sent, pair) if v is not None], route
+
+    def go(values, route):
+        values = list(values)
+        sent, pair, own, closing = line["sent"]
+        sent = values.pop(0) if sent is not None else None
+        pair = values.pop(0) if pair is not None else None
+        line["sent"] = (sent, pair, own, closing)
+        flight = [None, None]
+        if sent is not None:
+            flight[0] = lax.ppermute(sent, "ctx", route)
+        if pair is not None:
+            flight[1] = lax.ppermute(pair, "ctx", [(1, 2), (2, 1)])
+        line["flight"] = flight
+
+    def plus(a, b):
+        return (a.astype(wide) + b.astype(wide)).astype(half)
+
+    def step(*held, more=()):
+        landed, crossed = line["flight"]
+        waiting = [v for v in (landed, crossed) if v is not None]
+        held, waiting = tie(held, waiting)
+        if landed is not None:
+            landed = waiting.pop(0)
+        if crossed is not None:
+            crossed = waiting.pop(0)
+        sent, pair, own, closing = line.get("sent", (None, None, None, False))
+        line["total"] = None if pair is None else plus(pair, crossed)
+        line["across"] = None if own is None else plus(own, landed)
+        if closing:
+            line["sums"].append((sent, landed))
+        line["queue"].extend(more)
+        ready, route = begin()
+        held, ready = tie(held, ready)
+        go(ready, route)
+        return held
+
+    def taken(number):
+        found, line["sums"] = line["sums"][:number], line["sums"][number:]
+        return found
+
+    terms, kept = mix_first_half(0, x_parts)
+    terms, gu_mine = tie(terms, gu_mine)
+    gu_other = [swap(piece) for piece in gu_mine]
+    middle, parts = mix_second_half(0, terms, x_in)
+    *terms, seen_two = feed_forward(0, place, parts, gu_mine, gu_other, down_mine, down_other)
+    saved_first = (x_in, *kept, middle, seen_two)
+    between, normed = join_forward(True, trade_parts(terms, "fsdp"), middle, gains_one[1])
+    terms, kept = mix_first_half(1, gather_parts(normed, "fsdp"))
+    terms, g_parts = tie(terms, gather_parts(g_in, "fsdp"))
+    middle, parts = mix_second_half(1, terms, between)
+    *terms_out, seen_two = feed_forward(1, place, parts, gu_mine, gu_other, down_mine, down_other)
+    saved_second = (between, *kept, middle, seen_two)
+    terms, feed = feed_step(1, g_parts, saved_second)
+    out = join_forward(True, trade_parts(terms_out, "fsdp"), middle, None)[0]
+    terms, out = tie(terms, out)
+    out = turn_plane(out)
+    other = grad_feed(1, count, place, *feed)[0]
+    terms, other, out = tie(trade_parts(terms, "fsdp"), other, out)
+    g_middle, g_branch = join_backward(terms, saved_second[5], gains_two[1], g_in)
+    parts = gather_parts(g_branch, "fsdp")
+    f1 = grad_feed(4, count, place, *feed, received=swap(other))
+    (parts,) = step(parts, more=f1)
+    terms, mix = mix_step(1, parts, saved_second)
+    (terms,) = step(terms)
+    other = grad_mix(1, count, place, *mix)[0]
+    terms, other = step(trade_parts(terms, "fsdp"), other)
+    g_middle, g_branch = join_backward(terms, between, gains_one[1], g_middle)
+    parts = gather_parts(g_branch, "fsdp")
+    m1 = grad_mix(2, count, place, *mix, received=swap(other))
+    (parts,) = step(parts, more=m1)
+    terms, feed = feed_step(0, parts, saved_first)
+    (terms,) = step(terms)
+    other = grad_feed(1, count, place, *feed)[0]
+    terms, other = step(trade_parts(terms, "fsdp"), other)
+    g_middle, g_branch = join_backward(terms, saved_first[5], gains_two[0], g_branch)
+    parts = gather_parts(g_branch, "fsdp")
+    f0 = grad_feed(4, count, place, *feed, received=swap(other))
+    (parts,) = step(parts, more=f0)
+    terms, mix = mix_step(0, parts, saved_first)
+    (terms,) = step(terms)
+    other = grad_mix(1, count, place, *mix)[0]
+    received = swap(other)
+    terms, received = step(trade_parts(terms, "fsdp"), received)
+    m0 = grad_mix(2, count, place, *mix, received=received)
+    g_input = join_backward(terms, x_in, gains_one[0], g_middle)[1]
+
+    def trade(block, chunks):
+        *blocks, local = spread(count, block, place, chunks)
+        return trade_parts(blocks, "fsdp"), local
+
+    feed_block = columns + SMALL
+    mix_block = 3 * inner + SMALL + slots
+    f1 = trade(feed_block, taken(4))
+    g_input, f1 = step(g_input, f1, more=m0)
+    feed_second = collect_feed(1, place, *f1)
+    m1 = trade(mix_block, taken(2))
+    feed_second, m1 = step(feed_second, m1)
+    mix_second = collect_mix(1, heads, place, *m1)
+    (mix_second,) = step(mix_second)
+    (mix_second,) = step(mix_second)
+    (mix_second,) = step(mix_second)
+    f0 = trade(feed_block, taken(4))
+    g_input, f0 = step(g_input, f0)
+    g_input = turn_plane(g_input)
+    m0 = trade(mix_block, taken(2))
+    feed_first = collect_feed(1, place, *f0)
+    mix_first = collect_mix(1, heads, place, *m0)
+
+    def owned(layer, chunks):
+        return chunks, [lax.ppermute(chunk, "section", [(1 - layer, layer)]) for chunk in chunks]
+
+    grad_gate_up, grad_down, grad_norm_two = unpack_feed(
+        count, columns, hidden, width, (owned(0, feed_first), owned(1, feed_second)), place
+    )
+    grad_qkv, grad_out, grad_norm_one, grad_decay, grad_bias, grad_fixed = unpack_mix(
+        count, heads, slots, width, (owned(0, mix_first), owned(1, mix_second)), place
+    )
+    return (
+        out[None, None],
+        g_input[None, None],
+        grad_norm_one,
+        grad_qkv[None],
+        grad_decay[None],
+        grad_bias,
+        grad_fixed[None],
+        grad_out[None],
+        grad_norm_two,
+        grad_gate_up[None],
+        grad_down[None],
+    )
 
 
 def scatter_sum(blocks, axis):
@@ -167,7 +1313,7 @@
     return grad_projected.astype(half), grad_logits.T, grad_persistent
 
 
-def per_device(
+def general_device(
     tokens,
     lengths,
     cotangent,
@@ -358,8 +1504,9 @@
     by_token = P(None, "fsdp", "ctx", None)
     by_output = P("section", "fsdp", "ctx", None)
     by_slot = P("section", None, "fsdp")
+    plane = mesh.shape["ctx"] == mesh.shape["fsdp"] == 4
     return jax.shard_map(
-        per_device,
+        plane_device if plane else general_device,
         mesh=mesh,
         in_specs=(
             by_token,

time: 848 us -> 566 us (0.67)
  local copies, waits for them, and re-layouts: 168 us -> 18.2 us
  Pallas kernels: 0 us -> 111 us
  matrix products: 90.6 us -> 0 us
  other arithmetic: 62.4 us -> 4.98 us
  starting transfers between devices: 210 us -> 172 us
  waiting for transfers between devices: 284 us -> 248 us
  between operations: 17.9 us -> 1.91 us
    pallas_call x0 -> x39, Pallas kernels: none -> 111 us  [the longest x2 21.1 us: mix_backward(): call(body, outs, specs, scratch, flops, moved, 'mix_backward')]
    dot_general x58 -> x0, matrix products: 90.6 us -> none  [the longest x30 70.4 us: dot(): lax.dot_general(a, b, (((contract[0],), (contract[1],)), ((), ())), prefe...]
    dynamic_update_slice x26 -> x0, local copies, waits for them, and re-layouts: 75.5 us -> none  [the longest x20 65.1 us: in_order(): lax.dynamic_update_slice_in_dim(whole, part, (index ^ r) * size, dim)]
    ppermute x17 -> x34, waiting for transfers between devices: 127 us -> 53.5 us  [the longest x14 27.8 us: go(): flight[0] = lax.ppermute(sent, 'ctx', route)]
    ppermute x73 -> x84, waiting for transfers between devices: 144 us -> 194 us  [exchange(): return lax.ppermute(value, axis, [(i, i ^ distance) for i in range(count)])]
    ppermute x17 -> x34, starting transfers between devices: 117 us -> 69.4 us  [the longest x14 35.9 us: go(): flight[0] = lax.ppermute(sent, 'ctx', route)]
    convert_element_type x29 -> x13, other arithmetic: 42.6 us -> 2.02 us  [plus(): return (a.astype(wide) + b.astype(wide)).astype(half)]
    reshape x18 -> x0, local copies, waits for them, and re-layouts: 21.4 us -> none  [the longest x4 7.48 us: rows_here(): parts.append(block.reshape(rows, kinds, 1, width))]
  transfers between devices with their start and end apart: 91 -> 118, of which waited for: 40 -> 57; matrix products, arithmetic and copies ran while one was open for 34% -> 1% of each run, Pallas kernels for 0% -> 15%
where the time goes in v1:
time: 566 us; the launch traced here: 556 us
  waiting for transfers between devices  248 us (44%)
  starting transfers between devices  172 us (30%)
  Pallas kernels  111 us (20%)
  local copies, waits for them, and re-layouts  18.2 us (3%)
    ppermute x84, waiting for transfers between devices, exchange(): return lax.ppermute(value, axis, [(i, i ^ distance) for i in range(count)])  194 us
    ppermute x84, starting transfers between devices, exchange(): return lax.ppermute(value, axis, [(i, i ^ distance) for i in range(count)])  103 us
    ppermute x14, starting transfers between devices, go(): flight[0] = lax.ppermute(sent, 'ctx', route)  35.9 us
    ppermute x14, waiting for transfers between devices, go(): flight[0] = lax.ppermute(sent, 'ctx', route)  27.8 us
    ppermute x4, waiting for transfers between devices, turn_plane(): return lax.ppermute(value, ('ctx', 'fsdp'), pairs)  25.7 us
    pallas_call x2, Pallas kernels, mix_backward(): call(body, outs, specs, scratch, flops, moved, 'mix_backward')  21.1 us
    pallas_call x2, Pallas kernels, feed_backward(): call(body, outs, specs, scratch, flops, moved, 'feed_backward')  17 us
    unnamed x83, local copies, waits for them, and re-layouts  16.7 us
  transfers between devices with their start and end apart: 118, of which 57 were waited for; matrix products, arithmetic and copies ran while one was open for 1% of the time, Pallas kernels for 15%

profile of v1, /device:TPU:2, one launch (start us, length us, event | category | flops | bytes accessed | tf_op | source)
XLA Modules:
  0.0 556.2 jit_solution(11216051109975088467)
XLA Ops:
  18.5 7.1 %collective-permute-done.3.refs_3_ = bf16[224,128]{1,0:T(8,128)(2,1)S(1)} collective-permute-done((bf16[224,128]{1,0:T(8,128)(2,1)S(1)}, bf16[224,128]{1,0:T(8,128)(2,1)S(1)}, u32[]{:S(2)}, u32[]{:S(2)}) %collective-permute-start.3) | collective-permute-done | bytes 57376 | tf_op jit(solution)/shard_map/ppermute | solution.py:927
  25.5 6.8 %collective-permute-start.2 = (bf16[224,128]{1,0:T(8,128)(2,1)S(1)}, bf16[224,128]{1,0:T(8,128)(2,1)S(1)}, u32[]{:S(2)}, u32[]{:S(2)}) collective-permute-start(bf16[224,128]{1,0:T(8,128)(2,1)S(1)} %constant_dynamic-update-slice_fusion.refs_0_), channel_id=1, source_target_pairs={{0,2},{1,3},{2,0},{3,1},{4,6},{5,7},{6,4},{7,5},{8,10},{9,11},{10,... | collective-permute-start | bytes 172040 | tf_op jit(solution)/shard_map/ppermute | solution.py:927
  32.3 7.1 %collective-permute-done.2.refs_2_ = bf16[224,128]{1,0:T(8,128)(2,1)S(1)} collective-permute-done((bf16[224,128]{1,0:T(8,128)(2,1)S(1)}, bf16[224,128]{1,0:T(8,128)(2,1)S(1)}, u32[]{:S(2)}, u32[]{:S(2)}) %collective-permute-start.2) | collective-permute-done | bytes 57376 | tf_op jit(solution)/shard_map/ppermute | solution.py:927
  73.8 7.3 %mix_forward.2 = (f32[128,1024]{1,0:T(8,128)S(1)}, bf16[128,1024]{1,0:T(8,128)(2,1)S(1)}, bf16[128,1024]{1,0:T(8,128)(2,1)S(1)}, bf16[128,1024]{1,0:T(8,128)(2,1...) custom-call(s32[4]{0:T(128)S(1)} %pad_add_fusion.1.place_ref, ...), custom_call_target="tpu_custom_call" | custom-call | flops 1342177280 | bytes 4718592 | tf_op jit(solution)/shard_map/mix_forward/pallas_call | solution.py:243
  82.0 15.9 %collective-permute-done.17.refs_6_.refs_8_ = bf16[256,1408]{1,0:T(8,128)(2,1)S(1)} collective-permute-done((bf16[256,1408]{1,0:T(8,128)(2,1)}, bf16[256,1408]{1,0:T(8,128)(2,1)S(1)}, u32[]{:S(2)}, u32[]{:S(2)}) %collective-permute-start.17) | collective-permute-done | bytes 720928 | tf_op jit(solution)/shard_map/ppermute | solution.py:927
  146.9 10.5 %collective-permute-done.30.refs_1_ = bf16[128,1024]{1,0:T(8,128)(2,1)S(1)} collective-permute-done((bf16[128,1024]{1,0:T(8,128)(2,1)S(1)}, bf16[128,1024]{1,0:T(8,128)(2,1)S(1)}, u32[]{:S(2)}, u32[]{:S(2)}) %collective-permute-start.30) | collective-permute-done | bytes 262176 | tf_op jit(solution)/shard_map/ppermute | solution.py:927
  179.0 7.3 %mix_forward.3 = (f32[128,1024]{1,0:T(8,128)S(1)}, bf16[128,1024]{1,0:T(8,128)(2,1)S(1)}, bf16[128,1024]{1,0:T(8,128)(2,1)S(1)}, bf16[128,1024]{1,0:T(8,128)(2,1...) custom-call(s32[4]{0:T(128)S(1)} %pad_add_fusion.1.place_ref, ...), custom_call_target="tpu_custom_call" | custom-call | flops 1342177280 | bytes 4718592 | tf_op jit(solution)/shard_map/mix_forward/pallas_call | solution.py:243
  209.2 6.3 %collective-permute-done.44.refs_2_ = bf16[128,1024]{1,0:T(8,128)(2,1)S(1)} collective-permute-done((bf16[128,1024]{1,0:T(8,128)(2,1)S(1)}, bf16[128,1024]{1,0:T(8,128)(2,1)S(1)}, u32[]{:S(2)}, u32[]{:S(2)}) %collective-permute-start.44) | collective-permute-done | bytes 262176 | tf_op jit(solution)/shard_map/ppermute | solution.py:927
  226.1 8.6 %feed_backward.2 = (f32[128,1024]{1,0:T(8,128)S(1)}, bf16[128,1024]{1,0:T(8,128)(2,1)S(1)}, bf16[128,1024]{1,0:T(8,128)(2,1)S(1)}, bf16[128,1024]{1,0:T(8,128)(2...) custom-call(s32[4]{0:T(128)S(1)} %pad_add_fusion.1.place_ref, ...), custom_call_target="tpu_custom_call" | custom-call | flops 3690987520 | bytes 12779520 | tf_op jit(solution)/shard_map/feed_backward/pallas_call | solution.py:474
  249.3 7.6 %collective-permute-done.52 = bf16[128,1024]{1,0:T(8,128)(2,1)S(1)} collective-permute-done((bf16[128,1024]{1,0:T(8,128)(2,1)S(1)}, bf16[128,1024]{1,0:T(8,128)(2,1)S(1)}, u32[]{:S(2)}, u32[]{:S(2)}) %collective-permute-start.52) | collective-permute-done | bytes 262176 | tf_op jit(solution)/shard_map/ppermute | solution.py:968
  260.8 6.6 %collective-permute-done.55.refs_3_ = bf16[128,1024]{1,0:T(8,128)(2,1)S(1)} collective-permute-done((bf16[128,1024]{1,0:T(8,128)(2,1)S(1)}, bf16[128,1024]{1,0:T(8,128)(2,1)S(1)}, u32[]{:S(2)}, u32[]{:S(2)}) %collective-permute-start.55) | collective-permute-done | bytes 262176 | tf_op jit(solution)/shard_map/ppermute | solution.py:927
  275.5 10.5 %mix_backward.2 = (f32[128,1024]{1,0:T(8,128)S(1)}, bf16[128,1024]{1,0:T(8,128)(2,1)S(1)}, bf16[128,1024]{1,0:T(8,128)(2,1)S(1)}, bf16[128,1024]{1,0:T(8,128)(2,...) custom-call(s32[4]{0:T(128)S(1)} %pad_add_fusion.1.place_ref, ...), custom_call_target="tpu_custom_call" | custom-call | flops 1744830464 | bytes 8912896 | tf_op jit(solution)/shard_map/mix_backward/pallas_call | solution.py:349
  326.1 8.4 %feed_backward.3 = (f32[128,1024]{1,0:T(8,128)S(1)}, bf16[128,1024]{1,0:T(8,128)(2,1)S(1)}, bf16[128,1024]{1,0:T(8,128)(2,1)S(1)}, bf16[128,1024]{1,0:T(8,128)(2...) custom-call(s32[4]{0:T(128)S(1)} %pad_add_fusion.1.place_ref, ...), custom_call_target="tpu_custom_call" | custom-call | flops 3690987520 | bytes 12779520 | tf_op jit(solution)/shard_map/feed_backward/pallas_call | solution.py:474
  362.0 7.4 %collective-permute-done.78.refs_3_ = bf16[128,1024]{1,0:T(8,128)(2,1)S(1)} collective-permute-done((bf16[128,1024]{1,0:T(8,128)(2,1)S(1)}, bf16[128,1024]{1,0:T(8,128)(2,1)S(1)}, u32[]{:S(2)}, u32[]{:S(2)}) %collective-permute-start.78) | collective-permute-done | bytes 262176 | tf_op jit(solution)/shard_map/ppermute | solution.py:927
  382.0 10.6 %mix_backward.3 = (f32[128,1024]{1,0:T(8,128)S(1)}, bf16[128,1024]{1,0:T(8,128)(2,1)S(1)}, bf16[128,1024]{1,0:T(8,128)(2,1)S(1)}, bf16[128,1024]{1,0:T(8,128)(2,...) custom-call(s32[4]{0:T(128)S(1)} %pad_add_fusion.1.place_ref, ...), custom_call_target="tpu_custom_call" | custom-call | flops 1744830464 | bytes 8912896 | tf_op jit(solution)/shard_map/mix_backward/pallas_call | solution.py:349
  400.2 6.7 %collective-permute-done.84.refs_1_ = bf16[128,1024]{1,0:T(8,128)(2,1)S(1)} collective-permute-done((bf16[128,1024]{1,0:T(8,128)(2,1)S(1)}, bf16[128,1024]{1,0:T(8,128)(2,1)S(1)}, u32[]{:S(2)}, u32[]{:S(2)}) %collective-permute-start.84) | collective-permute-done | bytes 262176 | tf_op jit(solution)/shard_map/ppermute | solution.py:927
  408.1 7.3 %collective-permute-done.86.refs_3_ = bf16[128,1024]{1,0:T(8,128)(2,1)S(1)} collective-permute-done((bf16[128,1024]{1,0:T(8,128)(2,1)S(1)}, bf16[128,1024]{1,0:T(8,128)(2,1)S(1)}, u32[]{:S(2)}, u32[]{:S(2)}) %collective-permute-start.86) | collective-permute-done | bytes 262176 | tf_op jit(solution)/shard_map/ppermute | solution.py:927
  425.2 5.9 %collective-permute-done.90.refs_1_ = bf16[1424,128]{1,0:T(8,128)(2,1)S(1)} collective-permute-done((bf16[1424,128]{1,0:T(8,128)(2,1)S(1)}, bf16[1424,128]{1,0:T(8,128)(2,1)S(1)}, u32[]{:S(2)}, u32[]{:S(2)}) %collective-permute-start.90) | collective-permute-done | bytes 364576 | tf_op jit(solution)/shard_map/ppermute | solution.py:927
  454.4 7.5 %collective-permute-done.100.refs_5_ = bf16[2128,128]{1,0:T(8,128)(2,1)S(1)} collective-permute-done((bf16[2128,128]{1,0:T(8,128)(2,1)S(1)}, bf16[2128,128]{1,0:T(8,128)(2,1)S(1)}, u32[]{:S(2)}, u32[]{:S(2)}) %collective-permute-start.100) | collective-permute-done | bytes 544800 | tf_op jit(solution)/shard_map/ppermute | solution.py:1045
  466.7 7.2 %collective-permute-done.102.refs_7_ = bf16[2128,128]{1,0:T(8,128)(2,1)S(1)} collective-permute-done((bf16[2128,128]{1,0:T(8,128)(2,1)S(1)}, bf16[2128,128]{1,0:T(8,128)(2,1)S(1)}, u32[]{:S(2)}, u32[]{:S(2)}) %collective-permute-start.102) | collective-permute-done | bytes 544800 | tf_op jit(solution)/shard_map/ppermute | solution.py:1045
  476.2 10.6 %collective-permute-done.107.refs_1_ = bf16[2128,128]{1,0:T(8,128)(2,1)S(1)} collective-permute-done((bf16[2128,128]{1,0:T(8,128)(2,1)S(1)}, bf16[2128,128]{1,0:T(8,128)(2,1)S(1)}, u32[]{:S(2)}, u32[]{:S(2)}) %collective-permute-start.107) | collective-permute-done | bytes 544800 | tf_op jit(solution)/shard_map/ppermute | solution.py:1045
  519.3 6.2 %collective-permute-start.110 = (bf16[128,1024]{1,0:T(8,128)(2,1)S(1)}, bf16[128,1024]{1,0:T(8,128)(2,1)S(1)}, u32[]{:S(2)}, u32[]{:S(2)}) collective-permute-start(bf16[128,1024]{1,0:T(8,128)(2,1)S(1)} %get-tuple-element.681), channel_id=1, source_target_pairs={{0,0},{1,4},{2,8},{3,12},{4,1},{5,5},{6,9},{7,13},{8,2},{9,6},{10,... | collective-permute-start | bytes 786440 | tf_op jit(solution)/shard_map/ppermute | solution.py:968
  525.5 18.1 %collective-permute-done.110 = bf16[128,1024]{1,0:T(8,128)(2,1)S(1)} collective-permute-done((bf16[128,1024]{1,0:T(8,128)(2,1)S(1)}, bf16[128,1024]{1,0:T(8,128)(2,1)S(1)}, u32[]{:S(2)}, u32[]{:S(2)}) %collective-permute-start.110) | collective-permute-done | bytes 262176 | tf_op jit(solution)/shard_map/ppermute | solution.py:968
  547.2 7.4 %unpack_feed.1 = (f32[256,5632]{1,0:T(8,128)}, f32[704,1024]{1,0:T(8,128)}, f32[1,256]{1,0:T(1,128)}) custom-call(s32[4]{0:T(128)S(1)} %pad_add_fusion.1.place_ref, bf16[8464,128]{1,0:T(8,128)(2,1)} %collect_feed.3.refs_0_, bf16[8464,128]{1,0:T(8,128)(2,1)} %collective-permute-done.116.refs_1_, bf16[8464,128]{1,0:T(8,128)(2,1)S(1)} %collect_feed.2.refs_2_, ...), custom_call_target="tpu_custom_call" | custom-call | bytes 12985344 | tf_op jit(solution)/shard_map/unpack_feed/pallas_call | solution.py:851
  (364 shorter events, 349.5 us)
Async XLA Ops:
  2.4 42.7 %collective-permute-start.7 = (bf16[128,1024]{1,0:T(8,128)(2,1)}, bf16[128,1024]{1,0:T(8,128)(2,1)}, u32[]{:S(2)}, u32[]{:S(2)}) collective-permute-start(bf16[128,1024]{1,0:T(8,128)(2,1)} %dynamic-slice_bitcast_fusion.1), channel_id=1, source_target_pairs={{0,0},{1,4},{2,8},{3,12},{4,1},{5,5},{6,9},{7,13},{8,2},{9,6},{10,... | collective-permute-start | bytes 786440 | tf_op jit(solution)/shard_map/ppermute | solution.py:968
  9.1 39.8 %collective-permute-start.4 = (bf16[256,768]{1,0:T(8,128)(2,1)}, bf16[256,768]{1,0:T(8,128)(2,1)}, u32[]{:S(2)}, u32[]{:S(2)}) collective-permute-start(bf16[256,768]{1,0:T(8,128)(2,1)} %get-tuple-element.360), channel_id=1, source_target_pairs={{0,1},{1,0},{2,3},{3,2},{4,5},{5,4},{6,7},{7,6},{8,9},{9,8},{10,11... | collective-permute-start | bytes 1179656 | tf_op jit(solution)/shard_map/ppermute | solution.py:927
  9.1 41.2 %collective-permute-start.5 = (bf16[256,768]{1,0:T(8,128)(2,1)}, bf16[256,768]{1,0:T(8,128)(2,1)}, u32[]{:S(2)}, u32[]{:S(2)}) collective-permute-start(bf16[256,768]{1,0:T(8,128)(2,1)} %get-tuple-element.361), channel_id=1, source_target_pairs={{0,2},{1,3},{2,0},{3,1},{4,6},{5,7},{6,4},{7,5},{8,10},{9,11},{10,... | collective-permute-start | bytes 1179656 | tf_op jit(solution)/shard_map/ppermute | solution.py:927
  16.9 37.4 %collective-permute-start.6 = (bf16[256,768]{1,0:T(8,128)(2,1)}, bf16[256,768]{1,0:T(8,128)(2,1)}, u32[]{:S(2)}, u32[]{:S(2)}) collective-permute-start(bf16[256,768]{1,0:T(8,128)(2,1)} %copy-done.24), channel_id=1, source_target_pairs={{0,3},{1,2},{2,1},{3,0},{4,7},{5,6},{6,5},{7,4},{8,11},{9,10},{10,... | collective-permute-start | bytes 1179656 | tf_op jit(solution)/shard_map/ppermute | solution.py:927
  62.2 53.0 %collective-permute-start.29 = (bf16[704,1024]{1,0:T(8,128)(2,1)}, bf16[704,1024]{1,0:T(8,128)(2,1)}, u32[]{:S(2)}, u32[]{:S(2)}) collective-permute-start(bf16[704,1024]{1,0:T(8,128)(2,1)} %bitcast.12.refs_12_.refs_14_), channel_id=1, source_target_pairs={{0,16},{16,0},{1,17},{17,1},{2,18},{18,2},{3,19},{19,3},{4,20},{20... | collective-permute-start | bytes 4325384 | tf_op jit(solution)/shard_map/ppermute | solution.py:927
  62.7 19.2 %collective-permute-start.16 = (bf16[256,1408]{1,0:T(8,128)(2,1)}, bf16[256,1408]{1,0:T(8,128)(2,1)S(1)}, u32[]{:S(2)}, u32[]{:S(2)}) collective-permute-start(bf16[256,1408]{1,0:T(8,128)(2,1)} %get-tuple-element.387), channel_id=1, source_target_pairs={{0,1},{1,0},{2,3},{3,2},{4,5},{5,4},{6,7},{7,6},{8,9},{9,8},{10,11... | collective-permute-start | bytes 2162696 | tf_op jit(solution)/shard_map/ppermute | solution.py:927
  64.0 33.8 %collective-permute-start.17 = (bf16[256,1408]{1,0:T(8,128)(2,1)}, bf16[256,1408]{1,0:T(8,128)(2,1)S(1)}, u32[]{:S(2)}, u32[]{:S(2)}) collective-permute-start(bf16[256,1408]{1,0:T(8,128)(2,1)} %get-tuple-element.388), channel_id=1, source_target_pairs={{0,2},{1,3},{2,0},{3,1},{4,6},{5,7},{6,4},{7,5},{8,10},{9,11},{10,... | collective-permute-start | bytes 2162696 | tf_op jit(solution)/shard_map/ppermute | solution.py:927
  65.3 32.5 %collective-permute-start.18 = (bf16[256,1408]{1,0:T(8,128)(2,1)}, bf16[256,1408]{1,0:T(8,128)(2,1)}, u32[]{:S(2)}, u32[]{:S(2)}) collective-permute-start(bf16[256,1408]{1,0:T(8,128)(2,1)} %get-tuple-element.389), channel_id=1, source_target_pairs={{0,3},{1,2},{2,1},{3,0},{4,7},{5,6},{6,5},{7,4},{8,11},{9,10},{10,... | collective-permute-start | bytes 2162696 | tf_op jit(solution)/shard_map/ppermute | solution.py:927
  114.7 18.5 %collective-permute-start.25 = (bf16[256,1408]{1,0:T(8,128)(2,1)S(1)}, bf16[256,1408]{1,0:T(8,128)(2,1)S(1)}, u32[]{:S(2)}, u32[]{:S(2)}) collective-permute-start(bf16[256,1408]{1,0:T(8,128)(2,1)S(1)} %copy-done.5), channel_id=1, source_target_pairs={{0,16},{16,0},{1,17},{17,1},{2,18},{18,2},{3,19},{19,3},{4,20},{20... | collective-permute-start | bytes 2162696 | tf_op jit(solution)/shard_map/ppermute | solution.py:927
  114.7 18.5 %collective-permute-start.26 = (bf16[256,1408]{1,0:T(8,128)(2,1)S(1)}, bf16[256,1408]{1,0:T(8,128)(2,1)S(1)}, u32[]{:S(2)}, u32[]{:S(2)}) collective-permute-start(bf16[256,1408]{1,0:T(8,128)(2,1)S(1)} %collective-permute-done.16.refs_5_.refs_7_), channel_id=1, source_target_pairs={{0,16},{16,0},{1,17},{17,1},{2,18},{18,2},{3,19},{19,3},{4,20},{20... | collective-permute-start | bytes 2162696 | tf_op jit(solution)/shard_map/ppermute | solution.py:927
  144.5 24.4 %collective-permute-start.36 = (bf16[128,1024]{1,0:T(8,128)(2,1)S(1)}, bf16[128,1024]{1,0:T(8,128)(2,1)S(1)}, u32[]{:S(2)}, u32[]{:S(2)}) collective-permute-start(bf16[128,1024]{1,0:T(8,128)(2,1)S(1)} %dynamic-slice_bitcast_fusion), channel_id=1, source_target_pairs={{0,0},{1,4},{2,8},{3,12},{4,1},{5,5},{6,9},{7,13},{8,2},{9,6},{10,... | collective-permute-start | bytes 786440 | tf_op jit(solution)/shard_map/ppermute | solution.py:968
  287.3 19.0 %collective-permute-start.61 = (bf16[2128,128]{1,0:T(8,128)(2,1)S(1)}, bf16[2128,128]{1,0:T(8,128)(2,1)S(1)}, u32[]{:S(2)}, u32[]{:S(2)}) collective-permute-start(bf16[2128,128]{1,0:T(8,128)(2,1)S(1)} %get-tuple-element.485), channel_id=1, source_target_pairs={{0,4},{12,8},{1,5},{13,9},{2,6},{14,10},{3,7},{15,11},{16,20},{28,... | collective-permute-start | bytes 1634312 | tf_op jit(solution)/shard_map/ppermute | solution.py:1045
  355.7 21.3 %collective-permute-start.81 = (bf16[8512,128]{1,0:T(8,128)(2,1)S(1)}, bf16[8512,128]{1,0:T(8,128)(2,1)S(1)}, u32[]{:S(2)}, u32[]{:S(2)}) collective-permute-start(bf16[8512,128]{1,0:T(8,128)(2,1)S(1)} %grad_feed.6), channel_id=1, source_target_pairs={{0,16},{16,0},{1,17},{17,1},{2,18},{18,2},{3,19},{19,3},{4,20},{20... | collective-permute-start | bytes 6537224 | tf_op jit(solution)/shard_map/ppermute | solution.py:927
  355.8 21.1 %collective-permute-start.79 = (bf16[2128,128]{1,0:T(8,128)(2,1)S(1)}, bf16[2128,128]{1,0:T(8,128)(2,1)S(1)}, u32[]{:S(2)}, u32[]{:S(2)}) collective-permute-start(bf16[2128,128]{1,0:T(8,128)(2,1)S(1)} %fusion.3.refs_6_), channel_id=1, source_target_pairs={{0,4},{12,8},{4,0},{8,12},{1,5},{13,9},{5,1},{9,13},{2,6},{14,10},... | collective-permute-start | bytes 1634312 | tf_op jit(solution)/shard_map/ppermute | solution.py:1045
  358.6 18.4 %collective-permute-start.80 = (bf16[2128,128]{1,0:T(8,128)(2,1)S(1)}, bf16[2128,128]{1,0:T(8,128)(2,1)S(1)}, u32[]{:S(2)}, u32[]{:S(2)}) collective-permute-start(bf16[2128,128]{1,0:T(8,128)(2,1)S(1)} %add_convert_fusion.15), channel_id=1, source_target_pairs={{4,8},{8,4},{5,9},{9,5},{6,10},{10,6},{7,11},{11,7},{20,24},{24,20... | collective-permute-start | bytes 1634312 | tf_op jit(solution)/shard_map/ppermute | solution.py:1047
  394.3 21.1 %collective-permute-start.87 = (bf16[4256,128]{1,0:T(8,128)(2,1)S(1)}, bf16[4256,128]{1,0:T(8,128)(2,1)S(1)}, u32[]{:S(2)}, u32[]{:S(2)}) collective-permute-start(bf16[4256,128]{1,0:T(8,128)(2,1)S(1)} %grad_mix.6), channel_id=1, source_target_pairs={{0,16},{16,0},{1,17},{17,1},{2,18},{18,2},{3,19},{19,3},{4,20},{20... | collective-permute-start | bytes 3268616 | tf_op jit(solution)/shard_map/ppermute | solution.py:927
  394.8 20.6 %collective-permute-start.88 = (bf16[2128,128]{1,0:T(8,128)(2,1)S(1)}, bf16[2128,128]{1,0:T(8,128)(2,1)S(1)}, u32[]{:S(2)}, u32[]{:S(2)}) collective-permute-start(bf16[2128,128]{1,0:T(8,128)(2,1)S(1)} %fusion.5.refs_2_), channel_id=1, source_target_pairs={{0,4},{12,8},{4,0},{8,12},{1,5},{13,9},{5,1},{9,13},{2,6},{14,10},... | collective-permute-start | bytes 1634312 | tf_op jit(solution)/shard_map/ppermute | solution.py:1045
  415.8 20.5 %collective-permute-start.93 = (bf16[2128,128]{1,0:T(8,128)(2,1)S(1)}, bf16[2128,128]{1,0:T(8,128)(2,1)S(1)}, u32[]{:S(2)}, u32[]{:S(2)}) collective-permute-start(bf16[2128,128]{1,0:T(8,128)(2,1)S(1)} %fusion.6.refs_0_), channel_id=1, source_target_pairs={{0,4},{12,8},{4,0},{8,12},{1,5},{13,9},{5,1},{9,13},{2,6},{14,10},... | collective-permute-start | bytes 1634312 | tf_op jit(solution)/shard_map/ppermute | solution.py:1045
  417.9 18.4 %collective-permute-start.94 = (bf16[2128,128]{1,0:T(8,128)(2,1)S(1)}, bf16[2128,128]{1,0:T(8,128)(2,1)S(1)}, u32[]{:S(2)}, u32[]{:S(2)}) collective-permute-start(bf16[2128,128]{1,0:T(8,128)(2,1)S(1)} %add_convert_fusion.9), channel_id=1, source_target_pairs={{4,8},{8,4},{5,9},{9,5},{6,10},{10,6},{7,11},{11,7},{20,24},{24,20... | collective-permute-start | bytes 1634312 | tf_op jit(solution)/shard_map/ppermute | solution.py:1047
  492.7 54.5 %collective-permute-start.117 = (bf16[8464,128]{1,0:T(8,128)(2,1)S(1)}, bf16[8464,128]{1,0:T(8,128)(2,1)}, u32[]{:S(2)}, u32[]{:S(2)}) collective-permute-start(bf16[8464,128]{1,0:T(8,128)(2,1)S(1)} %collect_feed.2.refs_2_), channel_id=1, source_target_pairs={{0,16},{1,17},{2,18},{3,19},{4,20},{5,21},{6,22},{7,23},{8,24},{9,... | collective-permute-start | bytes 6500360 | tf_op jit(solution)/shard_map/ppermute | solution.py:1145
  503.6 43.6 %collective-permute-start.116 = (bf16[8464,128]{1,0:T(8,128)(2,1)}, bf16[8464,128]{1,0:T(8,128)(2,1)}, u32[]{:S(2)}, u32[]{:S(2)}) collective-permute-start(bf16[8464,128]{1,0:T(8,128)(2,1)} %collect_feed.3.refs_0_), channel_id=1, source_target_pairs={{16,0},{17,1},{18,2},{19,3},{20,4},{21,5},{22,6},{23,7},{24,8},{25... | collective-permute-start | bytes 6500360 | tf_op jit(solution)/shard_map/ppermute | solution.py:1145
  512.0 31.6 %collective-permute-start.115 = (bf16[4176,128]{1,0:T(8,128)(2,1)S(1)}, bf16[4176,128]{1,0:T(8,128)(2,1)S(1)}, u32[]{:S(2)}, u32[]{:S(2)}) collective-permute-start(bf16[4176,128]{1,0:T(8,128)(2,1)S(1)} %collect_mix.2.refs_2_), channel_id=1, source_target_pairs={{0,16},{1,17},{2,18},{3,19},{4,20},{5,21},{6,22},{7,23},{8,24},{9,... | collective-permute-start | bytes 3207176 | tf_op jit(solution)/shard_map/ppermute | solution.py:1145
  518.0 25.6 %collective-permute-start.114 = (bf16[4176,128]{1,0:T(8,128)(2,1)S(1)}, bf16[4176,128]{1,0:T(8,128)(2,1)S(1)}, u32[]{:S(2)}, u32[]{:S(2)}) collective-permute-start(bf16[4176,128]{1,0:T(8,128)(2,1)S(1)} %collect_mix.3.refs_0_), channel_id=1, source_target_pairs={{16,0},{17,1},{18,2},{19,3},{20,4},{21,5},{22,6},{23,7},{24,8},{25... | collective-permute-start | bytes 3207176 | tf_op jit(solution)/shard_map/ppermute | solution.py:1145
  519.3 24.3 %collective-permute-start.110 = (bf16[128,1024]{1,0:T(8,128)(2,1)S(1)}, bf16[128,1024]{1,0:T(8,128)(2,1)S(1)}, u32[]{:S(2)}, u32[]{:S(2)}) collective-permute-start(bf16[128,1024]{1,0:T(8,128)(2,1)S(1)} %get-tuple-element.681), channel_id=1, source_target_pairs={{0,0},{1,4},{2,8},{3,12},{4,1},{5,5},{6,9},{7,13},{8,2},{9,6},{10,... | collective-permute-start | bytes 786440 | tf_op jit(solution)/shard_map/ppermute | solution.py:968
  (133 other events, 1411.1 us)

commit v2 on v1

--- a/solution.py
+++ b/solution.py
@@ -11,13 +11,22 @@
 half = jnp.bfloat16
 LANES = 128
 PAIR = 64
+ROOM = {
+    "mix_forward": 20,
+    "mix_backward": 24,
+    "feed_forward": 20,
+    "feed_backward": 24,
+    "grad_feed": 20,
+    "grad_mix": 16,
+    "assemble": 12,
+    "pack_gates": 16,
+    "spread": 12,
+    "collect_feed": 12,
+    "unpack_mix": 16,
+}
 vmem = pl.BlockSpec(memory_space=pltpu.VMEM)
 smem = pl.BlockSpec(memory_space=pltpu.SMEM)
-anywhere = pl.BlockSpec(memory_space=pltpu.HBM)
-
-
-def outside(*arrays):
-    return [pltpu.with_memory_space_constraint(array, pltpu.HBM) for array in arrays]
+anywhere = pl.BlockSpec(memory_space=pl.ANY)
 
 
 def mm(a, b):
@@ -43,7 +52,7 @@
         in_specs=in_specs,
         out_specs=jax.tree.map(lambda _: vmem, out_shape),
         scratch_shapes=scratch,
-        compiler_params=pltpu.CompilerParams(vmem_limit_bytes=26 * 1024 * 1024),
+        compiler_params=pltpu.CompilerParams(vmem_limit_bytes=ROOM.get(name, 8) * 1024 * 1024),
         cost_estimate=pl.CostEstimate(flops=flops, bytes_accessed=moved, transcendentals=0),
         name=name,
     )
@@ -92,29 +101,33 @@
     return call(body, outs, [smem, vmem], scratch, 0, 2 * shard.size * 2, "pack_gates")(place, shard)
 
 
-class Loader:
-    def __init__(self, place_ref, layer, sems):
-        self.place, self.layer, self.sems, self.used, self.waits = place_ref, layer, sems, 0, []
-
-    def start(self, mine, other, target, relative=False):
-        handles = []
-        rows = mine[0].shape[0]
-        for r in range(len(mine)):
-            at = r * rows if relative else pl.multiple_of((self.place[0] ^ r) * rows, rows)
-            where = target.at[pl.ds(at, rows)]
-            sem = self.sems.at[self.used]
-            self.used += 1
-
-            @pl.when(self.place[1] == self.layer)
-            def _(r=r, where=where, sem=sem):
-                pltpu.make_async_copy(mine[r], where, sem).start()
-
-            @pl.when(self.place[1] != self.layer)
-            def _(r=r, where=where, sem=sem):
-                pltpu.make_async_copy(other[r], where, sem).start()
-
-            handles.append(pltpu.make_async_copy(mine[r], where, sem))
-        return handles
+def assemble(place, parts):
+    count = len(parts)
+    rows, columns = parts[0].shape
+
+    def body(place_ref, *refs):
+        put_rows(refs[:count], refs[count], place_ref)
+
+    outs = [shape((rows * count, columns))]
+    moved = 4 * rows * count * columns
+    return call(body, outs, [smem] + [vmem] * count, [], 0, moved, "assemble")(place, *parts)[0]
+
+
+def fetch(place_ref, layer, mine, other, target, sems, span=None):
+    rows, columns = mine.shape
+    span = columns if span is None else span
+    handles = []
+    for k, at in enumerate(range(0, columns, span)):
+        lanes = pl.ds(at, min(span, columns - at))
+        where = target.at[pl.ds(0, rows), lanes]
+        for own, source in ((True, mine), (False, other)):
+
+            @pl.when((place_ref[1] == layer) == own)
+            def _(source=source, lanes=lanes, where=where, k=k):
+                pltpu.make_async_copy(source.at[pl.ds(0, rows), lanes], where, sems.at[k]).start()
+
+        handles.append(pltpu.make_async_copy(mine.at[pl.ds(0, rows), lanes], where, sems.at[k]))
+    return handles
 
 
 def finish(handles):
@@ -141,23 +154,24 @@
     return high, middle, (rest - middle.astype(wide)).astype(half)
 
 
-def exact_sum(mask, values):
-    return sum(mm(mask, piece) for piece in three_way(values))
-
-
-def gate_rows(logits, length, rows):
-    at = lax.broadcasted_iota(jnp.int32, (rows, LANES), 0)
+def exact_sum(values, mask):
+    return sum(mm(piece, mask) for piece in three_way(values))
+
+
+def gate_lanes(logits, length):
+    rows = logits.shape[1]
+    at = lax.broadcasted_iota(jnp.int32, logits.shape, 1)
     starts = (at == 0) | (at == length)
     spill = jnp.log(1.0 + jnp.exp(-jnp.abs(logits)))
     log_keep = jnp.minimum(logits, 0.0) - spill
     keep = jnp.where(starts, 0.0, sig(logits))
     lose = jnp.where(starts, 1.0, sig(-logits))
-    return log_keep, keep, lose
-
-
-def totals(log_keep, rows):
-    below = lax.broadcasted_iota(jnp.int32, (rows, rows), 1) <= lax.broadcasted_iota(jnp.int32, (rows, rows), 0)
-    return exact_sum(below.astype(wide).astype(half), log_keep)
+    before = lax.broadcasted_iota(jnp.int32, (rows, rows), 0) <= lax.broadcasted_iota(jnp.int32, (rows, rows), 1)
+    return log_keep, keep, lose, exact_sum(log_keep, before.astype(wide).astype(half))
+
+
+def turned(values):
+    return jnp.concatenate([values, jnp.zeros((LANES - values.shape[0], values.shape[1]), wide)], axis=0).T
 
 
 def block_scores(i, block, head, size, inner, projected, fixed, total, total_t, inflow_t, length, scale):
@@ -186,7 +200,68 @@
     return q, k, v, fixed_k, fixed_v, weights, fixed_weights, fall, reach, both
 
 
-def mix_forward(layer, heads, size, place, parts, qkv_mine, qkv_other, out_mine, out_other, decay, bias, fixed):
+def mix_forward(layer, heads, size, place, parts, rows, gain, weights, decay, bias, fixed):
+    count = len(parts)
+    width = parts[0].shape[1]
+    total_rows, inner = rows * count, heads * size
+    scale = size ** (-0.5)
+    block = rows
+
+    def body(place_ref, *refs):
+        parts_in, refs = refs[:count], refs[count:]
+        (mine, other, o_mine, o_other), refs = refs[:4], refs[4:]
+        (gain_ref, decay_ref, bias_ref, fixed_ref), refs = refs[:4], refs[4:]
+        terms, refs = refs[:count], refs[count:]
+        combined, normed, projected, logits_out, weight, out_weight, whole, sems = refs
+        handles = fetch(place_ref, layer, mine, other, weight, sems, inner)
+        out_handles = fetch(place_ref, layer, o_mine, o_other, out_weight, sems.at[pl.ds(3, 1)])
+        for r, part in enumerate(parts_in):
+            values = part[0:rows, :].astype(wide)
+            root = lax.rsqrt(jnp.mean(values * values, axis=1, keepdims=True) + epsilon)
+            here = pl.ds(pl.multiple_of((place_ref[0] ^ r) * rows, rows), rows)
+            normed[here, :] = (values * root * gain_ref[...]).astype(half)
+        length = place_ref[2]
+        logits = mm_nt(decay_ref[...], normed[...]) + bias_ref[:, 0:1]
+        logits_out[...] = logits
+        log_keep, keep, lose, total_t = gate_lanes(logits, length)
+        total = turned(total_t)
+        inflow_t = jnp.sqrt(lose * (1.0 + keep))
+        for kind in range(3):
+            handles[kind].wait()
+            lanes = slice(kind * inner, (kind + 1) * inner)
+            projected[:, lanes] = mm(normed[...], weight[:, lanes]).astype(half)
+        for head in range(heads):
+            for i in range(count):
+                q, k, v, fixed_k, fixed_v, soft, fixed_soft, fall, reach, both = block_scores(
+                    i, block, head, size, inner, projected, fixed_ref, total, total_t, inflow_t, length, scale
+                )
+                mixed = mm(both, v) + mm(fixed_soft.astype(half), fixed_v)
+                combined[i * block : (i + 1) * block, head * size : (head + 1) * size] = mixed.astype(half)
+        finish(out_handles)
+        whole[...] = mm(combined[...], out_weight[...])
+        take_rows(whole, terms, place_ref)
+
+    outs = [shape((rows, width), wide if r == 0 else half) for r in range(count)] + [
+        shape((total_rows, inner)),
+        shape((total_rows, width)),
+        shape((total_rows, 3 * inner)),
+        shape((16, total_rows), wide),
+    ]
+    scratch = [
+        pltpu.VMEM((width, 3 * inner), half),
+        pltpu.VMEM((inner, width), half),
+        pltpu.VMEM((total_rows, width), wide),
+        pltpu.SemaphoreType.DMA((4,)),
+    ]
+    specs = [smem] + [vmem] * count + [anywhere] * 4 + [vmem] * 4
+    flops = 2 * total_rows * (width * 4 * inner + inner * total_rows * 2)
+    moved = 2 * (width * 3 * inner + total_rows * (2 * width + 4 * inner))
+    return call(body, outs, specs, scratch, flops, moved, "mix_forward")(
+        place, *parts, *weights, gain, decay, bias, fixed
+    )
+
+
+def mix_backward(layer, heads, size, place, parts, weights, decay, fixed, projected, logits, normed, gain):
     count = len(parts)
     rows, width = parts[0].shape
     total_rows, inner = rows * count, heads * size
@@ -194,84 +269,21 @@
     block = rows
 
     def body(place_ref, *refs):
-        parts_in, mine, other = refs[:count], refs[count : 2 * count], refs[2 * count : 3 * count]
-        o_mine, o_other, refs = refs[3 * count : 3 * count + 1], refs[3 * count + 1 : 3 * count + 2], refs[3 * count + 2 :]
-        decay_ref, bias_ref, fixed_ref, refs = refs[0], refs[1], refs[2], refs[3:]
-        terms, refs = refs[:count], refs[count:]
-        combined, normed, projected, logits_out, weight, out_weight, whole, sems = refs
-        loader = Loader(place_ref, layer, sems)
-        handles = loader.start(mine, other, weight)
-        out_handles = loader.start(o_mine, o_other, out_weight, relative=True)
-        put_rows(parts_in, normed, place_ref)
-        length = place_ref[2]
-        logits = mm(normed[...], decay_ref[...]) + bias_ref[...]
-        logits_out[...] = logits
-        log_keep, keep, lose = gate_rows(logits, length, total_rows)
-        total = totals(log_keep, total_rows)
-        total_t = total.T
-        inflow_t = jnp.sqrt(lose * (1.0 + keep)).T
-        finish(handles)
-        for kind in range(3):
-            lanes = slice(kind * inner, (kind + 1) * inner)
-            projected[:, lanes] = mm(normed[...], weight[:, lanes]).astype(half)
-        for head in range(heads):
-            for i in range(count):
-                q, k, v, fixed_k, fixed_v, weights, fixed_weights, fall, reach, both = block_scores(
-                    i, block, head, size, inner, projected, fixed_ref, total, total_t, inflow_t, length, scale
-                )
-                mixed = mm(both, v) + mm(fixed_weights.astype(half), fixed_v)
-                combined[i * block : (i + 1) * block, head * size : (head + 1) * size] = mixed.astype(half)
-        finish(out_handles)
-        whole[...] = mm(combined[...], out_weight[...])
-        take_rows(whole, terms, place_ref)
-
-    outs = [shape((rows, width), wide if r == 0 else half) for r in range(count)] + [
-        shape((total_rows, inner)),
-        shape((total_rows, width)),
-        shape((total_rows, 3 * inner)),
-        shape((total_rows, LANES), wide),
-    ]
-    scratch = [
-        pltpu.VMEM((width, 3 * inner), half),
-        pltpu.VMEM((inner, width), half),
-        pltpu.VMEM((total_rows, width), wide),
-        pltpu.SemaphoreType.DMA((count + 1,)),
-    ]
-    specs = [smem] + [vmem] * count + [anywhere] * (2 * count + 2) + [vmem] * 3
-    flops = 2 * total_rows * (width * 4 * inner + inner * total_rows * 2)
-    moved = 2 * (width * 3 * inner + total_rows * (2 * width + 4 * inner))
-    return call(body, outs, specs, scratch, flops, moved, "mix_forward")(
-        place, *parts, *outside(*qkv_mine, *qkv_other, out_mine, out_other), decay, bias, fixed
-    )
-
-
-def mix_backward(layer, heads, size, place, parts, out_mine, out_other, qkv_mine, qkv_other, decay, fixed, projected, logits, normed, gain):
-    count = len(parts)
-    rows, width = parts[0].shape
-    total_rows, inner = rows * count, heads * size
-    scale = size ** (-0.5)
-    block = rows
-
-    def body(place_ref, *refs):
         parts_in, refs = refs[:count], refs[count:]
-        o_mine, o_other, refs = refs[:1], refs[1:2], refs[2:]
-        mine, other, refs = refs[:count], refs[count : 2 * count], refs[2 * count :]
+        (mine, other, o_mine, o_other), refs = refs[:4], refs[4:]
         decay_ref, fixed_ref, projected, logits_ref, normed_ref, gain_ref = refs[:6]
         refs = refs[6:]
         terms, refs = refs[:count], refs[count:]
         branch, g_projected, g_logits_out, g_fixed, g_gain, refs = refs[0], refs[1], refs[2], refs[3], refs[4], refs[5:]
         weight, out_weight, combined, g_k, g_v, pulled, pushed, whole, sems = refs
-        loader = Loader(place_ref, layer, sems)
-        out_handles = loader.start(o_mine, o_other, out_weight, relative=True)
-        handles = loader.start(mine, other, weight)
+        out_handles = fetch(place_ref, layer, o_mine, o_other, out_weight, sems.at[pl.ds(1, 1)])
+        handles = fetch(place_ref, layer, mine, other, weight, sems.at[pl.ds(0, 1)])
         put_rows(parts_in, branch, place_ref)
         length = place_ref[2]
         logits = logits_ref[...]
-        log_keep, keep, lose = gate_rows(logits, length, total_rows)
-        total = totals(log_keep, total_rows)
-        total_t = total.T
-        inflow = jnp.sqrt(lose * (1.0 + keep))
-        inflow_t = inflow.T
+        log_keep, keep, lose, total_t = gate_lanes(logits, length)
+        total = turned(total_t)
+        inflow_t = jnp.sqrt(lose * (1.0 + keep))
         finish(out_handles)
         combined[...] = mm_nt(branch[...], out_weight[...]).astype(half)
         g_k[...] = jnp.zeros_like(g_k)
@@ -306,20 +318,20 @@
                 pushed[here, head : head + 1] = jnp.sum(pull * inflow_row, axis=1, keepdims=True)
         g_projected[:, inner : 2 * inner] = (g_k[...] * scale).astype(half)
         g_projected[:, 2 * inner : 3 * inner] = g_v[...].astype(half)
-        g_inflow = jnp.concatenate([pulled[...], jnp.zeros((LANES - 8, total_rows), wide)], axis=0).T
-        g_total = pushed[...] - inflow * g_inflow
-        above = lax.broadcasted_iota(jnp.int32, (total_rows, total_rows), 1) >= lax.broadcasted_iota(
-            jnp.int32, (total_rows, total_rows), 0
+        g_inflow = pulled[...]
+        g_total = pushed[...].T[0:16] - inflow_t * g_inflow
+        after = lax.broadcasted_iota(jnp.int32, (total_rows, total_rows), 0) >= lax.broadcasted_iota(
+            jnp.int32, (total_rows, total_rows), 1
         )
-        g_log = exact_sum(above.astype(wide).astype(half), g_total)
-        g_logits = g_log * sig(-logits) - g_inflow * keep * keep * lose / inflow
-        lane = lax.broadcasted_iota(jnp.int32, (total_rows, LANES), 1)
-        g_logits = jnp.where(lane < heads, g_logits, 0.0)
+        g_log = exact_sum(g_total, after.astype(wide).astype(half))
+        g_logits = g_log * sig(-logits) - g_inflow * keep * keep * lose / inflow_t
+        row = lax.broadcasted_iota(jnp.int32, g_logits.shape, 0)
+        g_logits = jnp.where(row < heads, g_logits, 0.0)
         g_logits_out[...] = g_logits
         finish(handles)
         high, middle, low = three_way(g_logits)
         whole[...] = (
-            mm_nt(g_projected[...], weight[...]) + mm_nt(high, decay_ref[...]) + mm_nt(middle, decay_ref[...])
+            mm_nt(g_projected[...], weight[...]) + mm_tn(high, decay_ref[...]) + mm_tn(middle, decay_ref[...])
         )
         pulls = jnp.sum(whole[...] * normed_ref[...].astype(wide), axis=0, keepdims=True) / gain_ref[...]
         g_gain[...] = jnp.broadcast_to(pulls, g_gain.shape)
@@ -328,7 +340,7 @@
     outs = [shape((rows, width), wide if r == 0 else half) for r in range(count)] + [
         shape((total_rows, width)),
         shape((total_rows, 3 * inner)),
-        shape((total_rows, LANES), wide),
+        shape((16, total_rows), wide),
         shape((fixed.shape[0], 2 * inner), wide),
         shape((8, width), wide),
     ]
@@ -338,16 +350,16 @@
         pltpu.VMEM((total_rows, inner), half),
         pltpu.VMEM((total_rows, inner), wide),
         pltpu.VMEM((total_rows, inner), wide),
-        pltpu.VMEM((8, total_rows), wide),
+        pltpu.VMEM((16, total_rows), wide),
         pltpu.VMEM((total_rows, LANES), wide),
         pltpu.VMEM((total_rows, width), wide),
-        pltpu.SemaphoreType.DMA((count + 1,)),
+        pltpu.SemaphoreType.DMA((2,)),
     ]
-    specs = [smem] + [vmem] * count + [anywhere] * 2 + [anywhere] * (2 * count) + [vmem] * 6
+    specs = [smem] + [vmem] * count + [anywhere] * 4 + [vmem] * 6
     flops = 2 * total_rows * (width * 4 * inner + inner * total_rows * 5)
     moved = 2 * (width * 4 * inner + total_rows * (5 * width + 6 * inner))
     return call(body, outs, specs, scratch, flops, moved, "mix_backward")(
-        place, *parts, *outside(out_mine, out_other, *qkv_mine, *qkv_other), decay, fixed, projected, logits, normed, gain
+        place, *parts, *weights, decay, fixed, projected, logits, normed, gain
     )
 
 
@@ -376,22 +388,20 @@
     return [(at, min(2 * LANES, columns - at)) for at in range(0, columns, 2 * LANES)]
 
 
-def feed_forward(layer, place, parts, gu_mine, gu_other, down_mine, down_other):
+def feed_forward(layer, place, parts, weights):
     count = len(parts)
     rows, width = parts[0].shape
     total_rows = rows * count
-    columns, hidden = gu_mine[0].shape[1], down_mine.shape[0]
+    columns, hidden = weights[0].shape[1], weights[2].shape[0]
     padded = -(-hidden // LANES) * LANES
 
     def body(place_ref, *refs):
         parts_in, refs = refs[:count], refs[count:]
-        mine, other, refs = refs[:count], refs[count : 2 * count], refs[2 * count :]
-        d_mine, d_other, refs = refs[:1], refs[1:2], refs[2:]
+        (mine, other, d_mine, d_other), refs = refs[:4], refs[4:]
         terms, normed, refs = refs[:count], refs[count], refs[count + 1 :]
         weight, down, active, whole, sems = refs
-        loader = Loader(place_ref, layer, sems)
-        handles = loader.start(mine, other, weight)
-        down_handles = loader.start(d_mine, d_other, down, relative=True)
+        handles = fetch(place_ref, layer, mine, other, weight, sems.at[pl.ds(0, 1)])
+        down_handles = fetch(place_ref, layer, d_mine, d_other, down, sems.at[pl.ds(1, 1)])
         put_rows(parts_in, normed, place_ref)
         if padded != hidden:
             down[hidden:, :] = jnp.zeros((padded - hidden, width), half)
@@ -410,34 +420,32 @@
         pltpu.VMEM((padded, width), half),
         pltpu.VMEM((total_rows, padded), half),
         pltpu.VMEM((total_rows, width), wide),
-        pltpu.SemaphoreType.DMA((count + 1,)),
+        pltpu.SemaphoreType.DMA((2,)),
     ]
-    specs = [smem] + [vmem] * count + [anywhere] * (2 * count + 2)
+    specs = [smem] + [vmem] * count + [anywhere] * 4
     flops = 2 * total_rows * width * (columns + hidden)
     moved = 2 * (width * (columns + hidden) + total_rows * 4 * width)
     return call(body, outs, specs, scratch, flops, moved, "feed_forward")(
-        place, *parts, *outside(*gu_mine, *gu_other, down_mine, down_other)
+        place, *parts, *weights
     )
 
 
-def feed_backward(layer, place, parts, normed_two, gain, gu_mine, gu_other, down_mine, down_other):
+def feed_backward(layer, place, parts, normed_two, gain, weights):
     count = len(parts)
     rows, width = parts[0].shape
     total_rows = rows * count
-    columns, hidden = gu_mine[0].shape[1], down_mine.shape[0]
+    columns, hidden = weights[0].shape[1], weights[2].shape[0]
     padded = -(-hidden // LANES) * LANES
 
     def body(place_ref, *refs):
         parts_in, refs = refs[:count], refs[count:]
         normed, gain_ref, refs = refs[0], refs[1], refs[2:]
-        mine, other, refs = refs[:count], refs[count : 2 * count], refs[2 * count :]
-        d_mine, d_other, refs = refs[:1], refs[1:2], refs[2:]
+        (mine, other, d_mine, d_other), refs = refs[:4], refs[4:]
         terms, refs = refs[:count], refs[count:]
         g_out, g_gates, active, g_gain, refs = refs[0], refs[1], refs[2], refs[3], refs[4:]
         weight, down, whole, sems = refs
-        loader = Loader(place_ref, layer, sems)
-        handles = loader.start(mine, other, weight)
-        down_handles = loader.start(d_mine, d_other, down, relative=True)
+        handles = fetch(place_ref, layer, mine, other, weight, sems.at[pl.ds(0, 1)])
+        down_handles = fetch(place_ref, layer, d_mine, d_other, down, sems.at[pl.ds(1, 1)])
         put_rows(parts_in, g_out, place_ref)
         finish(handles)
         finish(down_handles)
@@ -466,13 +474,13 @@
         pltpu.VMEM((width, columns), half),
         pltpu.VMEM((hidden, width), half),
         pltpu.VMEM((total_rows, width), wide),
-        pltpu.SemaphoreType.DMA((count + 1,)),
+        pltpu.SemaphoreType.DMA((2,)),
     ]
-    specs = [smem] + [vmem] * (count + 2) + [anywhere] * (2 * count + 2)
+    specs = [smem] + [vmem] * (count + 2) + [anywhere] * 4
     flops = 2 * total_rows * width * (2 * columns + hidden)
     moved = 2 * (width * (columns + hidden) + total_rows * (6 * width + columns + hidden))
     return call(body, outs, specs, scratch, flops, moved, "feed_backward")(
-        place, *parts, normed_two, gain, *outside(*gu_mine, *gu_other, down_mine, down_other)
+        place, *parts, normed_two, gain, *weights
     )
 
 
@@ -505,11 +513,35 @@
     )[0]
 
 
-def unpack_small(heads, slots, width, place, parts):
+def beside(rows, mine, other):
+    height, width = rows.shape
+    groups = 2 * mine.shape[0] // 16
+    across = width // LANES
+    below = 16 * -(-groups // across)
+
+    def body(rows_ref, mine_ref, other_ref, out):
+        out[0:height, :] = rows_ref[...]
+        out[height:, :] = jnp.zeros((below, width), half)
+        for g in range(groups):
+            ref, at = (mine_ref, g) if g < groups // 2 else (other_ref, g - groups // 2)
+            spot = (height + 16 * (g // across), LANES * (g % across))
+            out[spot[0] : spot[0] + 16, spot[1] : spot[1] + LANES] = ref[16 * at : 16 * at + 16, :]
+
+    outs = [shape((height + below, width))]
+    return call(body, outs, [vmem] * 3, [], 0, 1 << 20, "beside")(rows, mine, other)[0]
+
+
+def turn_bias(row):
+    at = lax.broadcasted_iota(jnp.int32, (16, LANES), 0) == lax.broadcasted_iota(jnp.int32, (16, LANES), 1)
+    return jnp.broadcast_to(jnp.sum(jnp.where(at, row, 0.0), axis=1, keepdims=True), (16, LANES))
+
+
+def unpack_small(heads, slots, height, rows, place, parts):
     count = len(parts)
-    rows = parts[0].shape[0] // 2
+    width = parts[0].shape[1]
     cut = width // count
     lanes = cut // LANES
+    across = width // LANES
     inner = heads * LANES
 
     def body(place_ref, *refs):
@@ -518,7 +550,10 @@
         for r, part in enumerate(ins):
             for k in range(2):
                 layer = place_ref[1] if k == 0 else 1 - place_ref[1]
-                held[layer, f ^ r] = part[k * rows : (k + 1) * rows, :].astype(wide)
+                for g in range(rows // 16):
+                    at = k * (rows // 16) + g
+                    top, left = height + 16 * (at // across), LANES * (at % across)
+                    held[layer, f ^ r, 16 * g : 16 * g + 16, :] = part[top : top + 16, left : left + LANES].astype(wide)
         at = 2 * lanes + 1 + 2 * place_ref[1]
         found = held[place_ref[1], place_ref[2], pl.ds(at, 2), :]
         length[...] = jnp.broadcast_to(found[0:1] * 64.0 + found[1:2], length.shape).astype(jnp.int32)
@@ -534,9 +569,9 @@
                     mine = [
                         jnp.sum(jnp.where(row == f * heads + h, group, 0.0), axis=0, keepdims=True) for h in range(heads)
                     ]
-                    mine.append(jnp.zeros((LANES - heads, LANES), wide))
-                    decay[at : at + LANES, :] = jnp.concatenate(mine, axis=0).T.astype(half)
-            bias[...] = held[layer, f, 2 * lanes : 2 * lanes + 1, :]
+                    mine.append(jnp.zeros((16 - heads, LANES), wide))
+                    decay[:, at : at + LANES] = jnp.concatenate(mine, axis=0).astype(half)
+            bias[...] = turn_bias(held[layer, f, 2 * lanes : 2 * lanes + 1, :])
             for kind in range(2):
                 source = kind * (count // 2) + f // 2
                 for h in range(heads):
@@ -547,8 +582,8 @@
     outs = [
         shape((1, width), wide),
         shape((1, width), wide),
-        shape((width, LANES)),
-        shape((1, LANES), wide),
+        shape((16, width)),
+        shape((16, LANES), wide),
         shape((slots, 2 * inner)),
     ] * 2 + [shape((8, LANES), jnp.int32)]
     scratch = [pltpu.VMEM((2, count, rows, LANES), wide)]
@@ -582,15 +617,6 @@
     return call(body, outs, [vmem] * len(inputs), [], 0, dims[0] * dims[1] * 20, "join_forward")(*inputs)
 
 
-def norm_rows(values, gain):
-    def body(values_ref, gain_ref, normed):
-        total = values_ref[...].astype(wide)
-        scale = lax.rsqrt(jnp.mean(total * total, axis=1, keepdims=True) + epsilon)
-        normed[...] = (total * scale * gain_ref[...]).astype(half)
-
-    return call(body, [shape(values.shape)], [vmem, vmem], [], 0, values.size * 4, "norm_rows")(values, gain)[0]
-
-
 def join_backward(terms, values, gain, onward):
     dims = terms[0].shape
 
@@ -623,12 +649,29 @@
         target[:, t * LANES : (t + 1) * LANES] = source[:, pl.ds(at, LANES)]
 
 
-def packer(packed, received):
+STRIPS = 4
+
+
+def strip_of(columns):
+    return SMALL * -(-(columns + SMALL) // (SMALL * STRIPS))
+
+
+def packer(packed):
     def put(at, value):
-        rows = value.shape[0]
-        if received is not None:
-            value = value + received[at : at + rows, :].astype(wide)
-        packed[at : at + rows, :] = value.astype(half)
+        packed[at : at + value.shape[0], :] = value.astype(half)
+
+    return put
+
+
+def strip_packer(packed, strip, chunk):
+    def put(t, at, value):
+        done = 0
+        while done < value.shape[0]:
+            k, row = divmod(at + done, strip)
+            size = min(value.shape[0] - done, strip - row)
+            where = k * chunk + t * strip + row
+            packed[where : where + size, :] = value[done : done + size].astype(half)
+            done += size
 
     return put
 
@@ -638,54 +681,55 @@
     return jnp.concatenate([found, jnp.zeros((SMALL - found.shape[0], LANES), wide)], axis=0)
 
 
-def grad_call(body, chunks, total, inputs, received, scratch, flops, name):
-    outs = [shape((b - a, LANES)) for a, b in split_rows(total, chunks)]
-    if received is not None:
-        inputs = inputs + [received]
+def grad_call(body, chunks, total, inputs, scratch, flops, name):
+    outs = [shape((total, LANES))] + [shape((b - a, LANES)) for a, b in split_rows(total, chunks)]
     scratch = scratch + [pltpu.VMEM((total, LANES), half)]
-    moved = sum(v.size * v.dtype.itemsize for v in inputs) + total * LANES * 2
+    moved = sum(v.size * v.dtype.itemsize for v in inputs) + total * LANES * 4
     return call(body, outs, [smem] + [vmem] * (len(inputs) - 1), scratch, flops, moved, name)(*inputs)
 
 
-def grad_feed(chunks, count, place, normed, g_gates, active, g_out, g_gain, received=None):
+def grad_feed(chunks, count, place, normed, g_gates, active, g_out, g_gain):
     total_rows, width = normed.shape
     columns, hidden = g_gates.shape[1], active.shape[1]
     tiles = columns // LANES
-    block = columns + SMALL
+    strip = strip_of(columns)
+    chunk = count * strip + hidden
     side = width // 2
 
     def body(place_ref, normed_ref, gates_ref, active_ref, g_out_ref, gain_ref, *refs):
-        left, packed = refs[-2:]
-        got, outs = (None, refs[:-2]) if received is None else (refs[0], refs[1:-2])
-        which = 1 - place_ref[1] if received is None else place_ref[1]
-        put = packer(packed, got)
-        lane_half(normed_ref, left, which, count)
-        turned = left[...].T
-        for at in range(0, columns, 2 * LANES):
-            size = min(2 * LANES, columns - at)
-            tile = mm(turned, gates_ref[:, at : at + size])
+        sent, outs, left, packed = refs[0], refs[1:-2], refs[-2], refs[-1]
+        for turn in range(2):
+            which = 1 - place_ref[1] if turn == 0 else place_ref[1]
+            packed_here = sent if turn == 0 else packed
+            put, put_row = packer(packed_here), strip_packer(packed_here, strip, chunk)
+            lane_half(normed_ref, left, which, count)
+            turned = left[...].T
+            for at in range(0, columns, 2 * LANES):
+                size = min(2 * LANES, columns - at)
+                tile = mm(turned, gates_ref[:, at : at + size])
+                for t in range(count):
+                    for c in range(size // LANES):
+                        put_row(t, at + c * LANES, tile[t * LANES : (t + 1) * LANES, c * LANES : (c + 1) * LANES])
             for t in range(count):
-                for c in range(size // LANES):
-                    put(t * block + at + c * LANES, tile[t * LANES : (t + 1) * LANES, c * LANES : (c + 1) * LANES])
-        for t in range(count):
-            at = pl.multiple_of(t * 2 * LANES + which * LANES, LANES)
-            put(t * block + columns, small_rows([gain_ref[0:1, pl.ds(at, LANES)]]))
-        active_t = active_ref[...].T
-        for c in range(0, side // LANES, 2):
-            at = pl.multiple_of(which * side + c * LANES, LANES)
-            tile = mm(active_t, g_out_ref[:, pl.ds(at, 2 * LANES)])
-            put(count * block + c * hidden, tile[:, :LANES])
-            put(count * block + (c + 1) * hidden, tile[:, LANES:])
+                at = pl.multiple_of(t * 2 * LANES + which * LANES, LANES)
+                rest = STRIPS * strip - columns - SMALL
+                put_row(t, columns, small_rows([gain_ref[0:1, pl.ds(at, LANES)]]))
+                put_row(t, columns + SMALL, jnp.zeros((rest, LANES), wide))
+            active_t = active_ref[...].T
+            for c in range(0, side // LANES, 2):
+                at = pl.multiple_of(which * side + c * LANES, LANES)
+                tile = mm(active_t, g_out_ref[:, pl.ds(at, 2 * LANES)])
+                put(c * chunk + count * strip, tile[:, :LANES])
+                put((c + 1) * chunk + count * strip, tile[:, LANES:])
         chunk_out(packed, outs)
 
-    local = (side // LANES) * hidden
     inputs = [place, normed, g_gates, active, g_out, g_gain]
     scratch = [pltpu.VMEM((total_rows, side), half)]
     flops = total_rows * width * (columns + hidden)
-    return grad_call(body, chunks, count * block + local, inputs, received, scratch, flops, "grad_feed")
-
-
-def grad_mix(chunks, count, place, normed, g_projected, combined, branch, g_logits, g_gain, g_fixed, received=None):
+    return grad_call(body, chunks, STRIPS * chunk, inputs, scratch, flops, "grad_feed")
+
+
+def grad_mix(chunks, total, count, place, normed, g_projected, combined, branch, g_logits, g_gain, g_fixed):
     total_rows, width = normed.shape
     columns, inner = g_projected.shape[1], combined.shape[1]
     heads = inner // LANES
@@ -694,44 +738,44 @@
     side = width // 2
 
     def body(place_ref, normed_ref, proj_ref, comb_ref, branch_ref, logits_ref, gain_ref, fixed_ref, *refs):
-        left, packed = refs[-2:]
-        got, outs = (None, refs[:-2]) if received is None else (refs[0], refs[1:-2])
-        which = 1 - place_ref[1] if received is None else place_ref[1]
-        put = packer(packed, got)
-        lane_half(normed_ref, left, which, count)
-        turned = left[...].T
-        for at in range(0, columns, 2 * LANES):
-            tile = mm(turned, proj_ref[:, at : at + 2 * LANES])
+        sent, outs, left, packed = refs[0], refs[1:-2], refs[-2], refs[-1]
+        for turn in range(2):
+            which = 1 - place_ref[1] if turn == 0 else place_ref[1]
+            put = packer(sent if turn == 0 else packed)
+            lane_half(normed_ref, left, which, count)
+            turned = left[...].T
+            for at in range(0, columns, 2 * LANES):
+                tile = mm(turned, proj_ref[:, at : at + 2 * LANES])
+                for t in range(count):
+                    for c in range(2):
+                        put(t * block + at + c * LANES, tile[t * LANES : (t + 1) * LANES, c * LANES : (c + 1) * LANES])
+            logits = logits_ref[...]
+            decay = sum(mm(piece, left[...]) for piece in three_way(logits)[:2])
+            near = pl.multiple_of(which * LANES, LANES)
             for t in range(count):
-                for c in range(2):
-                    put(t * block + at + c * LANES, tile[t * LANES : (t + 1) * LANES, c * LANES : (c + 1) * LANES])
-        logits = logits_ref[...]
-        logits_t = logits.T
-        decay = sum(mm(piece, left[...]) for piece in three_way(logits_t)[:2])
-        near = pl.multiple_of(which * LANES, LANES)
-        for t in range(count):
-            at = pl.multiple_of(t * 2 * LANES + which * LANES, LANES)
-            rows = [decay[0:heads, t * LANES : (t + 1) * LANES], gain_ref[0:1, pl.ds(at, LANES)]]
-            put(t * block + columns, small_rows(rows))
-            keys_here = (place_ref[0] // 2 == t).astype(wide)
-            values_here = (place_ref[0] // 2 + 2 == t).astype(wide)
-            fixed = fixed_ref[:, pl.ds(near, LANES)] * keys_here
-            fixed = fixed + fixed_ref[:, pl.ds(pl.multiple_of(inner + near, LANES), LANES)] * values_here
-            put(t * block + columns + SMALL, fixed)
-        comb_t = comb_ref[:, pl.ds(near, LANES)].T
-        for c in range(0, width // LANES, 2):
-            tile = mm(comb_t, branch_ref[:, c * LANES : (c + 2) * LANES])
-            put(count * block + c * LANES, tile[:, :LANES])
-            put(count * block + (c + 1) * LANES, tile[:, LANES:])
-        put(count * block + width, small_rows([jnp.sum(logits, axis=0, keepdims=True)]))
-        packed[count * block + width + SMALL :, :] = jnp.zeros((SMALL, LANES), half)
+                at = pl.multiple_of(t * 2 * LANES + which * LANES, LANES)
+                rows = [decay[0:heads, t * LANES : (t + 1) * LANES], gain_ref[0:1, pl.ds(at, LANES)]]
+                put(t * block + columns, small_rows(rows))
+                keys_here = (place_ref[0] // 2 == t).astype(wide)
+                values_here = (place_ref[0] // 2 + 2 == t).astype(wide)
+                fixed = fixed_ref[:, pl.ds(near, LANES)] * keys_here
+                fixed = fixed + fixed_ref[:, pl.ds(pl.multiple_of(inner + near, LANES), LANES)] * values_here
+                put(t * block + columns + SMALL, fixed)
+            comb_t = comb_ref[:, pl.ds(near, LANES)].T
+            for c in range(0, width // LANES, 2):
+                tile = mm(comb_t, branch_ref[:, c * LANES : (c + 2) * LANES])
+                put(count * block + c * LANES, tile[:, :LANES])
+                put(count * block + (c + 1) * LANES, tile[:, LANES:])
+            put(count * block + width, jnp.broadcast_to(jnp.sum(logits, axis=1, keepdims=True), (SMALL, LANES)))
+            (sent if turn == 0 else packed)[count * block + width + SMALL :, :] = jnp.zeros(
+                (total - count * block - width - SMALL, LANES), half
+            )
         chunk_out(packed, outs)
 
-    local = width + 2 * SMALL
     inputs = [place, normed, g_projected, combined, branch, g_logits, g_gain, g_fixed]
     scratch = [pltpu.VMEM((total_rows, side), half)]
     flops = total_rows * width * (columns + inner)
-    return grad_call(body, chunks, count * block + local, inputs, received, scratch, flops, "grad_mix")
+    return grad_call(body, chunks, total, inputs, scratch, flops, "grad_mix")
 
 
 def split_rows(total, chunks):
@@ -747,12 +791,17 @@
         at += out.shape[0]
 
 
-def spread(count, block, place, chunks):
+def spread(count, block, place, chunks, add=False):
     total = sum(chunk.shape[0] for chunk, _ in chunks)
 
     def body(place_ref, *refs):
         ins, outs, whole = refs[: 2 * len(chunks)], refs[2 * len(chunks) : -1], refs[-1]
-        for inner in range(2):
+        at = 0
+        if add:
+            for one, two in zip(ins[0::2], ins[1::2]):
+                whole[at : at + one.shape[0], :] = (one[...].astype(wide) + two[...].astype(wide)).astype(half)
+                at += one.shape[0]
+        for inner in range(0 if add else 2):
 
             @pl.when(place_ref[3] == inner)
             def _(inner=inner):
@@ -770,32 +819,64 @@
     return call(body, outs, [smem] + [vmem] * len(flat), scratch, 0, total * 768, "spread")(place, *flat)
 
 
-def collect_feed(chunks, place, parts, local):
-    count = len(parts)
-    columns = parts[0].shape[0] - SMALL
-    total = count * columns + SMALL + local.shape[0]
+def spread_strips(count, strip, place, chunks):
+    chunk = chunks[0][0].shape[0]
+    own = chunk - count * strip
+    many = len(chunks)
 
     def body(place_ref, *refs):
-        parts_in, local_ref, outs, whole = refs[:count], refs[count], refs[count + 1 : -1], refs[-1]
-        for r, part in enumerate(parts_in):
-            at = pl.multiple_of((place_ref[0] ^ r) * columns, columns)
-            whole[pl.ds(at, columns), :] = part[0:columns, :]
-        small = sum(part[columns:, :].astype(wide) for part in parts_in)
+        ins, outs = refs[: 2 * many], refs[2 * many :]
+        for inner in range(2):
+
+            @pl.when(place_ref[3] == inner)
+            def _(inner=inner):
+                for k, ref in enumerate(ins[1 - inner :: 2]):
+                    for r in range(count):
+                        at = pl.multiple_of((place_ref[0] ^ r) * strip, SMALL)
+                        outs[r][k * strip : (k + 1) * strip, :] = ref[pl.ds(at, strip), :]
+                    outs[count][k * own : (k + 1) * own, :] = ref[count * strip :, :]
+
+    outs = [shape((many * strip, LANES))] * count + [shape((many * own, LANES))]
+    flat = [piece for pair in chunks for piece in pair]
+    return call(body, outs, [smem] + [vmem] * len(flat), [], 0, many * chunk * 768, "spread")(place, *flat)
+
+
+def collect_feed(columns, place, sets):
+    count = len(sets[0][0])
+    strip = strip_of(columns)
+    own = sum(local.shape[0] for _, local in sets)
+    total = count * columns + SMALL + own
+    flat = [piece for parts, local in sets for piece in (*parts, local)]
+
+    def body(place_ref, *refs):
+        ins, whole = refs[: len(flat)], refs[-1]
+        first, below = 0, count * columns + SMALL
+        small = jnp.zeros((SMALL, LANES), wide)
+        for number, (parts, local) in enumerate(sets):
+            here = ins[number * (count + 1) : (number + 1) * (count + 1)]
+            many = parts[0].shape[0] // strip
+            for k in range(many):
+                row = (first + k) * strip
+                size = min(strip, columns - row)
+                for r in range(count):
+                    at = pl.multiple_of((place_ref[0] ^ r) * columns + row, SMALL)
+                    whole[pl.ds(at, size), :] = here[r][k * strip : k * strip + size, :]
+                    if size < strip:
+                        small = small + here[r][k * strip + size : k * strip + size + SMALL, :].astype(wide)
+            first += many
+            whole[below : below + local.shape[0], :] = here[count][...]
+            below += local.shape[0]
         whole[count * columns : count * columns + SMALL, :] = small.astype(half)
-        whole[count * columns + SMALL :, :] = local_ref[...]
-        chunk_out(whole, outs)
-
-    outs = [shape((b - a, LANES)) for a, b in split_rows(total, chunks)]
-    return call(body, outs, [smem] + [vmem] * (count + 1), [pltpu.VMEM((total, LANES), half)], 0, total * 512, "collect_feed")(
-        place, *parts, local
-    )
-
-
-def collect_mix(chunks, heads, place, parts, local):
+
+    outs = [shape((total, LANES))]
+    return call(body, outs, [smem] + [vmem] * len(flat), [], 0, total * 512, "collect_feed")(place, *flat)
+
+
+def collect_mix(chunks, heads, total, place, parts, local):
     count = len(parts)
     slots = parts[0].shape[0] % (3 * heads * LANES) - SMALL
     columns = parts[0].shape[0] - SMALL - slots
-    total = count * columns + SMALL + 2 * slots + local.shape[0]
+    filled = count * columns + SMALL + 2 * slots + local.shape[0]
 
     def body(place_ref, *refs):
         parts_in, local_ref, outs, whole, few = refs[:count], refs[count], refs[count + 1 : -2], refs[-2], refs[-1]
@@ -812,12 +893,32 @@
         for k in range(2):
             at = base + SMALL + k * slots
             whole[at : at + slots, :] = few[near + k, SMALL:, :].astype(half)
-        whole[base + SMALL + 2 * slots :, :] = local_ref[...]
+        whole[base + SMALL + 2 * slots : filled, :] = local_ref[...]
+        whole[filled:, :] = jnp.zeros((total - filled, LANES), half)
         chunk_out(whole, outs)
 
     outs = [shape((b - a, LANES)) for a, b in split_rows(total, chunks)]
     scratch = [pltpu.VMEM((total, LANES), half), pltpu.VMEM((count, SMALL + slots, LANES), wide)]
     return call(body, outs, [smem] + [vmem] * (count + 1), scratch, 0, total * 512, "collect_mix")(place, *parts, local)
+
+
+def gather_halves(place_ref, ins, halves, sems, edges):
+    chunks = len(edges) - 1
+    handles = []
+    for side in range(2):
+        for c in range(chunks):
+            spot = place_ref[1] if side == 0 else 1 - place_ref[1]
+            where = halves.at[spot, pl.ds(edges[c], edges[c + 1] - edges[c])]
+            sem = sems.at[side * chunks + c]
+            for layer in range(2):
+                source = ins[layer * 2 * chunks + side * chunks + c]
+
+                @pl.when(place_ref[1] == layer)
+                def _(source=source, where=where, sem=sem):
+                    pltpu.make_async_copy(source, where, sem).start()
+
+            handles.append(pltpu.make_async_copy(ins[side * chunks + c], where, sem))
+    finish(handles)
 
 
 def unpack(body, totals, out_shape, place, name):
@@ -828,21 +929,7 @@
 
     def whole_body(place_ref, *refs):
         ins, outs, halves, sems = refs[: 4 * chunks], refs[4 * chunks : -2], refs[-2], refs[-1]
-        handles = []
-        for side in range(2):
-            for c in range(chunks):
-                spot = place_ref[1] if side == 0 else 1 - place_ref[1]
-                where = halves.at[spot, pl.ds(edges[c], edges[c + 1] - edges[c])]
-                sem = sems.at[side * chunks + c]
-                for layer in range(2):
-                    source = ins[layer * 2 * chunks + side * chunks + c]
-
-                    @pl.when(place_ref[1] == layer)
-                    def _(source=source, where=where, sem=sem):
-                        pltpu.make_async_copy(source, where, sem).start()
-
-                handles.append(pltpu.make_async_copy(ins[side * chunks + c], where, sem))
-        finish(handles)
+        gather_halves(place_ref, ins, halves, sems, edges)
         body(place_ref, halves, *outs)
 
     inputs = [piece for layer in totals for side in layer for piece in side]
@@ -854,27 +941,64 @@
 def unpack_feed(count, columns, hidden, width, totals, place):
     part = width // count
     side = width // 2
-    tiles = columns // LANES
-
-    def body(place_ref, halves, gate_up, down, gain):
+    chunks = len(totals[0][0])
+    edges = [0]
+    for chunk in totals[0][0]:
+        edges.append(edges[-1] + chunk.shape[0])
+    steps = 4
+    span = count * columns // steps
+    tiles = span // LANES
+
+    def body(place_ref, *refs):
+        ins, (gate_up, down, gain), halves, sems = refs[: 4 * chunks], refs[4 * chunks : -2], refs[-2], refs[-1]
+        step = pl.program_id(0)
+
+        @pl.when(step == 0)
+        def _():
+            gather_halves(place_ref, ins, halves, sems, edges)
+            base = count * columns
+            for h in range(2):
+                gain[0:1, h * LANES : (h + 1) * LANES] = halves[h, base : base + SMALL, :].astype(wide)[0:1]
+
         low = lax.broadcasted_iota(jnp.int32, (LANES, LANES), 1) < PAIR
-        middle = gate_up.shape[1] // 2
-        for h in range(2):
-            rows = slice(h * LANES, (h + 1) * LANES)
-            for m in range(middle // LANES):
-                even = halves[h, 2 * m * LANES : (2 * m + 1) * LANES, :].astype(wide)
-                odd = halves[h, (2 * m + 1) * LANES : (2 * m + 2) * LANES, :].astype(wide)
-                gate_up[rows, m * LANES : (m + 1) * LANES] = jnp.where(low, even, pltpu.roll(odd, PAIR, 1))
-                gate_up[rows, middle + m * LANES : middle + (m + 1) * LANES] = jnp.where(low, pltpu.roll(even, PAIR, 1), odd)
-            base = count * columns
-            gain[0:1, h * LANES : (h + 1) * LANES] = halves[h, base : base + SMALL, :].astype(wide)[0:1]
-            base += SMALL
-            for c in range(side // LANES):
-                at = h * side + c * LANES
-                down[:, at : at + LANES] = halves[h, base + c * hidden : base + (c + 1) * hidden, :].astype(wide)
+        for is_up in range(2):
+
+            @pl.when(step // 2 == is_up)
+            def _(is_up=is_up):
+                for h in range(2):
+                    for m in range(tiles):
+                        at = pl.multiple_of((step % 2) * 2 * span + 2 * m * LANES, LANES)
+                        even = halves[h, pl.ds(at, LANES), :].astype(wide)
+                        odd = halves[h, pl.ds(at + LANES, LANES), :].astype(wide)
+                        if is_up:
+                            value = jnp.where(low, pltpu.roll(even, PAIR, 1), odd)
+                        else:
+                            value = jnp.where(low, even, pltpu.roll(odd, PAIR, 1))
+                        gate_up[h * LANES : (h + 1) * LANES, m * LANES : (m + 1) * LANES] = value
+
+        base = count * columns + SMALL
+        for c in range(2):
+            at = pl.multiple_of(base + ((step % 2) * 2 + c) * hidden, SMALL)
+            down[:, c * LANES : (c + 1) * LANES] = halves[step // 2, pl.ds(at, hidden), :].astype(wide)
 
     outs = [shape((part, count * columns), wide), shape((hidden, width), wide), shape((1, part), wide)]
-    return unpack(body, totals, outs, place, "unpack_feed")
+    inputs = [piece for layer in totals for half_side in layer for piece in half_side]
+    moved = sum(o.size * 4 for o in outs) + 4 * edges[-1] * LANES
+    return pl.pallas_call(
+        body,
+        grid=(steps,),
+        out_shape=outs,
+        in_specs=[smem] + [anywhere] * len(inputs),
+        out_specs=[
+            pl.BlockSpec((part, span), lambda i: (0, i)),
+            pl.BlockSpec((hidden, width // steps), lambda i: (0, i)),
+            pl.BlockSpec((1, part), lambda i: (0, 0)),
+        ],
+        scratch_shapes=[pltpu.VMEM((2, edges[-1], LANES), half), pltpu.SemaphoreType.DMA((2 * chunks,))],
+        compiler_params=pltpu.CompilerParams(vmem_limit_bytes=16 * 1024 * 1024),
+        cost_estimate=pl.CostEstimate(flops=0, bytes_accessed=moved, transcendentals=0),
+        name="unpack_feed",
+    )(place, *inputs)
 
 
 def unpack_mix(count, heads, slots, width, totals, place):
@@ -905,7 +1029,8 @@
                 source = base + c * LANES
                 out[rows, c * LANES : (c + 1) * LANES] = halves[h, source : source + LANES, :].astype(wide)
             if h == 0:
-                bias[...] = halves[h, base + width : base + width + SMALL, :].astype(wide)[0:1, 0:heads]
+                found = halves[h, base + width : base + width + SMALL, :].astype(wide)
+                bias[...] = jnp.concatenate([found[k : k + 1, 0:1] for k in range(heads)], axis=1)
 
     outs = [
         shape((part, count * columns), wide),
@@ -962,41 +1087,52 @@
     def own_batch(value):
         return lax.dynamic_index_in_dim(value, section, 0, False)[0]
 
-    pairs = [(c * count + f, f * ctx_count + c) for c in range(ctx_count) for f in range(count)]
+    pairs = []
+    for s in range(2):
+        flip = s * (count - 1)
+        for c in range(ctx_count):
+            for f in range(count):
+                here, there = c * count + f, (f ^ flip) * count + (c ^ flip)
+                pairs.append((s * ctx_count * count + here, s * ctx_count * count + there))
 
     def turn_plane(value):
-        return lax.ppermute(value, ("ctx", "fsdp"), pairs)
+        return lax.ppermute(value, ("section", "ctx", "fsdp"), pairs)
 
     def swap(value):
         return exchange(value, "section", 1)
 
     slots = persistent.shape[1]
-    spot = jnp.stack([fsdp, section, ctx]).astype(jnp.int32)
+    flip = section * (count - 1)
+    spot = jnp.stack([fsdp, section, ctx ^ flip]).astype(jnp.int32)
     x_own, qkv_shard = tie(own_batch(tokens), qkv_weight[0])
     x_in = turn_plane(x_own)
     qkv_packed = pack_heads(count, qkv_shard, spot)
-    qkv_mine = trade_parts(qkv_packed, "fsdp")
+    qkv_parts = trade_parts(qkv_packed, "fsdp")
     small = pack_small(norm_one, norm_two, decay_weight[0], decay_bias, persistent[0], lengths[:, 0, 0])
-    small, qkv_packed = tie(small, qkv_packed)
-    smalls = gather_parts(jnp.concatenate([small, swap(small)]), "fsdp")
-    (gains_one, gains_two, decays, biases, fixeds), length = unpack_small(heads, slots, width, spot, smalls)
-    place = jnp.stack([fsdp, section, length, (ctx == 1) | (ctx == 2)]).astype(jnp.int32)
+    x_parts = gather_parts(beside(x_in, small, swap(small)), "fsdp")
+    (gains_one, gains_two, decays, biases, fixeds), length = unpack_small(
+        heads, slots, rows, small.shape[0], spot, x_parts
+    )
+    gu_packed = pack_gates(count, gate_up[0], spot)
+    qkv_parts, gu_packed, _, g_own = tie(qkv_parts, gu_packed, x_parts, own_batch(cotangent))
+    g_in = turn_plane(g_own)
+    gu_parts = trade_parts(gu_packed, "fsdp")
+    qkv_mine = assemble(spot, qkv_parts)
+    qkv_other = swap(qkv_mine)
     out_mine = out_weight[0]
     out_other = swap(out_mine)
-    gu_packed = pack_gates(count, gate_up[0], spot)
-    x_parts = gather_parts(norm_rows(x_in, gains_one[0]), "fsdp")
-    qkv_mine, x_parts, gu_packed, g_own = tie(qkv_mine, x_parts, gu_packed, own_batch(cotangent))
-    qkv_other = [swap(piece) for piece in qkv_mine]
-    gu_mine = trade_parts(gu_packed, "fsdp")
+    mix_weights = (qkv_mine, qkv_other, out_mine, out_other)
     down_mine = down_weight[0]
     down_other = swap(down_mine)
-    g_in = turn_plane(g_own)
+    length, down_other = tie(length, down_other)
+    place = jnp.stack([fsdp, section, length, (ctx == 1) | (ctx == 2)]).astype(jnp.int32)
+    seat = jnp.stack([fsdp ^ flip, section, length]).astype(jnp.int32)
     hidden = down_mine.shape[0]
-    columns = gu_mine[0].shape[1]
+    columns = gu_packed[0].shape[1]
 
     def mix_first_half(layer, parts):
         *terms, combined, seen, projected, logits = mix_forward(
-            layer, heads, size, place, parts, qkv_mine, qkv_other, out_mine, out_other, decays[layer], biases[layer], fixeds[layer]
+            layer, heads, size, seat, parts, rows, gains_one[layer], mix_weights, decays[layer], biases[layer], fixeds[layer]
         )
         return terms, (seen, projected, logits, combined)
 
@@ -1005,16 +1141,13 @@
         return middle, gather_parts(normed_two, "fsdp")
 
     def feed_step(layer, parts, saved):
-        *terms, g_rows, g_gates, active, g_gain = feed_backward(
-            layer, place, parts, saved[6], gains_two[layer], gu_mine, gu_other, down_mine, down_other
-        )
+        *terms, g_rows, g_gates, active, g_gain = feed_backward(layer, seat, parts, saved[6], gains_two[layer], feed_weights)
         return terms, (saved[6], g_gates, active, g_rows, g_gain)
 
     def mix_step(layer, parts, saved):
         x, seen, projected, logits, combined, middle, seen_two = saved
         *terms, branch, g_projected, g_logits, g_fixed, g_gain = mix_backward(
-            layer, heads, size, place, parts, out_mine, out_other, qkv_mine, qkv_other,
-            decays[layer], fixeds[layer], projected, logits, seen, gains_one[layer],
+            layer, heads, size, seat, parts, mix_weights, decays[layer], fixeds[layer], projected, logits, seen, gains_one[layer]
         )
         return terms, (seen, g_projected, combined, branch, g_logits, g_gain, g_fixed)
 
@@ -1050,7 +1183,7 @@
     def plus(a, b):
         return (a.astype(wide) + b.astype(wide)).astype(half)
 
-    def step(*held, more=()):
+    def step(*held, more=None):
         landed, crossed = line["flight"]
         waiting = [v for v in (landed, crossed) if v is not None]
         held, waiting = tie(held, waiting)
@@ -1063,96 +1196,130 @@
         line["across"] = None if own is None else plus(own, landed)
         if closing:
             line["sums"].append((sent, landed))
-        line["queue"].extend(more)
+        if more is not None:
+            line["queue"].extend(more(*held))
         ready, route = begin()
         held, ready = tie(held, ready)
         go(ready, route)
         return held
 
-    def taken(number):
-        found, line["sums"] = line["sums"][:number], line["sums"][number:]
+    def taken(number, skip=0):
+        found = line["sums"][skip : skip + number]
+        del line["sums"][skip : skip + number]
         return found
 
     terms, kept = mix_first_half(0, x_parts)
-    terms, gu_mine = tie(terms, gu_mine)
-    gu_other = [swap(piece) for piece in gu_mine]
-    middle, parts = mix_second_half(0, terms, x_in)
-    *terms, seen_two = feed_forward(0, place, parts, gu_mine, gu_other, down_mine, down_other)
+    terms, gu_parts[1], g_in = tie(terms, gu_parts[1], g_in)
+    terms, gu_parts = tie(trade_parts(terms, "fsdp"), gu_parts)
+    gu_mine = assemble(spot, gu_parts)
+    feed_weights = (gu_mine, swap(gu_mine), down_mine, down_other)
+    middle, normed_two = join_forward(False, terms, x_in, gains_two[0])
+    parts = gather_parts(normed_two, "fsdp")
+    *terms, seen_two = feed_forward(0, seat, parts, feed_weights)
+    terms = trade_parts(terms, "fsdp")
     saved_first = (x_in, *kept, middle, seen_two)
-    between, normed = join_forward(True, trade_parts(terms, "fsdp"), middle, gains_one[1])
-    terms, kept = mix_first_half(1, gather_parts(normed, "fsdp"))
-    terms, g_parts = tie(terms, gather_parts(g_in, "fsdp"))
+    between = join_forward(True, terms, middle, None)[0]
+    terms, kept = mix_first_half(1, gather_parts(between, "fsdp"))
+    terms, g_three, g_two, g_one = tie(terms, *(exchange(g_in, "fsdp", r) for r in (3, 2, 1)))
     middle, parts = mix_second_half(1, terms, between)
-    *terms_out, seen_two = feed_forward(1, place, parts, gu_mine, gu_other, down_mine, down_other)
+    *terms_out, seen_two = feed_forward(1, seat, parts, feed_weights)
     saved_second = (between, *kept, middle, seen_two)
-    terms, feed = feed_step(1, g_parts, saved_second)
-    out = join_forward(True, trade_parts(terms_out, "fsdp"), middle, None)[0]
-    terms, out = tie(terms, out)
-    out = turn_plane(out)
-    other = grad_feed(1, count, place, *feed)[0]
-    terms, other, out = tie(trade_parts(terms, "fsdp"), other, out)
+    terms, feed = feed_step(1, [g_in, g_one, g_two, g_three], saved_second)
+
+    def to_owner(layer, chunks):
+        return [lax.ppermute(chunk, "section", [(1 - layer, layer)]) for chunk in chunks]
+
+    def trade(block, chunks, add=False):
+        *blocks, local = spread(count, block, place, chunks, add)
+        return trade_parts(blocks, "fsdp"), local
+
+    def trade_strips(chunks):
+        *blocks, local = spread_strips(count, strip, place, chunks)
+        return trade_parts(blocks, "fsdp"), local
+
+    strip = strip_of(columns)
+    pad = 2 * (count * strip + hidden)
+    mix_block = 3 * inner + SMALL + slots
+
+    def summed(own, received):
+        at, chunks = 0, []
+        for chunk in own:
+            chunks.append(plus(chunk, received[at : at + chunk.shape[0]]))
+            at += chunk.shape[0]
+        return chunks
+
+    sent, *own = grad_feed(4, count, place, *feed)
+    terms, sent = tie(trade_parts(terms, "fsdp"), sent)
     g_middle, g_branch = join_backward(terms, saved_second[5], gains_two[1], g_in)
     parts = gather_parts(g_branch, "fsdp")
-    f1 = grad_feed(4, count, place, *feed, received=swap(other))
-    (parts,) = step(parts, more=f1)
+    parts, received = tie(parts, swap(sent))
+    (parts,) = step(parts, more=lambda _: summed(own, received))
     terms, mix = mix_step(1, parts, saved_second)
-    (terms,) = step(terms)
-    other = grad_mix(1, count, place, *mix)[0]
-    terms, other = step(trade_parts(terms, "fsdp"), other)
+    terms, terms_out = step(terms, trade_parts(terms_out, "fsdp"))
+    out = join_forward(True, terms_out, saved_second[5], None)[0]
+    sent, *own = grad_mix(2, pad, count, place, *mix)
+    terms, sent = step(trade_parts(terms, "fsdp"), sent)
     g_middle, g_branch = join_backward(terms, between, gains_one[1], g_middle)
-    parts = gather_parts(g_branch, "fsdp")
-    m1 = grad_mix(2, count, place, *mix, received=swap(other))
-    (parts,) = step(parts, more=m1)
+    parts, sent = step(gather_parts(g_branch, "fsdp"), sent)
     terms, feed = feed_step(0, parts, saved_first)
-    (terms,) = step(terms)
-    other = grad_feed(1, count, place, *feed)[0]
-    terms, other = step(trade_parts(terms, "fsdp"), other)
+    terms, _ = step(terms, swap(sent), more=lambda _, received: summed(own, received))
+    sent, *own = grad_feed(4, count, place, *feed)
+    terms, sent = step(trade_parts(terms, "fsdp"), sent)
+    received = swap(sent)
     g_middle, g_branch = join_backward(terms, saved_first[5], gains_two[0], g_branch)
-    parts = gather_parts(g_branch, "fsdp")
-    f0 = grad_feed(4, count, place, *feed, received=swap(other))
-    (parts,) = step(parts, more=f0)
+    g_branch, received = tie(g_branch, received)
+    (parts,) = step(gather_parts(g_branch, "fsdp"), more=lambda _: summed(own, received))
+    f1 = trade_strips(taken(4))
     terms, mix = mix_step(0, parts, saved_first)
-    (terms,) = step(terms)
-    other = grad_mix(1, count, place, *mix)[0]
-    received = swap(other)
-    terms, received = step(trade_parts(terms, "fsdp"), received)
-    m0 = grad_mix(2, count, place, *mix, received=received)
+    terms, f1 = step(terms, f1)
+    feed_second = collect_feed(columns, place, [f1])
+    sent, *own = grad_mix(1, pad, count, place, *mix)
+    (terms,) = step(trade_parts(terms, "fsdp"))
     g_input = join_backward(terms, x_in, gains_one[0], g_middle)[1]
-
-    def trade(block, chunks):
-        *blocks, local = spread(count, block, place, chunks)
-        return trade_parts(blocks, "fsdp"), local
-
-    feed_block = columns + SMALL
-    mix_block = 3 * inner + SMALL + slots
-    f1 = trade(feed_block, taken(4))
-    g_input, f1 = step(g_input, f1, more=m0)
-    feed_second = collect_feed(1, place, *f1)
+    received = swap(sent)
+    g_input, received, feed_second = step(g_input, received, feed_second)
+    m0 = trade(mix_block, [(own[0], received)], add=True)
+    (m0,) = step(m0, more=lambda pieces: collect_mix(2, heads, pad, place, *pieces))
+    f0 = trade_strips(taken(2, 2))
+    (f0,) = step(f0)
     m1 = trade(mix_block, taken(2))
-    feed_second, m1 = step(feed_second, m1)
-    mix_second = collect_mix(1, heads, place, *m1)
-    (mix_second,) = step(mix_second)
-    (mix_second,) = step(mix_second)
-    (mix_second,) = step(mix_second)
-    f0 = trade(feed_block, taken(4))
-    g_input, f0 = step(g_input, f0)
-    g_input = turn_plane(g_input)
-    m0 = trade(mix_block, taken(2))
-    feed_first = collect_feed(1, place, *f0)
-    mix_first = collect_mix(1, heads, place, *m0)
-
-    def owned(layer, chunks):
-        return chunks, [lax.ppermute(chunk, "section", [(1 - layer, layer)]) for chunk in chunks]
-
+    (m1,) = step(m1)
+    feed_second_other = to_owner(1, feed_second)
+    f0_last = trade_strips(taken(2))
+    mix_second = collect_mix(2, heads, pad, place, *m1)
+    f0_last, mix_second, g_input = step(f0_last, mix_second, g_input)
+    feed_first = collect_feed(columns, place, [f0, f0_last])
+    feed_first_other = to_owner(0, feed_first)
+    m0_first = [jnp.where(inside, *pair) for pair in taken(1)]
+    m0_first_other = to_owner(0, m0_first)
+    mix_second_other = to_owner(1, mix_second)
+    feed_first_other, feed_second_other, m0_first_other, mix_second_other, g_input, out = step(
+        feed_first_other, feed_second_other, m0_first_other, mix_second_other, g_input, out
+    )
+    m0_last = [jnp.where(inside, *pair) for pair in taken(1)]
+    m0_last_other = to_owner(0, m0_last)
+    out, g_turned = turn_plane(out), turn_plane(g_input)
     grad_gate_up, grad_down, grad_norm_two = unpack_feed(
-        count, columns, hidden, width, (owned(0, feed_first), owned(1, feed_second)), place
+        count,
+        columns,
+        hidden,
+        width,
+        ((feed_first, feed_first_other), (feed_second, feed_second_other)),
+        place,
     )
+    m0_last_other, grad_down = tie(m0_last_other, grad_down)
     grad_qkv, grad_out, grad_norm_one, grad_decay, grad_bias, grad_fixed = unpack_mix(
-        count, heads, slots, width, (owned(0, mix_first), owned(1, mix_second)), place
+        count,
+        heads,
+        slots,
+        width,
+        ((m0_first + m0_last, m0_first_other + m0_last_other), (mix_second, mix_second_other)),
+        place,
     )
+    out, g_turned, grad_bias = tie(out, g_turned, grad_bias)
     return (
         out[None, None],
-        g_input[None, None],
+        g_turned[None, None],
         grad_norm_one,
         grad_qkv[None],
         grad_decay[None],

time: 566 us -> 513 us (0.906)
  waiting for transfers between devices: 248 us -> 209 us
  starting transfers between devices: 172 us -> 155 us
  Pallas kernels: 111 us -> 99.5 us
  local copies, waits for them, and re-layouts: 18.2 us -> 29.7 us
    ppermute x84 -> x78, waiting for transfers between devices: 194 us -> 162 us  [exchange(): return lax.ppermute(value, axis, [(i, i ^ distance) for i in range(count)])]
    ppermute x84 -> x78, starting transfers between devices: 103 us -> 89.1 us  [exchange(): return lax.ppermute(value, axis, [(i, i ^ distance) for i in range(count)])]
    ppermute x8 -> x10, waiting for transfers between devices: 25.7 us -> 12.4 us  [the longest x4 12.3 us: turn_plane(): return lax.ppermute(value, ('section', 'ctx', 'fsdp'), pairs)]
    unnamed x83 -> x192, local copies, waits for them, and re-layouts: 16.7 us -> 26.7 us
    pallas_call x3 -> x9, Pallas kernels: 4.24 us -> 12 us  [the longest x1 5.11 us: unpack_feed(): pl.pallas_call(body, grid=(steps,), out_shape=outs, in_specs=[smem] + [an...]
    ppermute x14, waiting for transfers between devices: 27.8 us -> 35.4 us  [go(): flight[0] = lax.ppermute(sent, 'ctx', route)]
    pallas_call x2 -> x1, Pallas kernels: 10.3 us -> 3.08 us  [unpack(): call(whole_body, out_shape, [smem] + [anywhere] * len(inputs), scratch, 0...]
    pallas_call x8 -> x4, Pallas kernels: 16.4 us -> 12.2 us  [grad_call(): call(body, outs, [smem] + [vmem] * (len(inputs) - 1), scratch, flops, mov...]
  transfers between devices with their start and end apart: 118 -> 114, of which waited for: 57 -> 54; matrix products, arithmetic and copies ran while one was open for 1% -> 1% of each run, Pallas kernels for 15% -> 15%
where the time goes in v2:
time: 513 us; the launch traced here: 504 us
  waiting for transfers between devices  209 us (41%)
  starting transfers between devices  155 us (30%)
  Pallas kernels  99.5 us (19%)
  local copies, waits for them, and re-layouts  29.7 us (6%)
  other arithmetic  7.32 us (1%)
    ppermute x78, waiting for transfers between devices, exchange(): return lax.ppermute(value, axis, [(i, i ^ distance) for i in range(count)])  162 us
    ppermute x78, starting transfers between devices, exchange(): return lax.ppermute(value, axis, [(i, i ^ distance) for i in range(count)])  89.1 us
    ppermute x14, waiting for transfers between devices, go(): flight[0] = lax.ppermute(sent, 'ctx', route)  35.4 us
    ppermute x14, starting transfers between devices, go(): flight[0] = lax.ppermute(sent, 'ctx', route)  34.1 us
    unnamed x192, local copies, waits for them, and re-layouts  26.7 us
    pallas_call x2, Pallas kernels, mix_backward(): call(body, outs, specs, scratch, flops, moved, 'mix_backward')  17.8 us
    pallas_call x2, Pallas kernels, feed_backward(): call(body, outs, specs, scratch, flops, moved, 'feed_backward')  16.2 us
    pallas_call x2, Pallas kernels, mix_forward(): call(body, outs, specs, scratch, flops, moved, 'mix_forward')  15.3 us
  transfers between devices with their start and end apart: 114, of which 54 were waited for; matrix products, arithmetic and copies ran while one was open for 1% of the time, Pallas kernels for 15%

profile of v2, /device:TPU:2, one launch (start us, length us, event | category | flops | bytes accessed | tf_op | source)
XLA Modules:
  0.0 504.0 jit_solution(14113580266637431148)
XLA Ops:
  6.4 4.9 collective-permute-start
  24.9 16.7 %collective-permute-done.7.refs_2_ = bf16[256,768]{1,0:T(8,128)(2,1)} collective-permute-done((bf16[256,768]{1,0:T(8,128)(2,1)}, bf16[256,768]{1,0:T(8,128)(2,1)}, u32[]{:S(2)}, u32[]{:S(2)}) %collective-permute-start.7) | collective-permute-done | bytes 393248 | tf_op jit(solution)/shard_map/ppermute | solution.py:1052
  69.1 7.7 %mix_forward.2 = (f32[128,1024]{1,0:T(8,128)S(1)}, bf16[128,1024]{1,0:T(8,128)(2,1)S(1)}, bf16[128,1024]{1,0:T(8,128)(2,1)S(1)}, bf16[128,1024]{1,0:T(8,128)(2,1...) custom-call(s32[3]{0:T(128)S(1)} %pad_add_fusion.2.place_ref, ...), custom_call_target="tpu_custom_call" | custom-call | flops 1342177280 | bytes 4718592 | tf_op jit(solution)/shard_map/mix_forward/pallas_call | solution.py:259
  80.7 8.8 %collective-permute-done.16.refs_2_ = bf16[256,1408]{1,0:T(8,128)(2,1)} collective-permute-done((bf16[256,1408]{1,0:T(8,128)(2,1)}, bf16[256,1408]{1,0:T(8,128)(2,1)}, u32[]{:S(2)}, u32[]{:S(2)}) %collective-permute-start.16) | collective-permute-done | bytes 720928 | tf_op jit(solution)/shard_map/ppermute | solution.py:1052
  89.4 6.3 %collective-permute-done.13.refs_1_ = bf16[128,1024]{1,0:T(8,128)(2,1)S(1)} collective-permute-done((bf16[128,1024]{1,0:T(8,128)(2,1)S(1)}, bf16[128,1024]{1,0:T(8,128)(2,1)S(1)}, u32[]{:S(2)}, u32[]{:S(2)}) %collective-permute-start.13) | collective-permute-done | bytes 262176 | tf_op jit(solution)/shard_map/ppermute | solution.py:1052
  111.8 5.5 %collective-permute-done.19.refs_2_ = bf16[128,1024]{1,0:T(8,128)(2,1)S(1)} collective-permute-done((bf16[128,1024]{1,0:T(8,128)(2,1)S(1)}, bf16[128,1024]{1,0:T(8,128)(2,1)S(1)}, u32[]{:S(2)}, u32[]{:S(2)}) %collective-permute-start.19) | collective-permute-done | bytes 262176 | tf_op jit(solution)/shard_map/ppermute | solution.py:1052
  126.2 5.7 %collective-permute-done.22.refs_1_ = bf16[128,1024]{1,0:T(8,128)(2,1)S(1)} collective-permute-done((bf16[128,1024]{1,0:T(8,128)(2,1)S(1)}, bf16[128,1024]{1,0:T(8,128)(2,1)S(1)}, u32[]{:S(2)}, u32[]{:S(2)}) %collective-permute-start.22) | collective-permute-done | bytes 262176 | tf_op jit(solution)/shard_map/ppermute | solution.py:1052
  131.9 4.9 collective-permute-done.23.refs_2_
  153.8 7.7 %mix_forward.3 = (f32[128,1024]{1,0:T(8,128)S(1)}, bf16[128,1024]{1,0:T(8,128)(2,1)S(1)}, bf16[128,1024]{1,0:T(8,128)(2,1)S(1)}, bf16[128,1024]{1,0:T(8,128)(2,1...) custom-call(s32[3]{0:T(128)S(1)} %pad_add_fusion.2.place_ref, ...), custom_call_target="tpu_custom_call" | custom-call | flops 1342177280 | bytes 4718592 | tf_op jit(solution)/shard_map/mix_forward/pallas_call | solution.py:259
  167.5 5.5 %collective-permute-done.31.refs_1_ = bf16[128,1024]{1,0:T(8,128)(2,1)S(1)} collective-permute-done((bf16[128,1024]{1,0:T(8,128)(2,1)S(1)}, bf16[128,1024]{1,0:T(8,128)(2,1)S(1)}, u32[]{:S(2)}, u32[]{:S(2)}) %collective-permute-start.31) | collective-permute-done | bytes 262176 | tf_op jit(solution)/shard_map/ppermute | solution.py:1052
  193.6 8.6 %feed_backward.2 = (f32[128,1024]{1,0:T(8,128)S(1)}, bf16[128,1024]{1,0:T(8,128)(2,1)}, bf16[128,1024]{1,0:T(8,128)(2,1)}, bf16[128,1024]{1,0:T(8,128)(2,1)}, bf...) custom-call(s32[3]{0:T(128)S(1)} %pad_add_fusion.2.place_ref, ...), custom_call_target="tpu_custom_call" | custom-call | flops 3690987520 | bytes 12779520 | tf_op jit(solution)/shard_map/feed_backward/pallas_call | solution.py:482
  225.6 6.6 %collective-permute-done.42.refs_3_ = bf16[128,1024]{1,0:T(8,128)(2,1)S(1)} collective-permute-done((bf16[128,1024]{1,0:T(8,128)(2,1)S(1)}, bf16[128,1024]{1,0:T(8,128)(2,1)S(1)}, u32[]{:S(2)}, u32[]{:S(2)}) %collective-permute-start.42) | collective-permute-done | bytes 262176 | tf_op jit(solution)/shard_map/ppermute | solution.py:1052
  232.1 5.1 %collective-permute-done.41.refs_2_ = bf16[128,1024]{1,0:T(8,128)(2,1)S(1)} collective-permute-done((bf16[128,1024]{1,0:T(8,128)(2,1)S(1)}, bf16[128,1024]{1,0:T(8,128)(2,1)S(1)}, u32[]{:S(2)}, u32[]{:S(2)}) %collective-permute-start.41) | collective-permute-done | bytes 262176 | tf_op jit(solution)/shard_map/ppermute | solution.py:1052
  244.2 8.8 %mix_backward.2 = (f32[128,1024]{1,0:T(8,128)S(1)}, bf16[128,1024]{1,0:T(8,128)(2,1)S(1)}, bf16[128,1024]{1,0:T(8,128)(2,1)S(1)}, bf16[128,1024]{1,0:T(8,128)(2,...) custom-call(s32[3]{0:T(128)S(1)} %copy-done.74, ...), custom_call_target="tpu_custom_call" | custom-call | flops 1744830464 | bytes 8912896 | tf_op jit(solution)/shard_map/mix_backward/pallas_call | solution.py:361
  280.1 5.9 %collective-permute-done.55.refs_3_ = bf16[128,1024]{1,0:T(8,128)(2,1)S(1)} collective-permute-done((bf16[128,1024]{1,0:T(8,128)(2,1)S(1)}, bf16[128,1024]{1,0:T(8,128)(2,1)S(1)}, u32[]{:S(2)}, u32[]{:S(2)}) %collective-permute-start.55) | collective-permute-done | bytes 262176 | tf_op jit(solution)/shard_map/ppermute | solution.py:1052
  292.5 7.7 %feed_backward.3 = (f32[128,1024]{1,0:T(8,128)S(1)}, bf16[128,1024]{1,0:T(8,128)(2,1)S(1)}, bf16[128,1024]{1,0:T(8,128)(2,1)S(1)}, bf16[128,1024]{1,0:T(8,128)(2...) custom-call(s32[3]{0:T(128)S(1)} %copy-done.74, ...), custom_call_target="tpu_custom_call" | custom-call | flops 3690987520 | bytes 12779520 | tf_op jit(solution)/shard_map/feed_backward/pallas_call | solution.py:482
  332.1 7.7 %collective-permute-done.70.refs_7_ = bf16[2176,128]{1,0:T(8,128)(2,1)S(1)} collective-permute-done((bf16[2176,128]{1,0:T(8,128)(2,1)S(1)}, bf16[2176,128]{1,0:T(8,128)(2,1)S(1)}, u32[]{:S(2)}, u32[]{:S(2)}) %collective-permute-start.70) | collective-permute-done | bytes 557088 | tf_op jit(solution)/shard_map/ppermute | solution.py:1178
  351.3 9.0 %mix_backward.3 = (f32[128,1024]{1,0:T(8,128)S(1)}, bf16[128,1024]{1,0:T(8,128)(2,1)S(1)}, bf16[128,1024]{1,0:T(8,128)(2,1)S(1)}, bf16[128,1024]{1,0:T(8,128)(2,...) custom-call(s32[3]{0:T(128)S(1)} %copy-done.74, ...), custom_call_target="tpu_custom_call" | custom-call | flops 1744830464 | bytes 8912896 | tf_op jit(solution)/shard_map/mix_backward/pallas_call | solution.py:361
  360.3 6.8 %collective-permute-done.73.refs_2_ = bf16[1472,128]{1,0:T(8,128)(2,1)S(1)} collective-permute-done((bf16[1472,128]{1,0:T(8,128)(2,1)S(1)}, bf16[1472,128]{1,0:T(8,128)(2,1)S(1)}, u32[]{:S(2)}, u32[]{:S(2)}) %collective-permute-start.73) | collective-permute-done | bytes 376864 | tf_op jit(solution)/shard_map/ppermute | solution.py:1052
  389.1 7.3 %collective-permute-done.83.refs_1_ = bf16[2176,128]{1,0:T(8,128)(2,1)S(1)} collective-permute-done((bf16[2176,128]{1,0:T(8,128)(2,1)S(1)}, bf16[2176,128]{1,0:T(8,128)(2,1)S(1)}, u32[]{:S(2)}, u32[]{:S(2)}) %collective-permute-start.83) | collective-permute-done | bytes 557088 | tf_op jit(solution)/shard_map/ppermute | solution.py:1178
  461.6 15.5 %collective-permute-done.110 = bf16[2176,128]{1,0:T(8,128)(2,1)S(1)} collective-permute-done((bf16[2176,128]{1,0:T(8,128)(2,1)S(1)}, bf16[2176,128]{1,0:T(8,128)(2,1)S(1)}, u32[]{:S(2)}, u32[]{:S(2)}) %collective-permute-start.110) | collective-permute-done | bytes 557088 | tf_op jit(solution)/shard_map/ppermute | solution.py:1178
  480.5 4.8 collective-permute-start.112
  485.3 5.1 %unpack_feed.1 = (f32[256,5632]{1,0:T(8,128)}, f32[704,1024]{1,0:T(8,128)}, f32[1,256]{1,0:T(1,128)}) custom-call(s32[4]{0:T(128)S(1)} %pad_add_fusion.1.place_ref, bf16[8464,128]{1,0:T(8,128)(2,1)S(1)} %collect_feed.3.refs_0_, bf16[8464,128]{1,0:T(8,128)(2,1)S(1)} %collective-permute-done.105.refs_1_, bf16[8464,128]{1,0:T(8,128)(2,1)S(1)} %collect_feed.2.refs_2_, ...), custom_call_target="tpu_custom_call" | custom-call | bytes 12985344 | tf_op jit(solution)/shard_map/unpack_feed/pallas_call | solution.py:987
  493.6 5.4 %collective-permute-done.111 = bf16[128,1024]{1,0:T(8,128)(2,1)S(1)} collective-permute-done((bf16[128,1024]{1,0:T(8,128)(2,1)S(1)}, bf16[128,1024]{1,0:T(8,128)(2,1)S(1)}, u32[]{:S(2)}, u32[]{:S(2)}) %collective-permute-start.111) | collective-permute-done | bytes 262176 | tf_op jit(solution)/shard_map/ppermute | solution.py:1099
  (467 shorter events, 323.5 us)
Async XLA Ops:
  6.4 17.9 %collective-permute-start.6 = (bf16[256,768]{1,0:T(8,128)(2,1)}, bf16[256,768]{1,0:T(8,128)(2,1)}, u32[]{:S(2)}, u32[]{:S(2)}) collective-permute-start(bf16[256,768]{1,0:T(8,128)(2,1)} %get-tuple-element.419), channel_id=1, source_target_pairs={{0,1},{1,0},{2,3},{3,2},{4,5},{5,4},{6,7},{7,6},{8,9},{9,8},{10,11... | collective-permute-start | bytes 1179656 | tf_op jit(solution)/shard_map/ppermute | solution.py:1052
  11.3 30.3 %collective-permute-start.7 = (bf16[256,768]{1,0:T(8,128)(2,1)}, bf16[256,768]{1,0:T(8,128)(2,1)}, u32[]{:S(2)}, u32[]{:S(2)}) collective-permute-start(bf16[256,768]{1,0:T(8,128)(2,1)} %get-tuple-element.420), channel_id=1, source_target_pairs={{0,2},{1,3},{2,0},{3,1},{4,6},{5,7},{6,4},{7,5},{8,10},{9,11},{10,... | collective-permute-start | bytes 1179656 | tf_op jit(solution)/shard_map/ppermute | solution.py:1052
  14.9 31.5 %collective-permute-start.8 = (bf16[256,768]{1,0:T(8,128)(2,1)}, bf16[256,768]{1,0:T(8,128)(2,1)}, u32[]{:S(2)}, u32[]{:S(2)}) collective-permute-start(bf16[256,768]{1,0:T(8,128)(2,1)} %get-tuple-element.421), channel_id=1, source_target_pairs={{0,3},{1,2},{2,1},{3,0},{4,7},{5,6},{6,5},{7,4},{8,11},{9,10},{10,... | collective-permute-start | bytes 1179656 | tf_op jit(solution)/shard_map/ppermute | solution.py:1052
  21.1 25.2 %collective-permute-start.4 = (bf16[160,1024]{1,0:T(8,128)(2,1)S(1)}, bf16[160,1024]{1,0:T(8,128)(2,1)S(1)}, u32[]{:S(2)}, u32[]{:S(2)}) collective-permute-start(bf16[160,1024]{1,0:T(8,128)(2,1)S(1)} %beside.1.refs_0_), channel_id=1, source_target_pairs={{0,3},{1,2},{2,1},{3,0},{4,7},{5,6},{6,5},{7,4},{8,11},{9,10},{10,... | collective-permute-start | bytes 983048 | tf_op jit(solution)/shard_map/ppermute | solution.py:1052
  24.3 22.5 %collective-permute-start.3 = (bf16[160,1024]{1,0:T(8,128)(2,1)S(1)}, bf16[160,1024]{1,0:T(8,128)(2,1)S(1)}, u32[]{:S(2)}, u32[]{:S(2)}) collective-permute-start(bf16[160,1024]{1,0:T(8,128)(2,1)S(1)} %beside.1.refs_0_), channel_id=1, source_target_pairs={{0,2},{1,3},{2,0},{3,1},{4,6},{5,7},{6,4},{7,5},{8,10},{9,11},{10,... | collective-permute-start | bytes 983048 | tf_op jit(solution)/shard_map/ppermute | solution.py:1052
  24.3 22.5 %collective-permute-start.2 = (bf16[160,1024]{1,0:T(8,128)(2,1)S(1)}, bf16[160,1024]{1,0:T(8,128)(2,1)S(1)}, u32[]{:S(2)}, u32[]{:S(2)}) collective-permute-start(bf16[160,1024]{1,0:T(8,128)(2,1)S(1)} %beside.1.refs_0_), channel_id=1, source_target_pairs={{0,1},{1,0},{2,3},{3,2},{4,5},{5,4},{6,7},{7,6},{8,9},{9,8},{10,11... | collective-permute-start | bytes 983048 | tf_op jit(solution)/shard_map/ppermute | solution.py:1052
  48.4 17.7 %collective-permute-start.9 = (bf16[1024,768]{1,0:T(8,128)(2,1)S(1)}, bf16[1024,768]{1,0:T(8,128)(2,1)S(1)}, u32[]{:S(2)}, u32[]{:S(2)}) collective-permute-start(bf16[1024,768]{1,0:T(8,128)(2,1)S(1)} %assemble.2.refs_4_), channel_id=1, source_target_pairs={{0,16},{16,0},{1,17},{17,1},{2,18},{18,2},{3,19},{19,3},{4,20},{20... | collective-permute-start | bytes 4718600 | tf_op jit(solution)/shard_map/ppermute | solution.py:1052
  49.1 27.8 %collective-permute-start.11 = (bf16[256,1408]{1,0:T(8,128)(2,1)}, bf16[256,1408]{1,0:T(8,128)(2,1)}, u32[]{:S(2)}, u32[]{:S(2)}) collective-permute-start(bf16[256,1408]{1,0:T(8,128)(2,1)} %get-tuple-element.438), channel_id=1, source_target_pairs={{0,1},{1,0},{2,3},{3,2},{4,5},{5,4},{6,7},{7,6},{8,9},{9,8},{10,11... | collective-permute-start | bytes 2162696 | tf_op jit(solution)/shard_map/ppermute | solution.py:1052
  51.8 37.6 %collective-permute-start.16 = (bf16[256,1408]{1,0:T(8,128)(2,1)}, bf16[256,1408]{1,0:T(8,128)(2,1)}, u32[]{:S(2)}, u32[]{:S(2)}) collective-permute-start(bf16[256,1408]{1,0:T(8,128)(2,1)} %get-tuple-element.447), channel_id=1, source_target_pairs={{0,2},{1,3},{2,0},{3,1},{4,6},{5,7},{6,4},{7,5},{8,10},{9,11},{10,... | collective-permute-start | bytes 2162696 | tf_op jit(solution)/shard_map/ppermute | solution.py:1052
  54.0 35.4 %collective-permute-start.17 = (bf16[256,1408]{1,0:T(8,128)(2,1)}, bf16[256,1408]{1,0:T(8,128)(2,1)}, u32[]{:S(2)}, u32[]{:S(2)}) collective-permute-start(bf16[256,1408]{1,0:T(8,128)(2,1)} %get-tuple-element.448), channel_id=1, source_target_pairs={{0,3},{1,2},{2,1},{3,0},{4,7},{5,6},{6,5},{7,4},{8,11},{9,10},{10,... | collective-permute-start | bytes 2162696 | tf_op jit(solution)/shard_map/ppermute | solution.py:1052
  58.2 18.6 %collective-permute-start.12 = (bf16[128,1024]{1,0:T(8,128)(2,1)}, bf16[128,1024]{1,0:T(8,128)(2,1)}, u32[]{:S(2)}, u32[]{:S(2)}) collective-permute-start(bf16[128,1024]{1,0:T(8,128)(2,1)} %dynamic-slice_bitcast_fusion), channel_id=1, source_target_pairs={{0,0},{1,4},{2,8},{3,12},{4,1},{5,5},{6,9},{7,13},{8,2},{9,6},{10,... | collective-permute-start | bytes 786440 | tf_op jit(solution)/shard_map/ppermute | solution.py:1099
  76.8 18.9 %collective-permute-start.13 = (bf16[128,1024]{1,0:T(8,128)(2,1)S(1)}, bf16[128,1024]{1,0:T(8,128)(2,1)S(1)}, u32[]{:S(2)}, u32[]{:S(2)}) collective-permute-start(bf16[128,1024]{1,0:T(8,128)(2,1)S(1)} %get-tuple-element.442), channel_id=1, source_target_pairs={{0,1},{1,0},{2,3},{3,2},{4,5},{5,4},{6,7},{7,6},{8,9},{9,8},{10,11... | collective-permute-start | bytes 786440 | tf_op jit(solution)/shard_map/ppermute | solution.py:1052
  77.6 21.8 %collective-permute-start.14 = (bf16[128,1024]{1,0:T(8,128)(2,1)S(1)}, bf16[128,1024]{1,0:T(8,128)(2,1)S(1)}, u32[]{:S(2)}, u32[]{:S(2)}) collective-permute-start(bf16[128,1024]{1,0:T(8,128)(2,1)S(1)} %get-tuple-element.443), channel_id=1, source_target_pairs={{0,2},{1,3},{2,0},{3,1},{4,6},{5,7},{6,4},{7,5},{8,10},{9,11},{10,... | collective-permute-start | bytes 786440 | tf_op jit(solution)/shard_map/ppermute | solution.py:1052
  79.3 20.1 %collective-permute-start.15 = (bf16[128,1024]{1,0:T(8,128)(2,1)S(1)}, bf16[128,1024]{1,0:T(8,128)(2,1)S(1)}, u32[]{:S(2)}, u32[]{:S(2)}) collective-permute-start(bf16[128,1024]{1,0:T(8,128)(2,1)S(1)} %get-tuple-element.444), channel_id=1, source_target_pairs={{0,3},{1,2},{2,1},{3,0},{4,7},{5,6},{6,5},{7,4},{8,11},{9,10},{10,... | collective-permute-start | bytes 786440 | tf_op jit(solution)/shard_map/ppermute | solution.py:1052
  141.4 21.1 %collective-permute-start.30 = (bf16[128,1024]{1,0:T(8,128)(2,1)}, bf16[128,1024]{1,0:T(8,128)(2,1)S(1)}, u32[]{:S(2)}, u32[]{:S(2)}) collective-permute-start(bf16[128,1024]{1,0:T(8,128)(2,1)} %collective-permute-done.12.refs_0_.refs_6_), channel_id=1, source_target_pairs={{0,1},{1,0},{2,3},{3,2},{4,5},{5,4},{6,7},{7,6},{8,9},{9,8},{10,11... | collective-permute-start | bytes 786440 | tf_op jit(solution)/shard_map/ppermute | solution.py:1052
  142.7 19.8 %collective-permute-start.29 = (bf16[128,1024]{1,0:T(8,128)(2,1)}, bf16[128,1024]{1,0:T(8,128)(2,1)S(1)}, u32[]{:S(2)}, u32[]{:S(2)}) collective-permute-start(bf16[128,1024]{1,0:T(8,128)(2,1)} %collective-permute-done.12.refs_0_.refs_6_), channel_id=1, source_target_pairs={{0,2},{1,3},{2,0},{3,1},{4,6},{5,7},{6,4},{7,5},{8,10},{9,11},{10,... | collective-permute-start | bytes 786440 | tf_op jit(solution)/shard_map/ppermute | solution.py:1052
  305.5 18.1 %collective-permute-start.64 = (bf16[2176,128]{1,0:T(8,128)(2,1)S(1)}, bf16[2176,128]{1,0:T(8,128)(2,1)S(1)}, u32[]{:S(2)}, u32[]{:S(2)}) collective-permute-start(bf16[2176,128]{1,0:T(8,128)(2,1)S(1)} %fusion.2.refs_4_), channel_id=1, source_target_pairs={{0,4},{12,8},{4,0},{8,12},{1,5},{13,9},{5,1},{9,13},{2,6},{14,10},... | collective-permute-start | bytes 1671176 | tf_op jit(solution)/shard_map/ppermute | solution.py:1178
  344.0 23.1 %collective-permute-start.75 = (bf16[2176,128]{1,0:T(8,128)(2,1)S(1)}, bf16[2176,128]{1,0:T(8,128)(2,1)S(1)}, u32[]{:S(2)}, u32[]{:S(2)}) collective-permute-start(bf16[2176,128]{1,0:T(8,128)(2,1)S(1)} %fusion.4.refs_0_), channel_id=1, source_target_pairs={{0,4},{12,8},{4,0},{8,12},{1,5},{13,9},{5,1},{9,13},{2,6},{14,10},... | collective-permute-start | bytes 1671176 | tf_op jit(solution)/shard_map/ppermute | solution.py:1178
  346.3 20.8 %collective-permute-start.76 = (bf16[2176,128]{1,0:T(8,128)(2,1)S(1)}, bf16[2176,128]{1,0:T(8,128)(2,1)S(1)}, u32[]{:S(2)}, u32[]{:S(2)}) collective-permute-start(bf16[2176,128]{1,0:T(8,128)(2,1)S(1)} %add_convert_fusion.16), channel_id=1, source_target_pairs={{4,8},{8,4},{5,9},{9,5},{6,10},{10,6},{7,11},{11,7},{20,24},{24,20... | collective-permute-start | bytes 1671176 | tf_op jit(solution)/shard_map/ppermute | solution.py:1180
  348.9 18.2 %collective-permute-start.73 = (bf16[1472,128]{1,0:T(8,128)(2,1)S(1)}, bf16[1472,128]{1,0:T(8,128)(2,1)S(1)}, u32[]{:S(2)}, u32[]{:S(2)}) collective-permute-start(bf16[1472,128]{1,0:T(8,128)(2,1)S(1)} %get-tuple-element.642), channel_id=1, source_target_pairs={{0,2},{1,3},{2,0},{3,1},{4,6},{5,7},{6,4},{7,5},{8,10},{9,11},{10,... | collective-permute-start | bytes 1130504 | tf_op jit(solution)/shard_map/ppermute | solution.py:1052
  452.8 24.4 %collective-permute-start.105 = (bf16[8464,128]{1,0:T(8,128)(2,1)S(1)}, bf16[8464,128]{1,0:T(8,128)(2,1)S(1)}, u32[]{:S(2)}, u32[]{:S(2)}) collective-permute-start(bf16[8464,128]{1,0:T(8,128)(2,1)S(1)} %collect_feed.3.refs_0_), channel_id=1, source_target_pairs={{16,0},{17,1},{18,2},{19,3},{20,4},{21,5},{22,6},{23,7},{24,8},{25... | collective-permute-start | bytes 6500360 | tf_op jit(solution)/shard_map/ppermute | solution.py:1230
  458.9 18.3 %collective-permute-start.110 = (bf16[2176,128]{1,0:T(8,128)(2,1)S(1)}, bf16[2176,128]{1,0:T(8,128)(2,1)S(1)}, u32[]{:S(2)}, u32[]{:S(2)}) collective-permute-start(bf16[2176,128]{1,0:T(8,128)(2,1)S(1)} %add_convert_fusion), channel_id=1, source_target_pairs={{4,0},{8,12},{5,1},{9,13},{6,2},{10,14},{7,3},{11,15},{20,16},{24,... | collective-permute-start | bytes 1671176 | tf_op jit(solution)/shard_map/ppermute | solution.py:1178
  478.6 20.4 %collective-permute-start.111 = (bf16[128,1024]{1,0:T(8,128)(2,1)S(1)}, bf16[128,1024]{1,0:T(8,128)(2,1)S(1)}, u32[]{:S(2)}, u32[]{:S(2)}) collective-permute-start(bf16[128,1024]{1,0:T(8,128)(2,1)S(1)} %join_forward.7), channel_id=1, source_target_pairs={{0,0},{1,4},{2,8},{3,12},{4,1},{5,5},{6,9},{7,13},{8,2},{9,6},{10,... | collective-permute-start | bytes 786440 | tf_op jit(solution)/shard_map/ppermute | solution.py:1099
  480.5 21.3 %collective-permute-start.112 = (bf16[128,1024]{1,0:T(8,128)(2,1)S(1)}, bf16[128,1024]{1,0:T(8,128)(2,1)S(1)}, u32[]{:S(2)}, u32[]{:S(2)}) collective-permute-start(bf16[128,1024]{1,0:T(8,128)(2,1)S(1)} %get-tuple-element.796), channel_id=1, source_target_pairs={{0,0},{1,4},{2,8},{3,12},{4,1},{5,5},{6,9},{7,13},{8,2},{9,6},{10,... | collective-permute-start | bytes 786440 | tf_op jit(solution)/shard_map/ppermute | solution.py:1099
  (184 other events, 2481.8 us)

commit v3 on v2

--- a/solution.py
+++ b/solution.py
@@ -174,29 +174,28 @@
     return jnp.concatenate([values, jnp.zeros((LANES - values.shape[0], values.shape[1]), wide)], axis=0).T
 
 
-def block_scores(i, block, head, size, inner, projected, fixed, total, total_t, inflow_t, length, scale):
-    n = (i + 1) * block
-    rows = slice(i * block, n)
+def head_scores(head, size, inner, projected, fixed, total, total_t, inflow_t, length, scale):
+    rows = projected.shape[0]
     lanes = slice(head * size, (head + 1) * size)
-    q = projected[rows, lanes]
-    k = projected[0:n, inner + head * size : inner + (head + 1) * size]
-    v = projected[0:n, 2 * inner + head * size : 2 * inner + (head + 1) * size]
+    q = projected[:, lanes]
+    k = projected[:, inner + head * size : inner + (head + 1) * size]
+    v = projected[:, 2 * inner + head * size : 2 * inner + (head + 1) * size]
     fixed_k = fixed[:, lanes]
     fixed_v = fixed[:, inner + head * size : inner + (head + 1) * size]
     scores = mm_nt(q, k) * scale
     fixed_scores = mm_nt(q, fixed_k) * scale
-    at = i * block + lax.broadcasted_iota(jnp.int32, (block, 1), 0)
+    at = lax.broadcasted_iota(jnp.int32, (rows, 1), 0)
     begin = jnp.where(at >= length, length, 0)
-    column = lax.broadcasted_iota(jnp.int32, (block, n), 1)
+    column = lax.broadcasted_iota(jnp.int32, (rows, rows), 1)
     allowed = (column <= at) & (column >= begin)
     masked = jnp.where(allowed, scores, negative)
     top = jnp.maximum(jnp.max(masked, axis=1, keepdims=True), jnp.max(fixed_scores, axis=1, keepdims=True))
     weights, fixed_weights = jnp.exp(masked - top), jnp.exp(fixed_scores - top)
     mass = 1.0 / (jnp.sum(weights, axis=1, keepdims=True) + jnp.sum(fixed_weights, axis=1, keepdims=True))
     weights, fixed_weights = weights * mass, fixed_weights * mass
-    fall = jnp.exp(jnp.where(allowed, total[rows, head : head + 1] - total_t[head : head + 1, 0:n], negative))
+    fall = jnp.exp(jnp.where(allowed, total[:, head : head + 1] - total_t[head : head + 1, :], negative))
     reach = scores * fall
-    both = (weights + reach * inflow_t[head : head + 1, 0:n]).astype(half)
+    both = (weights + reach * inflow_t[head : head + 1, :]).astype(half)
     return q, k, v, fixed_k, fixed_v, weights, fixed_weights, fall, reach, both
 
 
@@ -205,7 +204,6 @@
     width = parts[0].shape[1]
     total_rows, inner = rows * count, heads * size
     scale = size ** (-0.5)
-    block = rows
 
     def body(place_ref, *refs):
         parts_in, refs = refs[:count], refs[count:]
@@ -231,12 +229,11 @@
             lanes = slice(kind * inner, (kind + 1) * inner)
             projected[:, lanes] = mm(normed[...], weight[:, lanes]).astype(half)
         for head in range(heads):
-            for i in range(count):
-                q, k, v, fixed_k, fixed_v, soft, fixed_soft, fall, reach, both = block_scores(
-                    i, block, head, size, inner, projected, fixed_ref, total, total_t, inflow_t, length, scale
-                )
-                mixed = mm(both, v) + mm(fixed_soft.astype(half), fixed_v)
-                combined[i * block : (i + 1) * block, head * size : (head + 1) * size] = mixed.astype(half)
+            q, k, v, fixed_k, fixed_v, soft, fixed_soft, fall, reach, both = head_scores(
+                head, size, inner, projected, fixed_ref, total, total_t, inflow_t, length, scale
+            )
+            mixed = mm(both, v) + mm(fixed_soft.astype(half), fixed_v)
+            combined[:, head * size : (head + 1) * size] = mixed.astype(half)
         finish(out_handles)
         whole[...] = mm(combined[...], out_weight[...])
         take_rows(whole, terms, place_ref)
@@ -266,7 +263,6 @@
     rows, width = parts[0].shape
     total_rows, inner = rows * count, heads * size
     scale = size ** (-0.5)
-    block = rows
 
     def body(place_ref, *refs):
         parts_in, refs = refs[:count], refs[count:]
@@ -275,7 +271,7 @@
         refs = refs[6:]
         terms, refs = refs[:count], refs[count:]
         branch, g_projected, g_logits_out, g_fixed, g_gain, refs = refs[0], refs[1], refs[2], refs[3], refs[4], refs[5:]
-        weight, out_weight, combined, g_k, g_v, pulled, pushed, whole, sems = refs
+        weight, out_weight, combined, pulled, pushed, whole, sems = refs
         out_handles = fetch(place_ref, layer, o_mine, o_other, out_weight, sems.at[pl.ds(1, 1)])
         handles = fetch(place_ref, layer, mine, other, weight, sems.at[pl.ds(0, 1)])
         put_rows(parts_in, branch, place_ref)
@@ -286,38 +282,32 @@
         inflow_t = jnp.sqrt(lose * (1.0 + keep))
         finish(out_handles)
         combined[...] = mm_nt(branch[...], out_weight[...]).astype(half)
-        g_k[...] = jnp.zeros_like(g_k)
-        g_v[...] = jnp.zeros_like(g_v)
         pulled[...] = jnp.zeros_like(pulled)
         pushed[...] = jnp.zeros_like(pushed)
-        g_fixed[...] = jnp.zeros_like(g_fixed)
         for head in range(heads):
-            lanes = slice(head * size, (head + 1) * size)
-            for i in range(count):
-                n = (i + 1) * block
-                here = slice(i * block, n)
-                q, k, v, fixed_k, fixed_v, weights, fixed_weights, fall, reach, both = block_scores(
-                    i, block, head, size, inner, projected, fixed_ref, total, total_t, inflow_t, length, scale
-                )
-                grad = combined[here, lanes]
-                g_both = mm_nt(grad, v)
-                g_few = mm_nt(grad, fixed_v)
-                delta = jnp.sum(weights * g_both, axis=1, keepdims=True) + jnp.sum(
-                    fixed_weights * g_few, axis=1, keepdims=True
-                )
-                inflow_row = inflow_t[head : head + 1, 0:n]
-                g_scores = (weights * (g_both - delta) + g_both * fall * inflow_row).astype(half)
-                g_few_scores = (fixed_weights * (g_few - delta)).astype(half)
-                g_projected[here, lanes] = ((mm(g_scores, k) + mm(g_few_scores, fixed_k)) * scale).astype(half)
-                g_k[0:n, lanes] += mm_tn(g_scores, q)
-                g_v[0:n, lanes] += mm_tn(both, grad)
-                g_fixed[:, lanes] += mm_tn(g_few_scores, q) * scale
-                g_fixed[:, inner + head * size : inner + (head + 1) * size] += mm_tn(fixed_weights.astype(half), grad)
-                pull = g_both * reach
-                pulled[head : head + 1, 0:n] += jnp.sum(pull, axis=0, keepdims=True)
-                pushed[here, head : head + 1] = jnp.sum(pull * inflow_row, axis=1, keepdims=True)
-        g_projected[:, inner : 2 * inner] = (g_k[...] * scale).astype(half)
-        g_projected[:, 2 * inner : 3 * inner] = g_v[...].astype(half)
+            lanes, key_lanes, value_lanes = (
+                slice(kind * inner + head * size, kind * inner + (head + 1) * size) for kind in range(3)
+            )
+            q, k, v, fixed_k, fixed_v, weights, fixed_weights, fall, reach, both = head_scores(
+                head, size, inner, projected, fixed_ref, total, total_t, inflow_t, length, scale
+            )
+            grad = combined[:, lanes]
+            g_both = mm_nt(grad, v)
+            g_few = mm_nt(grad, fixed_v)
+            delta = jnp.sum(weights * g_both, axis=1, keepdims=True) + jnp.sum(
+                fixed_weights * g_few, axis=1, keepdims=True
+            )
+            inflow_row = inflow_t[head : head + 1, :]
+            g_scores = (weights * (g_both - delta) + g_both * fall * inflow_row).astype(half)
+            g_few_scores = (fixed_weights * (g_few - delta)).astype(half)
+            g_projected[:, lanes] = ((mm(g_scores, k) + mm(g_few_scores, fixed_k)) * scale).astype(half)
+            g_projected[:, key_lanes] = (mm_tn(g_scores, q) * scale).astype(half)
+            g_projected[:, value_lanes] = mm_tn(both, grad).astype(half)
+            g_fixed[:, lanes] = mm_tn(g_few_scores, q) * scale
+            g_fixed[:, key_lanes] = mm_tn(fixed_weights.astype(half), grad)
+            pull = g_both * reach
+            pulled[head : head + 1, :] = jnp.sum(pull, axis=0, keepdims=True)
+            pushed[:, head : head + 1] = jnp.sum(pull * inflow_row, axis=1, keepdims=True)
         g_inflow = pulled[...]
         g_total = pushed[...].T[0:16] - inflow_t * g_inflow
         after = lax.broadcasted_iota(jnp.int32, (total_rows, total_rows), 0) >= lax.broadcasted_iota(
@@ -348,8 +338,6 @@
         pltpu.VMEM((width, 3 * inner), half),
         pltpu.VMEM((inner, width), half),
         pltpu.VMEM((total_rows, inner), half),
-        pltpu.VMEM((total_rows, inner), wide),
-        pltpu.VMEM((total_rows, inner), wide),
         pltpu.VMEM((16, total_rows), wide),
         pltpu.VMEM((total_rows, LANES), wide),
         pltpu.VMEM((total_rows, width), wide),
@@ -365,6 +353,9 @@
 
 def gates_of(tile_pair):
     rows, columns = tile_pair.shape
+    if columns > 2 * LANES:
+        found = [gates_of(tile_pair[:, at : at + size]) for at, size in tile_ranges(columns)]
+        return tuple(jnp.concatenate([pair[k] for pair in found], axis=1) for k in range(2))
     if columns == LANES:
         return tile_pair[:, :PAIR], pltpu.roll(tile_pair, PAIR, 1)[:, :PAIR]
     first, second = tile_pair[:, :LANES], tile_pair[:, LANES:]
@@ -376,6 +367,9 @@
 
 def tiles_of(gate, up):
     rows, columns = gate.shape
+    if columns > LANES:
+        steps = [(at, min(LANES, columns - at)) for at in range(0, columns, LANES)]
+        return jnp.concatenate([tiles_of(gate[:, at : at + size], up[:, at : at + size]) for at, size in steps], axis=1)
     if columns == PAIR:
         return jnp.concatenate([gate, up], axis=1)
     low = lax.broadcasted_iota(jnp.int32, (rows, LANES), 1) < PAIR
@@ -384,8 +378,8 @@
     return jnp.concatenate([first, second], axis=1)
 
 
-def tile_ranges(columns):
-    return [(at, min(2 * LANES, columns - at)) for at in range(0, columns, 2 * LANES)]
+def tile_ranges(columns, tiles=2):
+    return [(at, min(tiles * LANES, columns - at)) for at in range(0, columns, tiles * LANES)]
 
 
 def feed_forward(layer, place, parts, weights):
@@ -430,7 +424,7 @@
     )
 
 
-def feed_backward(layer, place, parts, normed_two, gain, weights):
+def feed_backward(layer, place, parts, normed_parts, gain, weights, forward):
     count = len(parts)
     rows, width = parts[0].shape
     total_rows = rows * count
@@ -439,23 +433,35 @@
 
     def body(place_ref, *refs):
         parts_in, refs = refs[:count], refs[count:]
-        normed, gain_ref, refs = refs[0], refs[1], refs[2:]
-        (mine, other, d_mine, d_other), refs = refs[:4], refs[4:]
+        normed_in, refs = refs[: len(normed_parts)], refs[len(normed_parts) :]
+        gain_ref, (mine, other, d_mine, d_other), refs = refs[0], refs[1:5], refs[5:]
         terms, refs = refs[:count], refs[count:]
         g_out, g_gates, active, g_gain, refs = refs[0], refs[1], refs[2], refs[3], refs[4:]
-        weight, down, whole, sems = refs
+        if forward:
+            ahead, normed, refs = refs[:count], refs[count], refs[count + 1 :]
+        else:
+            normed = normed_in[0]
+        weight, down, held, whole, sems = refs
         handles = fetch(place_ref, layer, mine, other, weight, sems.at[pl.ds(0, 1)])
         down_handles = fetch(place_ref, layer, d_mine, d_other, down, sems.at[pl.ds(1, 1)])
         put_rows(parts_in, g_out, place_ref)
+        if forward:
+            put_rows(normed_in, normed, place_ref)
+        if padded != hidden:
+            down[hidden:, :] = jnp.zeros((padded - hidden, width), half)
+            held[:, padded - LANES :] = jnp.zeros((total_rows, LANES), half)
         finish(handles)
         finish(down_handles)
-        for at, size in tile_ranges(columns):
+        for at, size in tile_ranges(columns, 4):
             inside = slice(at // 2, (at + size) // 2)
             gate, up = gates_of(mm(normed[...], weight[:, at : at + size]))
             g_active = mm_nt(g_out[...], down[inside, :])
             open_ = sig(gate)
             lit = gate * open_
-            active[:, inside] = (lit * up).astype(half)
+            product = (lit * up).astype(half)
+            active[:, inside] = product
+            if forward:
+                held[:, inside] = product
             g_up = g_active * lit
             g_gate = g_active * up * (open_ * (1.0 + gate - lit))
             g_gates[:, at : at + size] = tiles_of(g_gate, g_up).astype(half)
@@ -463,24 +469,31 @@
         pulls = jnp.sum(whole[...] * normed[...].astype(wide), axis=0, keepdims=True) / gain_ref[...]
         g_gain[...] = jnp.broadcast_to(pulls, g_gain.shape)
         take_rows(whole, terms, place_ref)
-
-    outs = [shape((rows, width), wide if r == 0 else half) for r in range(count)] + [
+        if forward:
+            whole[...] = mm(held[...], down[...])
+            take_rows(whole, ahead, place_ref)
+
+    term_shapes = [shape((rows, width), wide if r == 0 else half) for r in range(count)]
+    outs = term_shapes + [
         shape((total_rows, width)),
         shape((total_rows, columns)),
         shape((total_rows, hidden)),
         shape((8, width), wide),
     ]
+    if forward:
+        outs = outs + term_shapes + [shape((total_rows, width))]
     scratch = [
         pltpu.VMEM((width, columns), half),
-        pltpu.VMEM((hidden, width), half),
+        pltpu.VMEM((padded, width), half),
+        pltpu.VMEM((total_rows, padded), half),
         pltpu.VMEM((total_rows, width), wide),
         pltpu.SemaphoreType.DMA((2,)),
     ]
-    specs = [smem] + [vmem] * (count + 2) + [anywhere] * 4
+    specs = [smem] + [vmem] * (count + len(normed_parts) + 1) + [anywhere] * 4
     flops = 2 * total_rows * width * (2 * columns + hidden)
     moved = 2 * (width * (columns + hidden) + total_rows * (6 * width + columns + hidden))
     return call(body, outs, specs, scratch, flops, moved, "feed_backward")(
-        place, *parts, normed_two, gain, *weights
+        place, *parts, *normed_parts, gain, *weights
     )
 
 
@@ -1054,8 +1067,13 @@
 
 def gather_parts(block, axis):
     count = lax.axis_size(axis)
-    far = {r: exchange(block, axis, r) for r in reversed(range(1, count))}
-    return [block] + [far[r] for r in range(1, count)]
+    far = tie(*(exchange(block, axis, r) for r in reversed(range(1, count))))
+    return [block, *reversed(far)]
+
+
+def trade_terms(blocks, axis):
+    found = trade_parts(blocks, axis)
+    return found
 
 
 def trade_parts(blocks, axis):
@@ -1137,11 +1155,13 @@
         return terms, (seen, projected, logits, combined)
 
     def mix_second_half(layer, terms, x):
-        middle, normed_two = join_forward(False, trade_parts(terms, "fsdp"), x, gains_two[layer])
+        middle, normed_two = join_forward(False, trade_terms(terms, "fsdp"), x, gains_two[layer])
         return middle, gather_parts(normed_two, "fsdp")
 
     def feed_step(layer, parts, saved):
-        *terms, g_rows, g_gates, active, g_gain = feed_backward(layer, seat, parts, saved[6], gains_two[layer], feed_weights)
+        *terms, g_rows, g_gates, active, g_gain = feed_backward(
+            layer, seat, parts, [saved[6]], gains_two[layer], feed_weights, False
+        )
         return terms, (saved[6], g_gates, active, g_rows, g_gain)
 
     def mix_step(layer, parts, saved):
@@ -1210,21 +1230,22 @@
 
     terms, kept = mix_first_half(0, x_parts)
     terms, gu_parts[1], g_in = tie(terms, gu_parts[1], g_in)
-    terms, gu_parts = tie(trade_parts(terms, "fsdp"), gu_parts)
+    terms, gu_parts = tie(trade_terms(terms, "fsdp"), gu_parts)
     gu_mine = assemble(spot, gu_parts)
     feed_weights = (gu_mine, swap(gu_mine), down_mine, down_other)
     middle, normed_two = join_forward(False, terms, x_in, gains_two[0])
     parts = gather_parts(normed_two, "fsdp")
     *terms, seen_two = feed_forward(0, seat, parts, feed_weights)
-    terms = trade_parts(terms, "fsdp")
+    terms = trade_terms(terms, "fsdp")
     saved_first = (x_in, *kept, middle, seen_two)
     between = join_forward(True, terms, middle, None)[0]
     terms, kept = mix_first_half(1, gather_parts(between, "fsdp"))
     terms, g_three, g_two, g_one = tie(terms, *(exchange(g_in, "fsdp", r) for r in (3, 2, 1)))
     middle, parts = mix_second_half(1, terms, between)
-    *terms_out, seen_two = feed_forward(1, seat, parts, feed_weights)
+    made = feed_backward(1, seat, [g_in, g_one, g_two, g_three], parts, gains_two[1], feed_weights, True)
+    terms, (g_rows, g_gates, active, g_gain), terms_out, seen_two = made[:4], made[4:8], made[8:12], made[12]
+    feed = (seen_two, g_gates, active, g_rows, g_gain)
     saved_second = (between, *kept, middle, seen_two)
-    terms, feed = feed_step(1, [g_in, g_one, g_two, g_three], saved_second)
 
     def to_owner(layer, chunks):
         return [lax.ppermute(chunk, "section", [(1 - layer, layer)]) for chunk in chunks]
@@ -1249,22 +1270,22 @@
         return chunks
 
     sent, *own = grad_feed(4, count, place, *feed)
-    terms, sent = tie(trade_parts(terms, "fsdp"), sent)
+    terms, sent = tie(trade_terms(terms, "fsdp"), sent)
     g_middle, g_branch = join_backward(terms, saved_second[5], gains_two[1], g_in)
     parts = gather_parts(g_branch, "fsdp")
     parts, received = tie(parts, swap(sent))
     (parts,) = step(parts, more=lambda _: summed(own, received))
     terms, mix = mix_step(1, parts, saved_second)
-    terms, terms_out = step(terms, trade_parts(terms_out, "fsdp"))
+    terms, terms_out = step(terms, trade_terms(terms_out, "fsdp"))
     out = join_forward(True, terms_out, saved_second[5], None)[0]
     sent, *own = grad_mix(2, pad, count, place, *mix)
-    terms, sent = step(trade_parts(terms, "fsdp"), sent)
+    terms, sent = step(trade_terms(terms, "fsdp"), sent)
     g_middle, g_branch = join_backward(terms, between, gains_one[1], g_middle)
     parts, sent = step(gather_parts(g_branch, "fsdp"), sent)
     terms, feed = feed_step(0, parts, saved_first)
     terms, _ = step(terms, swap(sent), more=lambda _, received: summed(own, received))
     sent, *own = grad_feed(4, count, place, *feed)
-    terms, sent = step(trade_parts(terms, "fsdp"), sent)
+    terms, sent = step(trade_terms(terms, "fsdp"), sent)
     received = swap(sent)
     g_middle, g_branch = join_backward(terms, saved_first[5], gains_two[0], g_branch)
     g_branch, received = tie(g_branch, received)
@@ -1274,7 +1295,7 @@
     terms, f1 = step(terms, f1)
     feed_second = collect_feed(columns, place, [f1])
     sent, *own = grad_mix(1, pad, count, place, *mix)
-    (terms,) = step(trade_parts(terms, "fsdp"))
+    (terms,) = step(trade_terms(terms, "fsdp"))
     g_input = join_backward(terms, x_in, gains_one[0], g_middle)[1]
     received = swap(sent)
     g_input, received, feed_second = step(g_input, received, feed_second)
@@ -1298,7 +1319,7 @@
     )
     m0_last = [jnp.where(inside, *pair) for pair in taken(1)]
     m0_last_other = to_owner(0, m0_last)
-    out, g_turned = turn_plane(out), turn_plane(g_input)
+    turned_both = turn_plane(jnp.stack([out, g_input]))
     grad_gate_up, grad_down, grad_norm_two = unpack_feed(
         count,
         columns,
@@ -1316,10 +1337,10 @@
         ((m0_first + m0_last, m0_first_other + m0_last_other), (mix_second, mix_second_other)),
         place,
     )
-    out, g_turned, grad_bias = tie(out, g_turned, grad_bias)
+    turned_both, grad_bias = tie(turned_both, grad_bias)
     return (
-        out[None, None],
-        g_turned[None, None],
+        turned_both[0][None, None],
+        turned_both[1][None, None],
         grad_norm_one,
         grad_qkv[None],
         grad_decay[None],

time: 513 us -> 503 us (0.981)
  Pallas kernels: 99.5 us -> 87.1 us
  starting transfers between devices: 155 us -> 146 us
  waiting for transfers between devices: 209 us -> 218 us
    ppermute x78, waiting for transfers between devices: 162 us -> 171 us  [exchange(): return lax.ppermute(value, axis, [(i, i ^ distance) for i in range(count)])]
    ppermute x4 -> x3, starting transfers between devices: 14.1 us -> 8.33 us  [turn_plane(): return lax.ppermute(value, ('section', 'ctx', 'fsdp'), pairs)]
    ppermute x14, waiting for transfers between devices: 35.4 us -> 30 us  [go(): flight[0] = lax.ppermute(sent, 'ctx', route)]
    ppermute x4 -> x3, waiting for transfers between devices: 12.3 us -> 16.9 us  [turn_plane(): return lax.ppermute(value, ('section', 'ctx', 'fsdp'), pairs)]
    unnamed x192 -> x180, local copies, waits for them, and re-layouts: 26.7 us -> 30.2 us
  transfers between devices with their start and end apart: 114 -> 113, of which waited for: 54 -> 53; matrix products, arithmetic and copies ran while one was open for 1% -> 1% of each run, Pallas kernels for 15% -> 14%
where the time goes in v3:
time: 503 us; the launch traced here: 495 us
  waiting for transfers between devices  218 us (43%)
  starting transfers between devices  146 us (29%)
  Pallas kernels  87.1 us (17%)
  local copies, waits for them, and re-layouts  34.1 us (7%)
  other arithmetic  7.51 us (1%)
    ppermute x78, waiting for transfers between devices, exchange(): return lax.ppermute(value, axis, [(i, i ^ distance) for i in range(count)])  171 us
    ppermute x78, starting transfers between devices, exchange(): return lax.ppermute(value, axis, [(i, i ^ distance) for i in range(count)])  85.1 us
    ppermute x14, starting transfers between devices, go(): flight[0] = lax.ppermute(sent, 'ctx', route)  34.6 us
    unnamed x180, local copies, waits for them, and re-layouts  30.2 us
    ppermute x14, waiting for transfers between devices, go(): flight[0] = lax.ppermute(sent, 'ctx', route)  30 us
    ppermute x3, waiting for transfers between devices, turn_plane(): return lax.ppermute(value, ('section', 'ctx', 'fsdp'), pairs)  16.9 us
    pallas_call x2, Pallas kernels, feed_backward(): call(body, outs, specs, scratch, flops, moved, 'feed_backward')  14.8 us
    pallas_call x2, Pallas kernels, mix_backward(): call(body, outs, specs, scratch, flops, moved, 'mix_backward')  14.4 us
  transfers between devices with their start and end apart: 113, of which 53 were waited for; matrix products, arithmetic and copies ran while one was open for 1% of the time, Pallas kernels for 14%

profile of v3, /device:TPU:2, one launch (start us, length us, event | category | flops | bytes accessed | tf_op | source)
XLA Modules:
  0.0 494.8 jit_solution(9553906361219291269)
XLA Ops:
  32.8 15.8 %collective-permute-done.2.refs_3_ = bf16[160,1024]{1,0:T(8,128)(2,1)S(1)} collective-permute-done((bf16[160,1024]{1,0:T(8,128)(2,1)S(1)}, bf16[160,1024]{1,0:T(8,128)(2,1)S(1)}, u32[]{:S(2)}, u32[]{:S(2)}) %collective-permute-start.2) | collective-permute-done | bytes 327712 | tf_op jit(solution)/shard_map/ppermute | solution.py:1065
  67.2 6.7 %mix_forward.2 = (f32[128,1024]{1,0:T(8,128)S(1)}, bf16[128,1024]{1,0:T(8,128)(2,1)S(1)}, bf16[128,1024]{1,0:T(8,128)(2,1)S(1)}, bf16[128,1024]{1,0:T(8,128)(2,1...) custom-call(s32[3]{0:T(128)S(1)} %pad_add_fusion.2.place_ref, ...), custom_call_target="tpu_custom_call" | custom-call | flops 1342177280 | bytes 4718592 | tf_op jit(solution)/shard_map/mix_forward/pallas_call | solution.py:256
  80.5 8.7 %collective-permute-done.16.refs_2_ = bf16[256,1408]{1,0:T(8,128)(2,1)} collective-permute-done((bf16[256,1408]{1,0:T(8,128)(2,1)}, bf16[256,1408]{1,0:T(8,128)(2,1)}, u32[]{:S(2)}, u32[]{:S(2)}) %collective-permute-start.16) | collective-permute-done | bytes 720928 | tf_op jit(solution)/shard_map/ppermute | solution.py:1065
  89.2 6.8 %collective-permute-done.13.refs_1_ = bf16[128,1024]{1,0:T(8,128)(2,1)S(1)} collective-permute-done((bf16[128,1024]{1,0:T(8,128)(2,1)S(1)}, bf16[128,1024]{1,0:T(8,128)(2,1)S(1)}, u32[]{:S(2)}, u32[]{:S(2)}) %collective-permute-start.13) | collective-permute-done | bytes 262176 | tf_op jit(solution)/shard_map/ppermute | solution.py:1065
  106.5 5.6 %collective-permute-done.20.refs_1_ = bf16[128,1024]{1,0:T(8,128)(2,1)S(1)} collective-permute-done((bf16[128,1024]{1,0:T(8,128)(2,1)S(1)}, bf16[128,1024]{1,0:T(8,128)(2,1)S(1)}, u32[]{:S(2)}, u32[]{:S(2)}) %collective-permute-start.20) | collective-permute-done | bytes 262176 | tf_op jit(solution)/shard_map/ppermute | solution.py:1065
  112.1 6.9 %collective-permute-done.19.refs_2_ = bf16[128,1024]{1,0:T(8,128)(2,1)S(1)} collective-permute-done((bf16[128,1024]{1,0:T(8,128)(2,1)S(1)}, bf16[128,1024]{1,0:T(8,128)(2,1)S(1)}, u32[]{:S(2)}, u32[]{:S(2)}) %collective-permute-start.19) | collective-permute-done | bytes 262176 | tf_op jit(solution)/shard_map/ppermute | solution.py:1065
  127.1 5.8 %collective-permute-done.22.refs_1_ = bf16[128,1024]{1,0:T(8,128)(2,1)S(1)} collective-permute-done((bf16[128,1024]{1,0:T(8,128)(2,1)S(1)}, bf16[128,1024]{1,0:T(8,128)(2,1)S(1)}, u32[]{:S(2)}, u32[]{:S(2)}) %collective-permute-start.22) | collective-permute-done | bytes 262176 | tf_op jit(solution)/shard_map/ppermute | solution.py:1065
  148.0 5.7 %collective-permute-done.26.refs_2_ = bf16[128,1024]{1,0:T(8,128)(2,1)S(1)} collective-permute-done((bf16[128,1024]{1,0:T(8,128)(2,1)S(1)}, bf16[128,1024]{1,0:T(8,128)(2,1)S(1)}, u32[]{:S(2)}, u32[]{:S(2)}) %collective-permute-start.26) | collective-permute-done | bytes 262176 | tf_op jit(solution)/shard_map/ppermute | solution.py:1065
  153.7 6.2 %mix_forward.3 = (f32[128,1024]{1,0:T(8,128)S(1)}, bf16[128,1024]{1,0:T(8,128)(2,1)S(1)}, bf16[128,1024]{1,0:T(8,128)(2,1)S(1)}, bf16[128,1024]{1,0:T(8,128)(2,1...) custom-call(s32[3]{0:T(128)S(1)} %pad_add_fusion.2.place_ref, ...), custom_call_target="tpu_custom_call" | custom-call | flops 1342177280 | bytes 4718592 | tf_op jit(solution)/shard_map/mix_forward/pallas_call | solution.py:256
  185.3 8.8 %feed_backward.2 = (f32[128,1024]{1,0:T(8,128)S(1)}, bf16[128,1024]{1,0:T(8,128)(2,1)}, bf16[128,1024]{1,0:T(8,128)(2,1)}, bf16[128,1024]{1,0:T(8,128)(2,1)}, bf...) custom-call(s32[3]{0:T(128)S(1)} %pad_add_fusion.2.place_ref, ...), custom_call_target="tpu_custom_call" | custom-call | flops 3690987520 | bytes 12779520 | tf_op jit(solution)/shard_map/feed_backward/pallas_call | solution.py:495
  221.6 5.6 %collective-permute-done.42.refs_1_ = bf16[128,1024]{1,0:T(8,128)(2,1)S(1)} collective-permute-done((bf16[128,1024]{1,0:T(8,128)(2,1)S(1)}, bf16[128,1024]{1,0:T(8,128)(2,1)S(1)}, u32[]{:S(2)}, u32[]{:S(2)}) %collective-permute-start.42) | collective-permute-done | bytes 262176 | tf_op jit(solution)/shard_map/ppermute | solution.py:1065
  227.2 5.9 %collective-permute-done.41.refs_2_ = bf16[128,1024]{1,0:T(8,128)(2,1)S(1)} collective-permute-done((bf16[128,1024]{1,0:T(8,128)(2,1)S(1)}, bf16[128,1024]{1,0:T(8,128)(2,1)S(1)}, u32[]{:S(2)}, u32[]{:S(2)}) %collective-permute-start.41) | collective-permute-done | bytes 262176 | tf_op jit(solution)/shard_map/ppermute | solution.py:1065
  240.6 7.1 %mix_backward.2 = (f32[128,1024]{1,0:T(8,128)S(1)}, bf16[128,1024]{1,0:T(8,128)(2,1)S(1)}, bf16[128,1024]{1,0:T(8,128)(2,1)S(1)}, bf16[128,1024]{1,0:T(8,128)(2,...) custom-call(s32[3]{0:T(128)S(1)} %copy-done.71, ...), custom_call_target="tpu_custom_call" | custom-call | flops 1744830464 | bytes 8912896 | tf_op jit(solution)/shard_map/mix_backward/pallas_call | solution.py:349
  274.3 5.1 %collective-permute-done.55.refs_1_ = bf16[128,1024]{1,0:T(8,128)(2,1)S(1)} collective-permute-done((bf16[128,1024]{1,0:T(8,128)(2,1)S(1)}, bf16[128,1024]{1,0:T(8,128)(2,1)S(1)}, u32[]{:S(2)}, u32[]{:S(2)}) %collective-permute-start.55) | collective-permute-done | bytes 262176 | tf_op jit(solution)/shard_map/ppermute | solution.py:1065
  286.4 6.0 %feed_backward.3 = (f32[128,1024]{1,0:T(8,128)S(1)}, bf16[128,1024]{1,0:T(8,128)(2,1)S(1)}, bf16[128,1024]{1,0:T(8,128)(2,1)S(1)}, bf16[128,1024]{1,0:T(8,128)(2...) custom-call(s32[3]{0:T(128)S(1)} %copy-done.71, ...), custom_call_target="tpu_custom_call" | custom-call | flops 3690987520 | bytes 12779520 | tf_op jit(solution)/shard_map/feed_backward/pallas_call | solution.py:495
  292.4 6.5 %collective-permute-done.59.refs_3_ = bf16[2176,128]{1,0:T(8,128)(2,1)S(1)} collective-permute-done((bf16[2176,128]{1,0:T(8,128)(2,1)S(1)}, bf16[2176,128]{1,0:T(8,128)(2,1)S(1)}, u32[]{:S(2)}, u32[]{:S(2)}) %collective-permute-start.59) | collective-permute-done | bytes 557088 | tf_op jit(solution)/shard_map/ppermute | solution.py:1198
  326.4 5.7 %collective-permute-done.69.refs_1_ = bf16[128,1024]{1,0:T(8,128)(2,1)S(1)} collective-permute-done((bf16[128,1024]{1,0:T(8,128)(2,1)S(1)}, bf16[128,1024]{1,0:T(8,128)(2,1)S(1)}, u32[]{:S(2)}, u32[]{:S(2)}) %collective-permute-start.69) | collective-permute-done | bytes 262176 | tf_op jit(solution)/shard_map/ppermute | solution.py:1065
  332.1 5.1 %collective-permute-done.68.refs_2_ = bf16[128,1024]{1,0:T(8,128)(2,1)S(1)} collective-permute-done((bf16[128,1024]{1,0:T(8,128)(2,1)S(1)}, bf16[128,1024]{1,0:T(8,128)(2,1)S(1)}, u32[]{:S(2)}, u32[]{:S(2)}) %collective-permute-start.68) | collective-permute-done | bytes 262176 | tf_op jit(solution)/shard_map/ppermute | solution.py:1065
  345.0 7.3 %mix_backward.3 = (f32[128,1024]{1,0:T(8,128)S(1)}, bf16[128,1024]{1,0:T(8,128)(2,1)S(1)}, bf16[128,1024]{1,0:T(8,128)(2,1)S(1)}, bf16[128,1024]{1,0:T(8,128)(2,...) custom-call(s32[3]{0:T(128)S(1)} %copy-done.71, ...), custom_call_target="tpu_custom_call" | custom-call | flops 1744830464 | bytes 8912896 | tf_op jit(solution)/shard_map/mix_backward/pallas_call | solution.py:349
  353.2 7.1 %collective-permute-done.73.refs_2_ = bf16[1472,128]{1,0:T(8,128)(2,1)S(1)} collective-permute-done((bf16[1472,128]{1,0:T(8,128)(2,1)S(1)}, bf16[1472,128]{1,0:T(8,128)(2,1)S(1)}, u32[]{:S(2)}, u32[]{:S(2)}) %collective-permute-start.73) | collective-permute-done | bytes 376864 | tf_op jit(solution)/shard_map/ppermute | solution.py:1065
  380.9 7.5 %collective-permute-done.83.refs_1_ = bf16[2176,128]{1,0:T(8,128)(2,1)S(1)} collective-permute-done((bf16[2176,128]{1,0:T(8,128)(2,1)S(1)}, bf16[2176,128]{1,0:T(8,128)(2,1)S(1)}, u32[]{:S(2)}, u32[]{:S(2)}) %collective-permute-start.83) | collective-permute-done | bytes 557088 | tf_op jit(solution)/shard_map/ppermute | solution.py:1198
  452.5 16.0 %collective-permute-done.110 = bf16[2176,128]{1,0:T(8,128)(2,1)S(1)} collective-permute-done((bf16[2176,128]{1,0:T(8,128)(2,1)S(1)}, bf16[2176,128]{1,0:T(8,128)(2,1)S(1)}, u32[]{:S(2)}, u32[]{:S(2)}) %collective-permute-start.110) | collective-permute-done | bytes 557088 | tf_op jit(solution)/shard_map/ppermute | solution.py:1198
  471.9 5.1 %unpack_feed.1 = (f32[256,5632]{1,0:T(8,128)}, f32[704,1024]{1,0:T(8,128)}, f32[1,256]{1,0:T(1,128)}) custom-call(s32[4]{0:T(128)S(1)} %pad_add_fusion.1.place_ref, bf16[8464,128]{1,0:T(8,128)(2,1)S(1)} %collect_feed.3.refs_0_, bf16[8464,128]{1,0:T(8,128)(2,1)S(1)} %collective-permute-done.105.refs_1_, bf16[8464,128]{1,0:T(8,128)(2,1)S(1)} %collect_feed.2.refs_2_, ...), custom_call_target="tpu_custom_call" | custom-call | bytes 12985344 | tf_op jit(solution)/shard_map/unpack_feed/pallas_call | solution.py:1000
  480.2 13.0 %collective-permute-done.111 = bf16[2,128,1024]{2,1,0:T(8,128)(2,1)S(1)} collective-permute-done((bf16[2,128,1024]{2,1,0:T(8,128)(2,1)S(1)}, bf16[2,128,1024]{2,1,0:T(8,128)(2,1)S(1)}, u32[]{:S(2)}, u32[]{:S(2)}) %collective-permute-start.111) | collective-permute-done | bytes 524320 | tf_op jit(solution)/shard_map/ppermute | solution.py:1117
  (454 shorter events, 312.6 us)
Async XLA Ops:
  19.1 29.5 %collective-permute-start.6 = (bf16[256,768]{1,0:T(8,128)(2,1)S(1)}, bf16[256,768]{1,0:T(8,128)(2,1)S(1)}, u32[]{:S(2)}, u32[]{:S(2)}) collective-permute-start(bf16[256,768]{1,0:T(8,128)(2,1)S(1)} %get-tuple-element.442), channel_id=1, source_target_pairs={{0,1},{1,0},{2,3},{3,2},{4,5},{5,4},{6,7},{7,6},{8,9},{9,8},{10,11... | collective-permute-start | bytes 1179656 | tf_op jit(solution)/shard_map/ppermute | solution.py:1065
  21.0 27.8 %collective-permute-start.7 = (bf16[256,768]{1,0:T(8,128)(2,1)S(1)}, bf16[256,768]{1,0:T(8,128)(2,1)S(1)}, u32[]{:S(2)}, u32[]{:S(2)}) collective-permute-start(bf16[256,768]{1,0:T(8,128)(2,1)S(1)} %get-tuple-element.443), channel_id=1, source_target_pairs={{0,2},{1,3},{2,0},{3,1},{4,6},{5,7},{6,4},{7,5},{8,10},{9,11},{10,... | collective-permute-start | bytes 1179656 | tf_op jit(solution)/shard_map/ppermute | solution.py:1065
  23.0 25.8 %collective-permute-start.8 = (bf16[256,768]{1,0:T(8,128)(2,1)S(1)}, bf16[256,768]{1,0:T(8,128)(2,1)S(1)}, u32[]{:S(2)}, u32[]{:S(2)}) collective-permute-start(bf16[256,768]{1,0:T(8,128)(2,1)S(1)} %get-tuple-element.444), channel_id=1, source_target_pairs={{0,3},{1,2},{2,1},{3,0},{4,7},{5,6},{6,5},{7,4},{8,11},{9,10},{10,... | collective-permute-start | bytes 1179656 | tf_op jit(solution)/shard_map/ppermute | solution.py:1065
  25.7 22.9 %collective-permute-start.2 = (bf16[160,1024]{1,0:T(8,128)(2,1)S(1)}, bf16[160,1024]{1,0:T(8,128)(2,1)S(1)}, u32[]{:S(2)}, u32[]{:S(2)}) collective-permute-start(bf16[160,1024]{1,0:T(8,128)(2,1)S(1)} %beside.1.refs_0_), channel_id=1, source_target_pairs={{0,3},{1,2},{2,1},{3,0},{4,7},{5,6},{6,5},{7,4},{8,11},{9,10},{10,... | collective-permute-start | bytes 983048 | tf_op jit(solution)/shard_map/ppermute | solution.py:1065
  28.1 28.0 %collective-permute-start.5 = (bf16[704,1024]{1,0:T(8,128)(2,1)}, bf16[704,1024]{1,0:T(8,128)(2,1)S(1)}, u32[]{:S(2)}, u32[]{:S(2)}) collective-permute-start(bf16[704,1024]{1,0:T(8,128)(2,1)} %bitcast.36), channel_id=1, source_target_pairs={{0,16},{16,0},{1,17},{17,1},{2,18},{18,2},{3,19},{19,3},{4,20},{20... | collective-permute-start | bytes 4325384 | tf_op jit(solution)/shard_map/ppermute | solution.py:1065
  50.1 24.9 %collective-permute-start.11 = (bf16[256,1408]{1,0:T(8,128)(2,1)}, bf16[256,1408]{1,0:T(8,128)(2,1)}, u32[]{:S(2)}, u32[]{:S(2)}) collective-permute-start(bf16[256,1408]{1,0:T(8,128)(2,1)} %get-tuple-element.461), channel_id=1, source_target_pairs={{0,1},{1,0},{2,3},{3,2},{4,5},{5,4},{6,7},{7,6},{8,9},{9,8},{10,11... | collective-permute-start | bytes 2162696 | tf_op jit(solution)/shard_map/ppermute | solution.py:1065
  51.6 37.6 %collective-permute-start.16 = (bf16[256,1408]{1,0:T(8,128)(2,1)}, bf16[256,1408]{1,0:T(8,128)(2,1)}, u32[]{:S(2)}, u32[]{:S(2)}) collective-permute-start(bf16[256,1408]{1,0:T(8,128)(2,1)} %get-tuple-element.470), channel_id=1, source_target_pairs={{0,2},{1,3},{2,0},{3,1},{4,6},{5,7},{6,4},{7,5},{8,10},{9,11},{10,... | collective-permute-start | bytes 2162696 | tf_op jit(solution)/shard_map/ppermute | solution.py:1065
  54.5 34.6 %collective-permute-start.17 = (bf16[256,1408]{1,0:T(8,128)(2,1)}, bf16[256,1408]{1,0:T(8,128)(2,1)}, u32[]{:S(2)}, u32[]{:S(2)}) collective-permute-start(bf16[256,1408]{1,0:T(8,128)(2,1)} %get-tuple-element.471), channel_id=1, source_target_pairs={{0,3},{1,2},{2,1},{3,0},{4,7},{5,6},{6,5},{7,4},{8,11},{9,10},{10,... | collective-permute-start | bytes 2162696 | tf_op jit(solution)/shard_map/ppermute | solution.py:1065
  57.2 16.9 %collective-permute-start.12 = (bf16[128,1024]{1,0:T(8,128)(2,1)}, bf16[128,1024]{1,0:T(8,128)(2,1)}, u32[]{:S(2)}, u32[]{:S(2)}) collective-permute-start(bf16[128,1024]{1,0:T(8,128)(2,1)} %dynamic-slice_bitcast_fusion), channel_id=1, source_target_pairs={{0,0},{1,4},{2,8},{3,12},{4,1},{5,5},{6,9},{7,13},{8,2},{9,6},{10,... | collective-permute-start | bytes 786440 | tf_op jit(solution)/shard_map/ppermute | solution.py:1117
  75.0 21.0 %collective-permute-start.13 = (bf16[128,1024]{1,0:T(8,128)(2,1)S(1)}, bf16[128,1024]{1,0:T(8,128)(2,1)S(1)}, u32[]{:S(2)}, u32[]{:S(2)}) collective-permute-start(bf16[128,1024]{1,0:T(8,128)(2,1)S(1)} %get-tuple-element.465), channel_id=1, source_target_pairs={{0,1},{1,0},{2,3},{3,2},{4,5},{5,4},{6,7},{7,6},{8,9},{9,8},{10,11... | collective-permute-start | bytes 786440 | tf_op jit(solution)/shard_map/ppermute | solution.py:1065
  76.5 23.0 %collective-permute-start.14 = (bf16[128,1024]{1,0:T(8,128)(2,1)S(1)}, bf16[128,1024]{1,0:T(8,128)(2,1)S(1)}, u32[]{:S(2)}, u32[]{:S(2)}) collective-permute-start(bf16[128,1024]{1,0:T(8,128)(2,1)S(1)} %get-tuple-element.466), channel_id=1, source_target_pairs={{0,2},{1,3},{2,0},{3,1},{4,6},{5,7},{6,4},{7,5},{8,10},{9,11},{10,... | collective-permute-start | bytes 786440 | tf_op jit(solution)/shard_map/ppermute | solution.py:1065
  79.1 20.3 %collective-permute-start.15 = (bf16[128,1024]{1,0:T(8,128)(2,1)S(1)}, bf16[128,1024]{1,0:T(8,128)(2,1)S(1)}, u32[]{:S(2)}, u32[]{:S(2)}) collective-permute-start(bf16[128,1024]{1,0:T(8,128)(2,1)S(1)} %get-tuple-element.467), channel_id=1, source_target_pairs={{0,3},{1,2},{2,1},{3,0},{4,7},{5,6},{6,5},{7,4},{8,11},{9,10},{10,... | collective-permute-start | bytes 786440 | tf_op jit(solution)/shard_map/ppermute | solution.py:1065
  101.4 17.6 %collective-permute-start.21 = (bf16[1024,1408]{1,0:T(8,128)(2,1)S(1)}, bf16[1024,1408]{1,0:T(8,128)(2,1)S(1)}, u32[]{:S(2)}, u32[]{:S(2)}) collective-permute-start(bf16[1024,1408]{1,0:T(8,128)(2,1)S(1)} %assemble.3.refs_4_.refs_9_.refs_6_), channel_id=1, source_target_pairs={{0,16},{16,0},{1,17},{17,1},{2,18},{18,2},{3,19},{19,3},{4,20},{20... | collective-permute-start | bytes 8650760 | tf_op jit(solution)/shard_map/ppermute | solution.py:1065
  140.7 20.2 %collective-permute-start.30 = (bf16[128,1024]{1,0:T(8,128)(2,1)}, bf16[128,1024]{1,0:T(8,128)(2,1)S(1)}, u32[]{:S(2)}, u32[]{:S(2)}) collective-permute-start(bf16[128,1024]{1,0:T(8,128)(2,1)} %collective-permute-done.12.refs_0_.refs_6_), channel_id=1, source_target_pairs={{0,1},{1,0},{2,3},{3,2},{4,5},{5,4},{6,7},{7,6},{8,9},{9,8},{10,11... | collective-permute-start | bytes 786440 | tf_op jit(solution)/shard_map/ppermute | solution.py:1065
  142.2 19.8 %collective-permute-start.29 = (bf16[128,1024]{1,0:T(8,128)(2,1)}, bf16[128,1024]{1,0:T(8,128)(2,1)S(1)}, u32[]{:S(2)}, u32[]{:S(2)}) collective-permute-start(bf16[128,1024]{1,0:T(8,128)(2,1)} %collective-permute-done.12.refs_0_.refs_6_), channel_id=1, source_target_pairs={{0,2},{1,3},{2,0},{3,1},{4,6},{5,7},{6,4},{7,5},{8,10},{9,11},{10,... | collective-permute-start | bytes 786440 | tf_op jit(solution)/shard_map/ppermute | solution.py:1065
  299.4 18.6 %collective-permute-start.64 = (bf16[2176,128]{1,0:T(8,128)(2,1)S(1)}, bf16[2176,128]{1,0:T(8,128)(2,1)S(1)}, u32[]{:S(2)}, u32[]{:S(2)}) collective-permute-start(bf16[2176,128]{1,0:T(8,128)(2,1)S(1)} %fusion.2.refs_4_), channel_id=1, source_target_pairs={{0,4},{12,8},{4,0},{8,12},{1,5},{13,9},{5,1},{9,13},{2,6},{14,10},... | collective-permute-start | bytes 1671176 | tf_op jit(solution)/shard_map/ppermute | solution.py:1198
  318.6 18.6 %collective-permute-start.70 = (bf16[2176,128]{1,0:T(8,128)(2,1)S(1)}, bf16[2176,128]{1,0:T(8,128)(2,1)S(1)}, u32[]{:S(2)}, u32[]{:S(2)}) collective-permute-start(bf16[2176,128]{1,0:T(8,128)(2,1)S(1)} %fusion.3.refs_6_), channel_id=1, source_target_pairs={{0,4},{12,8},{4,0},{8,12},{1,5},{13,9},{5,1},{9,13},{2,6},{14,10},... | collective-permute-start | bytes 1671176 | tf_op jit(solution)/shard_map/ppermute | solution.py:1198
  337.8 22.6 %collective-permute-start.75 = (bf16[2176,128]{1,0:T(8,128)(2,1)S(1)}, bf16[2176,128]{1,0:T(8,128)(2,1)S(1)}, u32[]{:S(2)}, u32[]{:S(2)}) collective-permute-start(bf16[2176,128]{1,0:T(8,128)(2,1)S(1)} %fusion.4.refs_0_), channel_id=1, source_target_pairs={{0,4},{12,8},{4,0},{8,12},{1,5},{13,9},{5,1},{9,13},{2,6},{14,10},... | collective-permute-start | bytes 1671176 | tf_op jit(solution)/shard_map/ppermute | solution.py:1198
  340.1 20.3 %collective-permute-start.76 = (bf16[2176,128]{1,0:T(8,128)(2,1)S(1)}, bf16[2176,128]{1,0:T(8,128)(2,1)S(1)}, u32[]{:S(2)}, u32[]{:S(2)}) collective-permute-start(bf16[2176,128]{1,0:T(8,128)(2,1)S(1)} %add_convert_fusion.16), channel_id=1, source_target_pairs={{4,8},{8,4},{5,9},{9,5},{6,10},{10,6},{7,11},{11,7},{20,24},{24,20... | collective-permute-start | bytes 1671176 | tf_op jit(solution)/shard_map/ppermute | solution.py:1200
  343.0 17.4 %collective-permute-start.73 = (bf16[1472,128]{1,0:T(8,128)(2,1)S(1)}, bf16[1472,128]{1,0:T(8,128)(2,1)S(1)}, u32[]{:S(2)}, u32[]{:S(2)}) collective-permute-start(bf16[1472,128]{1,0:T(8,128)(2,1)S(1)} %get-tuple-element.683), channel_id=1, source_target_pairs={{0,2},{1,3},{2,0},{3,1},{4,6},{5,7},{6,4},{7,5},{8,10},{9,11},{10,... | collective-permute-start | bytes 1130504 | tf_op jit(solution)/shard_map/ppermute | solution.py:1065
  443.7 24.8 %collective-permute-start.105 = (bf16[8464,128]{1,0:T(8,128)(2,1)S(1)}, bf16[8464,128]{1,0:T(8,128)(2,1)S(1)}, u32[]{:S(2)}, u32[]{:S(2)}) collective-permute-start(bf16[8464,128]{1,0:T(8,128)(2,1)S(1)} %collect_feed.3.refs_0_), channel_id=1, source_target_pairs={{16,0},{17,1},{18,2},{19,3},{20,4},{21,5},{22,6},{23,7},{24,8},{25... | collective-permute-start | bytes 6500360 | tf_op jit(solution)/shard_map/ppermute | solution.py:1251
  449.8 18.8 %collective-permute-start.110 = (bf16[2176,128]{1,0:T(8,128)(2,1)S(1)}, bf16[2176,128]{1,0:T(8,128)(2,1)S(1)}, u32[]{:S(2)}, u32[]{:S(2)}) collective-permute-start(bf16[2176,128]{1,0:T(8,128)(2,1)S(1)} %add_convert_fusion), channel_id=1, source_target_pairs={{4,0},{8,12},{5,1},{9,13},{6,2},{10,14},{7,3},{11,15},{20,16},{24,... | collective-permute-start | bytes 1671176 | tf_op jit(solution)/shard_map/ppermute | solution.py:1198
  451.1 17.4 %collective-permute-start.107 = (bf16[2176,128]{1,0:T(8,128)(2,1)S(1)}, bf16[2176,128]{1,0:T(8,128)(2,1)S(1)}, u32[]{:S(2)}, u32[]{:S(2)}) collective-permute-start(bf16[2176,128]{1,0:T(8,128)(2,1)S(1)} %broadcast_select_fusion.1.refs_0_), channel_id=1, source_target_pairs={{16,0},{17,1},{18,2},{19,3},{20,4},{21,5},{22,6},{23,7},{24,8},{25... | collective-permute-start | bytes 1671176 | tf_op jit(solution)/shard_map/ppermute | solution.py:1251
  470.0 23.2 %collective-permute-start.111 = (bf16[2,128,1024]{2,1,0:T(8,128)(2,1)S(1)}, bf16[2,128,1024]{2,1,0:T(8,128)(2,1)S(1)}, u32[]{:S(2)}, u32[]{:S(2)}) collective-permute-start(bf16[2,128,1024]{2,1,0:T(8,128)(2,1)S(1)} %pad_maximum_fusion), channel_id=1, source_target_pairs={{0,0},{1,4},{2,8},{3,12},{4,1},{5,5},{6,9},{7,13},{8,2},{9,6},{10,... | collective-permute-start | bytes 1572872 | tf_op jit(solution)/shard_map/ppermute | solution.py:1117
  (178 other events, 2315.4 us)

commit v4 on v3

--- a/solution.py
+++ b/solution.py
@@ -60,6 +60,10 @@
 
 def shape(dims, kind=half):
     return jax.ShapeDtypeStruct(tuple(dims), kind)
+
+
+def kept(dims, kind=half):
+    return pltpu.HBM(tuple(dims), kind)
 
 
 def pack_heads(count, shard, place):
@@ -240,7 +244,7 @@
 
     outs = [shape((rows, width), wide if r == 0 else half) for r in range(count)] + [
         shape((total_rows, inner)),
-        shape((total_rows, width)),
+        (kept if layer else shape)((total_rows, width)),
         shape((total_rows, 3 * inner)),
         shape((16, total_rows), wide),
     ]
@@ -474,14 +478,15 @@
             take_rows(whole, ahead, place_ref)
 
     term_shapes = [shape((rows, width), wide if r == 0 else half) for r in range(count)]
-    outs = term_shapes + [
-        shape((total_rows, width)),
-        shape((total_rows, columns)),
-        shape((total_rows, hidden)),
-        shape((8, width), wide),
+    place_of = kept if forward else shape
+    outs = [place_of((rows, width), wide), *term_shapes[1:]] + [
+        place_of((total_rows, width)),
+        place_of((total_rows, columns)),
+        place_of((total_rows, hidden)),
+        place_of((8, width), wide),
     ]
     if forward:
-        outs = outs + term_shapes + [shape((total_rows, width))]
+        outs = outs + [kept(term.shape, term.dtype) for term in term_shapes] + [kept((total_rows, width))]
     scratch = [
         pltpu.VMEM((width, columns), half),
         pltpu.VMEM((padded, width), half),

time: 503 us -> 496 us (0.986)
  local copies, waits for them, and re-layouts: 34.1 us -> 25.6 us
    unnamed x180 -> x158, local copies, waits for them, and re-layouts: 30.2 us -> 21.7 us
  transfers between devices with their start and end apart: 113 -> 113, of which waited for: 53 -> 55; matrix products, arithmetic and copies ran while one was open for 1% -> 1% of each run, Pallas kernels for 14% -> 15%
where the time goes in v4:
time: 496 us; the launch traced here: 487 us
  waiting for transfers between devices  215 us (43%)
  starting transfers between devices  148 us (30%)
  Pallas kernels  89 us (18%)
  local copies, waits for them, and re-layouts  25.6 us (5%)
  other arithmetic  7.54 us (2%)
    ppermute x78, waiting for transfers between devices, exchange(): return lax.ppermute(value, axis, [(i, i ^ distance) for i in range(count)])  169 us
    ppermute x78, starting transfers between devices, exchange(): return lax.ppermute(value, axis, [(i, i ^ distance) for i in range(count)])  86 us
    ppermute x14, starting transfers between devices, go(): flight[0] = lax.ppermute(sent, 'ctx', route)  34.9 us
    ppermute x14, waiting for transfers between devices, go(): flight[0] = lax.ppermute(sent, 'ctx', route)  29.4 us
    unnamed x158, local copies, waits for them, and re-layouts  21.7 us
    ppermute x3, waiting for transfers between devices, turn_plane(): return lax.ppermute(value, ('section', 'ctx', 'fsdp'), pairs)  16.5 us
    pallas_call x2, Pallas kernels, feed_backward(): call(body, outs, specs, scratch, flops, moved, 'feed_backward')  16 us
    pallas_call x2, Pallas kernels, mix_backward(): call(body, outs, specs, scratch, flops, moved, 'mix_backward')  14.4 us
  transfers between devices with their start and end apart: 113, of which 55 were waited for; matrix products, arithmetic and copies ran while one was open for 1% of the time, Pallas kernels for 15%

profile of v4, /device:TPU:2, one launch (start us, length us, event | category | flops | bytes accessed | tf_op | source)
XLA Modules:
  0.0 487.3 jit_solution(9191180871902849669)
XLA Ops:
  32.9 15.8 %collective-permute-done.2.refs_3_ = bf16[160,1024]{1,0:T(8,128)(2,1)S(1)} collective-permute-done((bf16[160,1024]{1,0:T(8,128)(2,1)S(1)}, bf16[160,1024]{1,0:T(8,128)(2,1)S(1)}, u32[]{:S(2)}, u32[]{:S(2)}) %collective-permute-start.2) | collective-permute-done | bytes 327712 | tf_op jit(solution)/shard_map/ppermute | solution.py:1070
  67.2 6.7 %mix_forward.2 = (f32[128,1024]{1,0:T(8,128)S(1)}, bf16[128,1024]{1,0:T(8,128)(2,1)S(1)}, bf16[128,1024]{1,0:T(8,128)(2,1)S(1)}, bf16[128,1024]{1,0:T(8,128)(2,1...) custom-call(s32[3]{0:T(128)S(1)} %pad_add_fusion.2.place_ref, ...), custom_call_target="tpu_custom_call" | custom-call | flops 1342177280 | bytes 4718592 | tf_op jit(solution)/shard_map/mix_forward/pallas_call | solution.py:260
  81.3 7.8 %collective-permute-done.16.refs_2_ = bf16[256,1408]{1,0:T(8,128)(2,1)} collective-permute-done((bf16[256,1408]{1,0:T(8,128)(2,1)}, bf16[256,1408]{1,0:T(8,128)(2,1)}, u32[]{:S(2)}, u32[]{:S(2)}) %collective-permute-start.16) | collective-permute-done | bytes 720928 | tf_op jit(solution)/shard_map/ppermute | solution.py:1070
  89.2 6.8 %collective-permute-done.13.refs_1_ = bf16[128,1024]{1,0:T(8,128)(2,1)S(1)} collective-permute-done((bf16[128,1024]{1,0:T(8,128)(2,1)S(1)}, bf16[128,1024]{1,0:T(8,128)(2,1)S(1)}, u32[]{:S(2)}, u32[]{:S(2)}) %collective-permute-start.13) | collective-permute-done | bytes 262176 | tf_op jit(solution)/shard_map/ppermute | solution.py:1070
  106.4 5.6 %collective-permute-done.20.refs_1_ = bf16[128,1024]{1,0:T(8,128)(2,1)S(1)} collective-permute-done((bf16[128,1024]{1,0:T(8,128)(2,1)S(1)}, bf16[128,1024]{1,0:T(8,128)(2,1)S(1)}, u32[]{:S(2)}, u32[]{:S(2)}) %collective-permute-start.20) | collective-permute-done | bytes 262176 | tf_op jit(solution)/shard_map/ppermute | solution.py:1070
  112.1 6.9 %collective-permute-done.19.refs_2_ = bf16[128,1024]{1,0:T(8,128)(2,1)S(1)} collective-permute-done((bf16[128,1024]{1,0:T(8,128)(2,1)S(1)}, bf16[128,1024]{1,0:T(8,128)(2,1)S(1)}, u32[]{:S(2)}, u32[]{:S(2)}) %collective-permute-start.19) | collective-permute-done | bytes 262176 | tf_op jit(solution)/shard_map/ppermute | solution.py:1070
  127.1 5.8 %collective-permute-done.22.refs_1_ = bf16[128,1024]{1,0:T(8,128)(2,1)S(1)} collective-permute-done((bf16[128,1024]{1,0:T(8,128)(2,1)S(1)}, bf16[128,1024]{1,0:T(8,128)(2,1)S(1)}, u32[]{:S(2)}, u32[]{:S(2)}) %collective-permute-start.22) | collective-permute-done | bytes 262176 | tf_op jit(solution)/shard_map/ppermute | solution.py:1070
  148.0 5.7 %collective-permute-done.26.refs_2_ = bf16[128,1024]{1,0:T(8,128)(2,1)S(1)} collective-permute-done((bf16[128,1024]{1,0:T(8,128)(2,1)S(1)}, bf16[128,1024]{1,0:T(8,128)(2,1)S(1)}, u32[]{:S(2)}, u32[]{:S(2)}) %collective-permute-start.26) | collective-permute-done | bytes 262176 | tf_op jit(solution)/shard_map/ppermute | solution.py:1070
  153.7 7.0 %mix_forward.3 = (f32[128,1024]{1,0:T(8,128)S(1)}, bf16[128,1024]{1,0:T(8,128)(2,1)S(1)}, bf16[128,1024]{1,0:T(8,128)(2,1)S(1)}, bf16[128,1024]{1,0:T(8,128)(2,1...) custom-call(s32[3]{0:T(128)S(1)} %pad_add_fusion.2.place_ref, ...), custom_call_target="tpu_custom_call" | custom-call | flops 1342177280 | bytes 4718592 | tf_op jit(solution)/shard_map/mix_forward/pallas_call | solution.py:260
  185.3 10.0 %feed_backward.2 = (f32[128,1024]{1,0:T(8,128)}, bf16[128,1024]{1,0:T(8,128)(2,1)}, bf16[128,1024]{1,0:T(8,128)(2,1)}, bf16[128,1024]{1,0:T(8,128)(2,1)}, bf16[5...) custom-call(s32[3]{0:T(128)S(1)} %pad_add_fusion.2.place_ref, ...), custom_call_target="tpu_custom_call" | custom-call | flops 3690987520 | bytes 12779520 | tf_op jit(solution)/shard_map/feed_backward/pallas_call | solution.py:500
  214.4 5.6 %collective-permute-done.42.refs_1_ = bf16[128,1024]{1,0:T(8,128)(2,1)S(1)} collective-permute-done((bf16[128,1024]{1,0:T(8,128)(2,1)S(1)}, bf16[128,1024]{1,0:T(8,128)(2,1)S(1)}, u32[]{:S(2)}, u32[]{:S(2)}) %collective-permute-start.42) | collective-permute-done | bytes 262176 | tf_op jit(solution)/shard_map/ppermute | solution.py:1070
  220.0 5.9 %collective-permute-done.41.refs_2_ = bf16[128,1024]{1,0:T(8,128)(2,1)S(1)} collective-permute-done((bf16[128,1024]{1,0:T(8,128)(2,1)S(1)}, bf16[128,1024]{1,0:T(8,128)(2,1)S(1)}, u32[]{:S(2)}, u32[]{:S(2)}) %collective-permute-start.41) | collective-permute-done | bytes 262176 | tf_op jit(solution)/shard_map/ppermute | solution.py:1070
  233.4 7.1 %mix_backward.2 = (f32[128,1024]{1,0:T(8,128)S(1)}, bf16[128,1024]{1,0:T(8,128)(2,1)S(1)}, bf16[128,1024]{1,0:T(8,128)(2,1)S(1)}, bf16[128,1024]{1,0:T(8,128)(2,...) custom-call(s32[3]{0:T(128)S(1)} %copy-done.63, ...), custom_call_target="tpu_custom_call" | custom-call | flops 1744830464 | bytes 8912896 | tf_op jit(solution)/shard_map/mix_backward/pallas_call | solution.py:353
  267.0 5.0 %collective-permute-done.55.refs_1_ = bf16[128,1024]{1,0:T(8,128)(2,1)S(1)} collective-permute-done((bf16[128,1024]{1,0:T(8,128)(2,1)S(1)}, bf16[128,1024]{1,0:T(8,128)(2,1)S(1)}, u32[]{:S(2)}, u32[]{:S(2)}) %collective-permute-start.55) | collective-permute-done | bytes 262176 | tf_op jit(solution)/shard_map/ppermute | solution.py:1070
  279.1 6.0 %feed_backward.3 = (f32[128,1024]{1,0:T(8,128)S(1)}, bf16[128,1024]{1,0:T(8,128)(2,1)S(1)}, bf16[128,1024]{1,0:T(8,128)(2,1)S(1)}, bf16[128,1024]{1,0:T(8,128)(2...) custom-call(s32[3]{0:T(128)S(1)} %copy-done.63, ...), custom_call_target="tpu_custom_call" | custom-call | flops 3690987520 | bytes 12779520 | tf_op jit(solution)/shard_map/feed_backward/pallas_call | solution.py:500
  285.1 6.5 %collective-permute-done.59.refs_3_ = bf16[2176,128]{1,0:T(8,128)(2,1)S(1)} collective-permute-done((bf16[2176,128]{1,0:T(8,128)(2,1)S(1)}, bf16[2176,128]{1,0:T(8,128)(2,1)S(1)}, u32[]{:S(2)}, u32[]{:S(2)}) %collective-permute-start.59) | collective-permute-done | bytes 557088 | tf_op jit(solution)/shard_map/ppermute | solution.py:1203
  319.1 5.7 %collective-permute-done.69.refs_1_ = bf16[128,1024]{1,0:T(8,128)(2,1)S(1)} collective-permute-done((bf16[128,1024]{1,0:T(8,128)(2,1)S(1)}, bf16[128,1024]{1,0:T(8,128)(2,1)S(1)}, u32[]{:S(2)}, u32[]{:S(2)}) %collective-permute-start.69) | collective-permute-done | bytes 262176 | tf_op jit(solution)/shard_map/ppermute | solution.py:1070
  324.7 5.2 %collective-permute-done.68.refs_2_ = bf16[128,1024]{1,0:T(8,128)(2,1)S(1)} collective-permute-done((bf16[128,1024]{1,0:T(8,128)(2,1)S(1)}, bf16[128,1024]{1,0:T(8,128)(2,1)S(1)}, u32[]{:S(2)}, u32[]{:S(2)}) %collective-permute-start.68) | collective-permute-done | bytes 262176 | tf_op jit(solution)/shard_map/ppermute | solution.py:1070
  337.8 7.3 %mix_backward.3 = (f32[128,1024]{1,0:T(8,128)S(1)}, bf16[128,1024]{1,0:T(8,128)(2,1)S(1)}, bf16[128,1024]{1,0:T(8,128)(2,1)S(1)}, bf16[128,1024]{1,0:T(8,128)(2,...) custom-call(s32[3]{0:T(128)S(1)} %copy-done.63, ...), custom_call_target="tpu_custom_call" | custom-call | flops 1744830464 | bytes 8912896 | tf_op jit(solution)/shard_map/mix_backward/pallas_call | solution.py:353
  346.0 7.0 %collective-permute-done.73.refs_2_ = bf16[1472,128]{1,0:T(8,128)(2,1)S(1)} collective-permute-done((bf16[1472,128]{1,0:T(8,128)(2,1)S(1)}, bf16[1472,128]{1,0:T(8,128)(2,1)S(1)}, u32[]{:S(2)}, u32[]{:S(2)}) %collective-permute-start.73) | collective-permute-done | bytes 376864 | tf_op jit(solution)/shard_map/ppermute | solution.py:1070
  373.7 7.4 %collective-permute-done.83.refs_1_ = bf16[2176,128]{1,0:T(8,128)(2,1)S(1)} collective-permute-done((bf16[2176,128]{1,0:T(8,128)(2,1)S(1)}, bf16[2176,128]{1,0:T(8,128)(2,1)S(1)}, u32[]{:S(2)}, u32[]{:S(2)}) %collective-permute-start.83) | collective-permute-done | bytes 557088 | tf_op jit(solution)/shard_map/ppermute | solution.py:1203
  445.7 15.2 %collective-permute-done.110 = bf16[2176,128]{1,0:T(8,128)(2,1)S(1)} collective-permute-done((bf16[2176,128]{1,0:T(8,128)(2,1)S(1)}, bf16[2176,128]{1,0:T(8,128)(2,1)S(1)}, u32[]{:S(2)}, u32[]{:S(2)}) %collective-permute-start.110) | collective-permute-done | bytes 557088 | tf_op jit(solution)/shard_map/ppermute | solution.py:1203
  464.8 5.1 %unpack_feed.1 = (f32[256,5632]{1,0:T(8,128)}, f32[704,1024]{1,0:T(8,128)}, f32[1,256]{1,0:T(1,128)}) custom-call(s32[4]{0:T(128)S(1)} %pad_add_fusion.1.place_ref, bf16[8464,128]{1,0:T(8,128)(2,1)S(1)} %collect_feed.3.refs_0_, bf16[8464,128]{1,0:T(8,128)(2,1)S(1)} %collective-permute-done.105.refs_1_, bf16[8464,128]{1,0:T(8,128)(2,1)S(1)} %collect_feed.2.refs_2_, ...), custom_call_target="tpu_custom_call" | custom-call | bytes 12985344 | tf_op jit(solution)/shard_map/unpack_feed/pallas_call | solution.py:1005
  473.0 12.6 %collective-permute-done.111 = bf16[2,128,1024]{2,1,0:T(8,128)(2,1)S(1)} collective-permute-done((bf16[2,128,1024]{2,1,0:T(8,128)(2,1)S(1)}, bf16[2,128,1024]{2,1,0:T(8,128)(2,1)S(1)}, u32[]{:S(2)}, u32[]{:S(2)}) %collective-permute-start.111) | collective-permute-done | bytes 524320 | tf_op jit(solution)/shard_map/ppermute | solution.py:1122
  (432 shorter events, 305.5 us)
Async XLA Ops:
  19.1 29.5 %collective-permute-start.6 = (bf16[256,768]{1,0:T(8,128)(2,1)S(1)}, bf16[256,768]{1,0:T(8,128)(2,1)S(1)}, u32[]{:S(2)}, u32[]{:S(2)}) collective-permute-start(bf16[256,768]{1,0:T(8,128)(2,1)S(1)} %get-tuple-element.442), channel_id=1, source_target_pairs={{0,1},{1,0},{2,3},{3,2},{4,5},{5,4},{6,7},{7,6},{8,9},{9,8},{10,11... | collective-permute-start | bytes 1179656 | tf_op jit(solution)/shard_map/ppermute | solution.py:1070
  21.0 27.8 %collective-permute-start.7 = (bf16[256,768]{1,0:T(8,128)(2,1)S(1)}, bf16[256,768]{1,0:T(8,128)(2,1)S(1)}, u32[]{:S(2)}, u32[]{:S(2)}) collective-permute-start(bf16[256,768]{1,0:T(8,128)(2,1)S(1)} %get-tuple-element.443), channel_id=1, source_target_pairs={{0,2},{1,3},{2,0},{3,1},{4,6},{5,7},{6,4},{7,5},{8,10},{9,11},{10,... | collective-permute-start | bytes 1179656 | tf_op jit(solution)/shard_map/ppermute | solution.py:1070
  23.0 25.8 %collective-permute-start.8 = (bf16[256,768]{1,0:T(8,128)(2,1)S(1)}, bf16[256,768]{1,0:T(8,128)(2,1)S(1)}, u32[]{:S(2)}, u32[]{:S(2)}) collective-permute-start(bf16[256,768]{1,0:T(8,128)(2,1)S(1)} %get-tuple-element.444), channel_id=1, source_target_pairs={{0,3},{1,2},{2,1},{3,0},{4,7},{5,6},{6,5},{7,4},{8,11},{9,10},{10,... | collective-permute-start | bytes 1179656 | tf_op jit(solution)/shard_map/ppermute | solution.py:1070
  25.7 22.9 %collective-permute-start.2 = (bf16[160,1024]{1,0:T(8,128)(2,1)S(1)}, bf16[160,1024]{1,0:T(8,128)(2,1)S(1)}, u32[]{:S(2)}, u32[]{:S(2)}) collective-permute-start(bf16[160,1024]{1,0:T(8,128)(2,1)S(1)} %beside.1.refs_0_), channel_id=1, source_target_pairs={{0,3},{1,2},{2,1},{3,0},{4,7},{5,6},{6,5},{7,4},{8,11},{9,10},{10,... | collective-permute-start | bytes 983048 | tf_op jit(solution)/shard_map/ppermute | solution.py:1070
  28.1 28.0 %collective-permute-start.5 = (bf16[704,1024]{1,0:T(8,128)(2,1)}, bf16[704,1024]{1,0:T(8,128)(2,1)S(1)}, u32[]{:S(2)}, u32[]{:S(2)}) collective-permute-start(bf16[704,1024]{1,0:T(8,128)(2,1)} %bitcast.36), channel_id=1, source_target_pairs={{0,16},{16,0},{1,17},{17,1},{2,18},{18,2},{3,19},{19,3},{4,20},{20... | collective-permute-start | bytes 4325384 | tf_op jit(solution)/shard_map/ppermute | solution.py:1070
  50.1 24.9 %collective-permute-start.11 = (bf16[256,1408]{1,0:T(8,128)(2,1)}, bf16[256,1408]{1,0:T(8,128)(2,1)}, u32[]{:S(2)}, u32[]{:S(2)}) collective-permute-start(bf16[256,1408]{1,0:T(8,128)(2,1)} %get-tuple-element.461), channel_id=1, source_target_pairs={{0,1},{1,0},{2,3},{3,2},{4,5},{5,4},{6,7},{7,6},{8,9},{9,8},{10,11... | collective-permute-start | bytes 2162696 | tf_op jit(solution)/shard_map/ppermute | solution.py:1070
  51.6 37.6 %collective-permute-start.16 = (bf16[256,1408]{1,0:T(8,128)(2,1)}, bf16[256,1408]{1,0:T(8,128)(2,1)}, u32[]{:S(2)}, u32[]{:S(2)}) collective-permute-start(bf16[256,1408]{1,0:T(8,128)(2,1)} %get-tuple-element.470), channel_id=1, source_target_pairs={{0,2},{1,3},{2,0},{3,1},{4,6},{5,7},{6,4},{7,5},{8,10},{9,11},{10,... | collective-permute-start | bytes 2162696 | tf_op jit(solution)/shard_map/ppermute | solution.py:1070
  54.5 34.7 %collective-permute-start.17 = (bf16[256,1408]{1,0:T(8,128)(2,1)}, bf16[256,1408]{1,0:T(8,128)(2,1)}, u32[]{:S(2)}, u32[]{:S(2)}) collective-permute-start(bf16[256,1408]{1,0:T(8,128)(2,1)} %get-tuple-element.471), channel_id=1, source_target_pairs={{0,3},{1,2},{2,1},{3,0},{4,7},{5,6},{6,5},{7,4},{8,11},{9,10},{10,... | collective-permute-start | bytes 2162696 | tf_op jit(solution)/shard_map/ppermute | solution.py:1070
  57.2 17.7 %collective-permute-start.12 = (bf16[128,1024]{1,0:T(8,128)(2,1)}, bf16[128,1024]{1,0:T(8,128)(2,1)}, u32[]{:S(2)}, u32[]{:S(2)}) collective-permute-start(bf16[128,1024]{1,0:T(8,128)(2,1)} %dynamic-slice_bitcast_fusion), channel_id=1, source_target_pairs={{0,0},{1,4},{2,8},{3,12},{4,1},{5,5},{6,9},{7,13},{8,2},{9,6},{10,... | collective-permute-start | bytes 786440 | tf_op jit(solution)/shard_map/ppermute | solution.py:1122
  75.0 21.0 %collective-permute-start.13 = (bf16[128,1024]{1,0:T(8,128)(2,1)S(1)}, bf16[128,1024]{1,0:T(8,128)(2,1)S(1)}, u32[]{:S(2)}, u32[]{:S(2)}) collective-permute-start(bf16[128,1024]{1,0:T(8,128)(2,1)S(1)} %get-tuple-element.465), channel_id=1, source_target_pairs={{0,1},{1,0},{2,3},{3,2},{4,5},{5,4},{6,7},{7,6},{8,9},{9,8},{10,11... | collective-permute-start | bytes 786440 | tf_op jit(solution)/shard_map/ppermute | solution.py:1070
  77.3 22.1 %collective-permute-start.14 = (bf16[128,1024]{1,0:T(8,128)(2,1)S(1)}, bf16[128,1024]{1,0:T(8,128)(2,1)S(1)}, u32[]{:S(2)}, u32[]{:S(2)}) collective-permute-start(bf16[128,1024]{1,0:T(8,128)(2,1)S(1)} %get-tuple-element.466), channel_id=1, source_target_pairs={{0,2},{1,3},{2,0},{3,1},{4,6},{5,7},{6,4},{7,5},{8,10},{9,11},{10,... | collective-permute-start | bytes 786440 | tf_op jit(solution)/shard_map/ppermute | solution.py:1070
  79.9 19.5 %collective-permute-start.15 = (bf16[128,1024]{1,0:T(8,128)(2,1)S(1)}, bf16[128,1024]{1,0:T(8,128)(2,1)S(1)}, u32[]{:S(2)}, u32[]{:S(2)}) collective-permute-start(bf16[128,1024]{1,0:T(8,128)(2,1)S(1)} %get-tuple-element.467), channel_id=1, source_target_pairs={{0,3},{1,2},{2,1},{3,0},{4,7},{5,6},{6,5},{7,4},{8,11},{9,10},{10,... | collective-permute-start | bytes 786440 | tf_op jit(solution)/shard_map/ppermute | solution.py:1070
  101.4 17.6 %collective-permute-start.21 = (bf16[1024,1408]{1,0:T(8,128)(2,1)S(1)}, bf16[1024,1408]{1,0:T(8,128)(2,1)S(1)}, u32[]{:S(2)}, u32[]{:S(2)}) collective-permute-start(bf16[1024,1408]{1,0:T(8,128)(2,1)S(1)} %assemble.3.refs_4_.refs_9_.refs_6_), channel_id=1, source_target_pairs={{0,16},{16,0},{1,17},{17,1},{2,18},{18,2},{3,19},{19,3},{4,20},{20... | collective-permute-start | bytes 8650760 | tf_op jit(solution)/shard_map/ppermute | solution.py:1070
  140.7 20.0 %collective-permute-start.30 = (bf16[128,1024]{1,0:T(8,128)(2,1)}, bf16[128,1024]{1,0:T(8,128)(2,1)S(1)}, u32[]{:S(2)}, u32[]{:S(2)}) collective-permute-start(bf16[128,1024]{1,0:T(8,128)(2,1)} %collective-permute-done.12.refs_0_.refs_6_), channel_id=1, source_target_pairs={{0,1},{1,0},{2,3},{3,2},{4,5},{5,4},{6,7},{7,6},{8,9},{9,8},{10,11... | collective-permute-start | bytes 786440 | tf_op jit(solution)/shard_map/ppermute | solution.py:1070
  142.2 19.8 %collective-permute-start.29 = (bf16[128,1024]{1,0:T(8,128)(2,1)}, bf16[128,1024]{1,0:T(8,128)(2,1)S(1)}, u32[]{:S(2)}, u32[]{:S(2)}) collective-permute-start(bf16[128,1024]{1,0:T(8,128)(2,1)} %collective-permute-done.12.refs_0_.refs_6_), channel_id=1, source_target_pairs={{0,2},{1,3},{2,0},{3,1},{4,6},{5,7},{6,4},{7,5},{8,10},{9,11},{10,... | collective-permute-start | bytes 786440 | tf_op jit(solution)/shard_map/ppermute | solution.py:1070
  226.2 16.8 %collective-permute-start.47 = (bf16[2176,128]{1,0:T(8,128)(2,1)S(1)}, bf16[2176,128]{1,0:T(8,128)(2,1)S(1)}, u32[]{:S(2)}, u32[]{:S(2)}) collective-permute-start(bf16[2176,128]{1,0:T(8,128)(2,1)S(1)} %get-tuple-element.559), channel_id=1, source_target_pairs={{0,4},{12,8},{1,5},{13,9},{2,6},{14,10},{3,7},{15,11},{16,20},{28,... | collective-permute-start | bytes 1671176 | tf_op jit(solution)/shard_map/ppermute | solution.py:1203
  292.1 18.6 %collective-permute-start.64 = (bf16[2176,128]{1,0:T(8,128)(2,1)S(1)}, bf16[2176,128]{1,0:T(8,128)(2,1)S(1)}, u32[]{:S(2)}, u32[]{:S(2)}) collective-permute-start(bf16[2176,128]{1,0:T(8,128)(2,1)S(1)} %fusion.2.refs_4_), channel_id=1, source_target_pairs={{0,4},{12,8},{4,0},{8,12},{1,5},{13,9},{5,1},{9,13},{2,6},{14,10},... | collective-permute-start | bytes 1671176 | tf_op jit(solution)/shard_map/ppermute | solution.py:1203
  311.3 18.7 %collective-permute-start.70 = (bf16[2176,128]{1,0:T(8,128)(2,1)S(1)}, bf16[2176,128]{1,0:T(8,128)(2,1)S(1)}, u32[]{:S(2)}, u32[]{:S(2)}) collective-permute-start(bf16[2176,128]{1,0:T(8,128)(2,1)S(1)} %fusion.3.refs_6_), channel_id=1, source_target_pairs={{0,4},{12,8},{4,0},{8,12},{1,5},{13,9},{5,1},{9,13},{2,6},{14,10},... | collective-permute-start | bytes 1671176 | tf_op jit(solution)/shard_map/ppermute | solution.py:1203
  330.5 22.5 %collective-permute-start.75 = (bf16[2176,128]{1,0:T(8,128)(2,1)S(1)}, bf16[2176,128]{1,0:T(8,128)(2,1)S(1)}, u32[]{:S(2)}, u32[]{:S(2)}) collective-permute-start(bf16[2176,128]{1,0:T(8,128)(2,1)S(1)} %fusion.4.refs_0_), channel_id=1, source_target_pairs={{0,4},{12,8},{4,0},{8,12},{1,5},{13,9},{5,1},{9,13},{2,6},{14,10},... | collective-permute-start | bytes 1671176 | tf_op jit(solution)/shard_map/ppermute | solution.py:1203
  332.9 20.2 %collective-permute-start.76 = (bf16[2176,128]{1,0:T(8,128)(2,1)S(1)}, bf16[2176,128]{1,0:T(8,128)(2,1)S(1)}, u32[]{:S(2)}, u32[]{:S(2)}) collective-permute-start(bf16[2176,128]{1,0:T(8,128)(2,1)S(1)} %add_convert_fusion.16), channel_id=1, source_target_pairs={{4,8},{8,4},{5,9},{9,5},{6,10},{10,6},{7,11},{11,7},{20,24},{24,20... | collective-permute-start | bytes 1671176 | tf_op jit(solution)/shard_map/ppermute | solution.py:1205
  335.7 17.4 %collective-permute-start.73 = (bf16[1472,128]{1,0:T(8,128)(2,1)S(1)}, bf16[1472,128]{1,0:T(8,128)(2,1)S(1)}, u32[]{:S(2)}, u32[]{:S(2)}) collective-permute-start(bf16[1472,128]{1,0:T(8,128)(2,1)S(1)} %get-tuple-element.683), channel_id=1, source_target_pairs={{0,2},{1,3},{2,0},{3,1},{4,6},{5,7},{6,4},{7,5},{8,10},{9,11},{10,... | collective-permute-start | bytes 1130504 | tf_op jit(solution)/shard_map/ppermute | solution.py:1070
  436.9 24.1 %collective-permute-start.105 = (bf16[8464,128]{1,0:T(8,128)(2,1)S(1)}, bf16[8464,128]{1,0:T(8,128)(2,1)S(1)}, u32[]{:S(2)}, u32[]{:S(2)}) collective-permute-start(bf16[8464,128]{1,0:T(8,128)(2,1)S(1)} %collect_feed.3.refs_0_), channel_id=1, source_target_pairs={{16,0},{17,1},{18,2},{19,3},{20,4},{21,5},{22,6},{23,7},{24,8},{25... | collective-permute-start | bytes 6500360 | tf_op jit(solution)/shard_map/ppermute | solution.py:1256
  442.9 18.0 %collective-permute-start.110 = (bf16[2176,128]{1,0:T(8,128)(2,1)S(1)}, bf16[2176,128]{1,0:T(8,128)(2,1)S(1)}, u32[]{:S(2)}, u32[]{:S(2)}) collective-permute-start(bf16[2176,128]{1,0:T(8,128)(2,1)S(1)} %add_convert_fusion), channel_id=1, source_target_pairs={{4,0},{8,12},{5,1},{9,13},{6,2},{10,14},{7,3},{11,15},{20,16},{24,... | collective-permute-start | bytes 1671176 | tf_op jit(solution)/shard_map/ppermute | solution.py:1203
  462.4 23.2 %collective-permute-start.111 = (bf16[2,128,1024]{2,1,0:T(8,128)(2,1)S(1)}, bf16[2,128,1024]{2,1,0:T(8,128)(2,1)S(1)}, u32[]{:S(2)}, u32[]{:S(2)}) collective-permute-start(bf16[2,128,1024]{2,1,0:T(8,128)(2,1)S(1)} %pad_maximum_fusion), channel_id=1, source_target_pairs={{0,0},{1,4},{2,8},{3,12},{4,1},{5,5},{6,9},{7,13},{8,2},{9,6},{10,... | collective-permute-start | bytes 1572872 | tf_op jit(solution)/shard_map/ppermute | solution.py:1122
  (167 other events, 2280.3 us)

commit v5 on v4

--- a/solution.py
+++ b/solution.py
@@ -920,60 +920,58 @@
     return call(body, outs, [smem] + [vmem] * (count + 1), scratch, 0, total * 512, "collect_mix")(place, *parts, local)
 
 
-def gather_halves(place_ref, ins, halves, sems, edges):
-    chunks = len(edges) - 1
-    handles = []
-    for side in range(2):
-        for c in range(chunks):
-            spot = place_ref[1] if side == 0 else 1 - place_ref[1]
-            where = halves.at[spot, pl.ds(edges[c], edges[c + 1] - edges[c])]
-            sem = sems.at[side * chunks + c]
-            for layer in range(2):
-                source = ins[layer * 2 * chunks + side * chunks + c]
-
-                @pl.when(place_ref[1] == layer)
-                def _(source=source, where=where, sem=sem):
-                    pltpu.make_async_copy(source, where, sem).start()
-
-            handles.append(pltpu.make_async_copy(ins[side * chunks + c], where, sem))
-    finish(handles)
+def gather_halves(place_ref, ins, halves, sems, counts):
+    first = 0
+    for layer, many in enumerate(counts):
+        pieces = [ins[first : first + many], ins[first + many : first + 2 * many]]
+        first += 2 * many
+
+        @pl.when(place_ref[1] == layer)
+        def _(pieces=pieces, many=many):
+            handles = []
+            for side in range(2):
+                spot = place_ref[1] if side == 0 else 1 - place_ref[1]
+                at = 0
+                for c, piece in enumerate(pieces[side]):
+                    where = halves.at[spot, pl.ds(at, piece.shape[0])]
+                    handles.append(pltpu.make_async_copy(piece, where, sems.at[side * many + c]))
+                    handles[-1].start()
+                    at += piece.shape[0]
+            finish(handles)
 
 
 def unpack(body, totals, out_shape, place, name):
-    chunks = len(totals[0][0])
-    edges = [0]
-    for chunk in totals[0][0]:
-        edges.append(edges[-1] + chunk.shape[0])
+    counts = [len(own) for own, _ in totals]
+    rows = sum(chunk.shape[0] for chunk in totals[0][0])
+    inputs = [piece for layer in totals for side in layer for piece in side]
 
     def whole_body(place_ref, *refs):
-        ins, outs, halves, sems = refs[: 4 * chunks], refs[4 * chunks : -2], refs[-2], refs[-1]
-        gather_halves(place_ref, ins, halves, sems, edges)
+        ins, outs, halves, sems = refs[: len(inputs)], refs[len(inputs) : -2], refs[-2], refs[-1]
+        gather_halves(place_ref, ins, halves, sems, counts)
         body(place_ref, halves, *outs)
 
-    inputs = [piece for layer in totals for side in layer for piece in side]
-    scratch = [pltpu.VMEM((2, edges[-1], LANES), half), pltpu.SemaphoreType.DMA((2 * chunks,))]
-    moved = sum(o.size * 4 for o in out_shape) + 4 * edges[-1] * LANES
+    scratch = [pltpu.VMEM((2, rows, LANES), half), pltpu.SemaphoreType.DMA((2 * max(counts),))]
+    moved = sum(o.size * 4 for o in out_shape) + 4 * rows * LANES
     return call(whole_body, out_shape, [smem] + [anywhere] * len(inputs), scratch, 0, moved, name)(place, *inputs)
 
 
 def unpack_feed(count, columns, hidden, width, totals, place):
     part = width // count
     side = width // 2
-    chunks = len(totals[0][0])
-    edges = [0]
-    for chunk in totals[0][0]:
-        edges.append(edges[-1] + chunk.shape[0])
+    counts = [len(own) for own, _ in totals]
+    total = sum(chunk.shape[0] for chunk in totals[0][0])
+    inputs = [piece for layer in totals for half_side in layer for piece in half_side]
     steps = 4
     span = count * columns // steps
     tiles = span // LANES
 
     def body(place_ref, *refs):
-        ins, (gate_up, down, gain), halves, sems = refs[: 4 * chunks], refs[4 * chunks : -2], refs[-2], refs[-1]
+        ins, (gate_up, down, gain), halves, sems = refs[: len(inputs)], refs[len(inputs) : -2], refs[-2], refs[-1]
         step = pl.program_id(0)
 
         @pl.when(step == 0)
         def _():
-            gather_halves(place_ref, ins, halves, sems, edges)
+            gather_halves(place_ref, ins, halves, sems, counts)
             base = count * columns
             for h in range(2):
                 gain[0:1, h * LANES : (h + 1) * LANES] = halves[h, base : base + SMALL, :].astype(wide)[0:1]
@@ -1000,8 +998,7 @@
             down[:, c * LANES : (c + 1) * LANES] = halves[step // 2, pl.ds(at, hidden), :].astype(wide)
 
     outs = [shape((part, count * columns), wide), shape((hidden, width), wide), shape((1, part), wide)]
-    inputs = [piece for layer in totals for half_side in layer for piece in half_side]
-    moved = sum(o.size * 4 for o in outs) + 4 * edges[-1] * LANES
+    moved = sum(o.size * 4 for o in outs) + 4 * total * LANES
     return pl.pallas_call(
         body,
         grid=(steps,),
@@ -1012,7 +1009,7 @@
             pl.BlockSpec((hidden, width // steps), lambda i: (0, i)),
             pl.BlockSpec((1, part), lambda i: (0, 0)),
         ],
-        scratch_shapes=[pltpu.VMEM((2, edges[-1], LANES), half), pltpu.SemaphoreType.DMA((2 * chunks,))],
+        scratch_shapes=[pltpu.VMEM((2, total, LANES), half), pltpu.SemaphoreType.DMA((2 * max(counts),))],
         compiler_params=pltpu.CompilerParams(vmem_limit_bytes=16 * 1024 * 1024),
         cost_estimate=pl.CostEstimate(flops=0, bytes_accessed=moved, transcendentals=0),
         name="unpack_feed",
@@ -1312,7 +1309,7 @@
     (m1,) = step(m1)
     feed_second_other = to_owner(1, feed_second)
     f0_last = trade_strips(taken(2))
-    mix_second = collect_mix(2, heads, pad, place, *m1)
+    mix_second = collect_mix(1, heads, pad, place, *m1)
     f0_last, mix_second, g_input = step(f0_last, mix_second, g_input)
     feed_first = collect_feed(columns, place, [f0, f0_last])
     feed_first_other = to_owner(0, feed_first)

time: 496 us -> 495 us (level)
    ppermute x6 -> x5, starting transfers between devices: 9.95 us -> 8.66 us  [to_owner(): lax.ppermute(chunk, 'section', [(1 - layer, layer)])]
  transfers between devices with their start and end apart: 113 -> 112, of which waited for: 55 -> 54; matrix products, arithmetic and copies ran while one was open for 1% -> 1% of each run, Pallas kernels for 15% -> 15%
where the time goes in v5:
time: 495 us; the launch traced here: 486 us
  waiting for transfers between devices  215 us (43%)
  starting transfers between devices  146 us (29%)
  Pallas kernels  88.9 us (18%)
  local copies, waits for them, and re-layouts  25.6 us (5%)
  other arithmetic  7.29 us (1%)
    ppermute x78, waiting for transfers between devices, exchange(): return lax.ppermute(value, axis, [(i, i ^ distance) for i in range(count)])  169 us
    ppermute x78, starting transfers between devices, exchange(): return lax.ppermute(value, axis, [(i, i ^ distance) for i in range(count)])  85.8 us
    ppermute x14, starting transfers between devices, go(): flight[0] = lax.ppermute(sent, 'ctx', route)  35 us
    ppermute x14, waiting for transfers between devices, go(): flight[0] = lax.ppermute(sent, 'ctx', route)  29.3 us
    unnamed x158, local copies, waits for them, and re-layouts  21.8 us
    ppermute x3, waiting for transfers between devices, turn_plane(): return lax.ppermute(value, ('section', 'ctx', 'fsdp'), pairs)  16.6 us
    pallas_call x2, Pallas kernels, feed_backward(): call(body, outs, specs, scratch, flops, moved, 'feed_backward')  16 us
    pallas_call x2, Pallas kernels, mix_backward(): call(body, outs, specs, scratch, flops, moved, 'mix_backward')  14.4 us
  transfers between devices with their start and end apart: 112, of which 54 were waited for; matrix products, arithmetic and copies ran while one was open for 1% of the time, Pallas kernels for 15%

profile of v5, /device:TPU:2, one launch (start us, length us, event | category | flops | bytes accessed | tf_op | source)
XLA Modules:
  0.0 486.0 jit_solution(12873952854655287838)
XLA Ops:
  32.8 15.8 %collective-permute-done.2.refs_3_ = bf16[160,1024]{1,0:T(8,128)(2,1)S(1)} collective-permute-done((bf16[160,1024]{1,0:T(8,128)(2,1)S(1)}, bf16[160,1024]{1,0:T(8,128)(2,1)S(1)}, u32[]{:S(2)}, u32[]{:S(2)}) %collective-permute-start.2) | collective-permute-done | bytes 327712 | tf_op jit(solution)/shard_map/ppermute | solution.py:1067
  67.1 6.7 %mix_forward.2 = (f32[128,1024]{1,0:T(8,128)S(1)}, bf16[128,1024]{1,0:T(8,128)(2,1)S(1)}, bf16[128,1024]{1,0:T(8,128)(2,1)S(1)}, bf16[128,1024]{1,0:T(8,128)(2,1...) custom-call(s32[3]{0:T(128)S(1)} %pad_add_fusion.2.place_ref, ...), custom_call_target="tpu_custom_call" | custom-call | flops 1342177280 | bytes 4718592 | tf_op jit(solution)/shard_map/mix_forward/pallas_call | solution.py:260
  81.2 8.0 %collective-permute-done.16.refs_2_ = bf16[256,1408]{1,0:T(8,128)(2,1)} collective-permute-done((bf16[256,1408]{1,0:T(8,128)(2,1)}, bf16[256,1408]{1,0:T(8,128)(2,1)}, u32[]{:S(2)}, u32[]{:S(2)}) %collective-permute-start.16) | collective-permute-done | bytes 720928 | tf_op jit(solution)/shard_map/ppermute | solution.py:1067
  89.2 6.8 %collective-permute-done.13.refs_1_ = bf16[128,1024]{1,0:T(8,128)(2,1)S(1)} collective-permute-done((bf16[128,1024]{1,0:T(8,128)(2,1)S(1)}, bf16[128,1024]{1,0:T(8,128)(2,1)S(1)}, u32[]{:S(2)}, u32[]{:S(2)}) %collective-permute-start.13) | collective-permute-done | bytes 262176 | tf_op jit(solution)/shard_map/ppermute | solution.py:1067
  106.4 5.6 %collective-permute-done.20.refs_1_ = bf16[128,1024]{1,0:T(8,128)(2,1)S(1)} collective-permute-done((bf16[128,1024]{1,0:T(8,128)(2,1)S(1)}, bf16[128,1024]{1,0:T(8,128)(2,1)S(1)}, u32[]{:S(2)}, u32[]{:S(2)}) %collective-permute-start.20) | collective-permute-done | bytes 262176 | tf_op jit(solution)/shard_map/ppermute | solution.py:1067
  112.1 6.9 %collective-permute-done.19.refs_2_ = bf16[128,1024]{1,0:T(8,128)(2,1)S(1)} collective-permute-done((bf16[128,1024]{1,0:T(8,128)(2,1)S(1)}, bf16[128,1024]{1,0:T(8,128)(2,1)S(1)}, u32[]{:S(2)}, u32[]{:S(2)}) %collective-permute-start.19) | collective-permute-done | bytes 262176 | tf_op jit(solution)/shard_map/ppermute | solution.py:1067
  127.1 5.8 %collective-permute-done.22.refs_1_ = bf16[128,1024]{1,0:T(8,128)(2,1)S(1)} collective-permute-done((bf16[128,1024]{1,0:T(8,128)(2,1)S(1)}, bf16[128,1024]{1,0:T(8,128)(2,1)S(1)}, u32[]{:S(2)}, u32[]{:S(2)}) %collective-permute-start.22) | collective-permute-done | bytes 262176 | tf_op jit(solution)/shard_map/ppermute | solution.py:1067
  148.0 5.7 %collective-permute-done.26.refs_2_ = bf16[128,1024]{1,0:T(8,128)(2,1)S(1)} collective-permute-done((bf16[128,1024]{1,0:T(8,128)(2,1)S(1)}, bf16[128,1024]{1,0:T(8,128)(2,1)S(1)}, u32[]{:S(2)}, u32[]{:S(2)}) %collective-permute-start.26) | collective-permute-done | bytes 262176 | tf_op jit(solution)/shard_map/ppermute | solution.py:1067
  153.7 7.0 %mix_forward.3 = (f32[128,1024]{1,0:T(8,128)S(1)}, bf16[128,1024]{1,0:T(8,128)(2,1)S(1)}, bf16[128,1024]{1,0:T(8,128)(2,1)S(1)}, bf16[128,1024]{1,0:T(8,128)(2,1...) custom-call(s32[3]{0:T(128)S(1)} %pad_add_fusion.2.place_ref, ...), custom_call_target="tpu_custom_call" | custom-call | flops 1342177280 | bytes 4718592 | tf_op jit(solution)/shard_map/mix_forward/pallas_call | solution.py:260
  185.3 10.0 %feed_backward.2 = (f32[128,1024]{1,0:T(8,128)}, bf16[128,1024]{1,0:T(8,128)(2,1)}, bf16[128,1024]{1,0:T(8,128)(2,1)}, bf16[128,1024]{1,0:T(8,128)(2,1)}, bf16[5...) custom-call(s32[3]{0:T(128)S(1)} %pad_add_fusion.2.place_ref, ...), custom_call_target="tpu_custom_call" | custom-call | flops 3690987520 | bytes 12779520 | tf_op jit(solution)/shard_map/feed_backward/pallas_call | solution.py:500
  214.2 5.6 %collective-permute-done.42.refs_1_ = bf16[128,1024]{1,0:T(8,128)(2,1)S(1)} collective-permute-done((bf16[128,1024]{1,0:T(8,128)(2,1)S(1)}, bf16[128,1024]{1,0:T(8,128)(2,1)S(1)}, u32[]{:S(2)}, u32[]{:S(2)}) %collective-permute-start.42) | collective-permute-done | bytes 262176 | tf_op jit(solution)/shard_map/ppermute | solution.py:1067
  219.9 5.9 %collective-permute-done.41.refs_2_ = bf16[128,1024]{1,0:T(8,128)(2,1)S(1)} collective-permute-done((bf16[128,1024]{1,0:T(8,128)(2,1)S(1)}, bf16[128,1024]{1,0:T(8,128)(2,1)S(1)}, u32[]{:S(2)}, u32[]{:S(2)}) %collective-permute-start.41) | collective-permute-done | bytes 262176 | tf_op jit(solution)/shard_map/ppermute | solution.py:1067
  233.3 7.1 %mix_backward.2 = (f32[128,1024]{1,0:T(8,128)S(1)}, bf16[128,1024]{1,0:T(8,128)(2,1)S(1)}, bf16[128,1024]{1,0:T(8,128)(2,1)S(1)}, bf16[128,1024]{1,0:T(8,128)(2,...) custom-call(s32[3]{0:T(128)S(1)} %copy-done.63, ...), custom_call_target="tpu_custom_call" | custom-call | flops 1744830464 | bytes 8912896 | tf_op jit(solution)/shard_map/mix_backward/pallas_call | solution.py:353
  266.9 5.0 %collective-permute-done.55.refs_1_ = bf16[128,1024]{1,0:T(8,128)(2,1)S(1)} collective-permute-done((bf16[128,1024]{1,0:T(8,128)(2,1)S(1)}, bf16[128,1024]{1,0:T(8,128)(2,1)S(1)}, u32[]{:S(2)}, u32[]{:S(2)}) %collective-permute-start.55) | collective-permute-done | bytes 262176 | tf_op jit(solution)/shard_map/ppermute | solution.py:1067
  278.9 6.0 %feed_backward.3 = (f32[128,1024]{1,0:T(8,128)S(1)}, bf16[128,1024]{1,0:T(8,128)(2,1)S(1)}, bf16[128,1024]{1,0:T(8,128)(2,1)S(1)}, bf16[128,1024]{1,0:T(8,128)(2...) custom-call(s32[3]{0:T(128)S(1)} %copy-done.63, ...), custom_call_target="tpu_custom_call" | custom-call | flops 3690987520 | bytes 12779520 | tf_op jit(solution)/shard_map/feed_backward/pallas_call | solution.py:500
  285.0 6.5 %collective-permute-done.59.refs_3_ = bf16[2176,128]{1,0:T(8,128)(2,1)S(1)} collective-permute-done((bf16[2176,128]{1,0:T(8,128)(2,1)S(1)}, bf16[2176,128]{1,0:T(8,128)(2,1)S(1)}, u32[]{:S(2)}, u32[]{:S(2)}) %collective-permute-start.59) | collective-permute-done | bytes 557088 | tf_op jit(solution)/shard_map/ppermute | solution.py:1200
  319.0 5.7 %collective-permute-done.69.refs_1_ = bf16[128,1024]{1,0:T(8,128)(2,1)S(1)} collective-permute-done((bf16[128,1024]{1,0:T(8,128)(2,1)S(1)}, bf16[128,1024]{1,0:T(8,128)(2,1)S(1)}, u32[]{:S(2)}, u32[]{:S(2)}) %collective-permute-start.69) | collective-permute-done | bytes 262176 | tf_op jit(solution)/shard_map/ppermute | solution.py:1067
  324.6 5.2 %collective-permute-done.68.refs_2_ = bf16[128,1024]{1,0:T(8,128)(2,1)S(1)} collective-permute-done((bf16[128,1024]{1,0:T(8,128)(2,1)S(1)}, bf16[128,1024]{1,0:T(8,128)(2,1)S(1)}, u32[]{:S(2)}, u32[]{:S(2)}) %collective-permute-start.68) | collective-permute-done | bytes 262176 | tf_op jit(solution)/shard_map/ppermute | solution.py:1067
  337.7 7.3 %mix_backward.3 = (f32[128,1024]{1,0:T(8,128)S(1)}, bf16[128,1024]{1,0:T(8,128)(2,1)S(1)}, bf16[128,1024]{1,0:T(8,128)(2,1)S(1)}, bf16[128,1024]{1,0:T(8,128)(2,...) custom-call(s32[3]{0:T(128)S(1)} %copy-done.63, ...), custom_call_target="tpu_custom_call" | custom-call | flops 1744830464 | bytes 8912896 | tf_op jit(solution)/shard_map/mix_backward/pallas_call | solution.py:353
  345.9 6.9 %collective-permute-done.73.refs_2_ = bf16[1472,128]{1,0:T(8,128)(2,1)S(1)} collective-permute-done((bf16[1472,128]{1,0:T(8,128)(2,1)S(1)}, bf16[1472,128]{1,0:T(8,128)(2,1)S(1)}, u32[]{:S(2)}, u32[]{:S(2)}) %collective-permute-start.73) | collective-permute-done | bytes 376864 | tf_op jit(solution)/shard_map/ppermute | solution.py:1067
  373.6 7.4 %collective-permute-done.83.refs_1_ = bf16[2176,128]{1,0:T(8,128)(2,1)S(1)} collective-permute-done((bf16[2176,128]{1,0:T(8,128)(2,1)S(1)}, bf16[2176,128]{1,0:T(8,128)(2,1)S(1)}, u32[]{:S(2)}, u32[]{:S(2)}) %collective-permute-start.83) | collective-permute-done | bytes 557088 | tf_op jit(solution)/shard_map/ppermute | solution.py:1200
  444.4 15.3 %collective-permute-done.109 = bf16[2176,128]{1,0:T(8,128)(2,1)S(1)} collective-permute-done((bf16[2176,128]{1,0:T(8,128)(2,1)S(1)}, bf16[2176,128]{1,0:T(8,128)(2,1)S(1)}, u32[]{:S(2)}, u32[]{:S(2)}) %collective-permute-start.109) | collective-permute-done | bytes 557088 | tf_op jit(solution)/shard_map/ppermute | solution.py:1200
  463.4 5.1 %unpack_feed.1 = (f32[256,5632]{1,0:T(8,128)}, f32[704,1024]{1,0:T(8,128)}, f32[1,256]{1,0:T(1,128)}) custom-call(s32[4]{0:T(128)S(1)} %pad_add_fusion.1.place_ref, bf16[8464,128]{1,0:T(8,128)(2,1)S(1)} %collect_feed.3.refs_0_, bf16[8464,128]{1,0:T(8,128)(2,1)S(1)} %collective-permute-done.105.refs_1_, bf16[8464,128]{1,0:T(8,128)(2,1)S(1)} %collect_feed.2.refs_2_, ...), custom_call_target="tpu_custom_call" | custom-call | bytes 12985344 | tf_op jit(solution)/shard_map/unpack_feed/pallas_call | solution.py:1002
  471.6 12.7 %collective-permute-done.110 = bf16[2,128,1024]{2,1,0:T(8,128)(2,1)S(1)} collective-permute-done((bf16[2,128,1024]{2,1,0:T(8,128)(2,1)S(1)}, bf16[2,128,1024]{2,1,0:T(8,128)(2,1)S(1)}, u32[]{:S(2)}, u32[]{:S(2)}) %collective-permute-start.110) | collective-permute-done | bytes 524320 | tf_op jit(solution)/shard_map/ppermute | solution.py:1119
  (430 shorter events, 304.0 us)
Async XLA Ops:
  19.1 29.5 %collective-permute-start.6 = (bf16[256,768]{1,0:T(8,128)(2,1)S(1)}, bf16[256,768]{1,0:T(8,128)(2,1)S(1)}, u32[]{:S(2)}, u32[]{:S(2)}) collective-permute-start(bf16[256,768]{1,0:T(8,128)(2,1)S(1)} %get-tuple-element.436), channel_id=1, source_target_pairs={{0,1},{1,0},{2,3},{3,2},{4,5},{5,4},{6,7},{7,6},{8,9},{9,8},{10,11... | collective-permute-start | bytes 1179656 | tf_op jit(solution)/shard_map/ppermute | solution.py:1067
  21.0 27.8 %collective-permute-start.7 = (bf16[256,768]{1,0:T(8,128)(2,1)S(1)}, bf16[256,768]{1,0:T(8,128)(2,1)S(1)}, u32[]{:S(2)}, u32[]{:S(2)}) collective-permute-start(bf16[256,768]{1,0:T(8,128)(2,1)S(1)} %get-tuple-element.437), channel_id=1, source_target_pairs={{0,2},{1,3},{2,0},{3,1},{4,6},{5,7},{6,4},{7,5},{8,10},{9,11},{10,... | collective-permute-start | bytes 1179656 | tf_op jit(solution)/shard_map/ppermute | solution.py:1067
  23.0 25.8 %collective-permute-start.8 = (bf16[256,768]{1,0:T(8,128)(2,1)S(1)}, bf16[256,768]{1,0:T(8,128)(2,1)S(1)}, u32[]{:S(2)}, u32[]{:S(2)}) collective-permute-start(bf16[256,768]{1,0:T(8,128)(2,1)S(1)} %get-tuple-element.438), channel_id=1, source_target_pairs={{0,3},{1,2},{2,1},{3,0},{4,7},{5,6},{6,5},{7,4},{8,11},{9,10},{10,... | collective-permute-start | bytes 1179656 | tf_op jit(solution)/shard_map/ppermute | solution.py:1067
  25.7 22.9 %collective-permute-start.2 = (bf16[160,1024]{1,0:T(8,128)(2,1)S(1)}, bf16[160,1024]{1,0:T(8,128)(2,1)S(1)}, u32[]{:S(2)}, u32[]{:S(2)}) collective-permute-start(bf16[160,1024]{1,0:T(8,128)(2,1)S(1)} %beside.1.refs_0_), channel_id=1, source_target_pairs={{0,3},{1,2},{2,1},{3,0},{4,7},{5,6},{6,5},{7,4},{8,11},{9,10},{10,... | collective-permute-start | bytes 983048 | tf_op jit(solution)/shard_map/ppermute | solution.py:1067
  28.1 28.0 %collective-permute-start.5 = (bf16[704,1024]{1,0:T(8,128)(2,1)}, bf16[704,1024]{1,0:T(8,128)(2,1)S(1)}, u32[]{:S(2)}, u32[]{:S(2)}) collective-permute-start(bf16[704,1024]{1,0:T(8,128)(2,1)} %bitcast.36), channel_id=1, source_target_pairs={{0,16},{16,0},{1,17},{17,1},{2,18},{18,2},{3,19},{19,3},{4,20},{20... | collective-permute-start | bytes 4325384 | tf_op jit(solution)/shard_map/ppermute | solution.py:1067
  50.1 24.9 %collective-permute-start.11 = (bf16[256,1408]{1,0:T(8,128)(2,1)}, bf16[256,1408]{1,0:T(8,128)(2,1)}, u32[]{:S(2)}, u32[]{:S(2)}) collective-permute-start(bf16[256,1408]{1,0:T(8,128)(2,1)} %get-tuple-element.455), channel_id=1, source_target_pairs={{0,1},{1,0},{2,3},{3,2},{4,5},{5,4},{6,7},{7,6},{8,9},{9,8},{10,11... | collective-permute-start | bytes 2162696 | tf_op jit(solution)/shard_map/ppermute | solution.py:1067
  51.6 37.6 %collective-permute-start.16 = (bf16[256,1408]{1,0:T(8,128)(2,1)}, bf16[256,1408]{1,0:T(8,128)(2,1)}, u32[]{:S(2)}, u32[]{:S(2)}) collective-permute-start(bf16[256,1408]{1,0:T(8,128)(2,1)} %get-tuple-element.464), channel_id=1, source_target_pairs={{0,2},{1,3},{2,0},{3,1},{4,6},{5,7},{6,4},{7,5},{8,10},{9,11},{10,... | collective-permute-start | bytes 2162696 | tf_op jit(solution)/shard_map/ppermute | solution.py:1067
  54.5 34.7 %collective-permute-start.17 = (bf16[256,1408]{1,0:T(8,128)(2,1)}, bf16[256,1408]{1,0:T(8,128)(2,1)}, u32[]{:S(2)}, u32[]{:S(2)}) collective-permute-start(bf16[256,1408]{1,0:T(8,128)(2,1)} %get-tuple-element.465), channel_id=1, source_target_pairs={{0,3},{1,2},{2,1},{3,0},{4,7},{5,6},{6,5},{7,4},{8,11},{9,10},{10,... | collective-permute-start | bytes 2162696 | tf_op jit(solution)/shard_map/ppermute | solution.py:1067
  57.2 17.6 %collective-permute-start.12 = (bf16[128,1024]{1,0:T(8,128)(2,1)}, bf16[128,1024]{1,0:T(8,128)(2,1)}, u32[]{:S(2)}, u32[]{:S(2)}) collective-permute-start(bf16[128,1024]{1,0:T(8,128)(2,1)} %dynamic-slice_bitcast_fusion), channel_id=1, source_target_pairs={{0,0},{1,4},{2,8},{3,12},{4,1},{5,5},{6,9},{7,13},{8,2},{9,6},{10,... | collective-permute-start | bytes 786440 | tf_op jit(solution)/shard_map/ppermute | solution.py:1119
  75.0 21.0 %collective-permute-start.13 = (bf16[128,1024]{1,0:T(8,128)(2,1)S(1)}, bf16[128,1024]{1,0:T(8,128)(2,1)S(1)}, u32[]{:S(2)}, u32[]{:S(2)}) collective-permute-start(bf16[128,1024]{1,0:T(8,128)(2,1)S(1)} %get-tuple-element.459), channel_id=1, source_target_pairs={{0,1},{1,0},{2,3},{3,2},{4,5},{5,4},{6,7},{7,6},{8,9},{9,8},{10,11... | collective-permute-start | bytes 786440 | tf_op jit(solution)/shard_map/ppermute | solution.py:1067
  77.2 22.3 %collective-permute-start.14 = (bf16[128,1024]{1,0:T(8,128)(2,1)S(1)}, bf16[128,1024]{1,0:T(8,128)(2,1)S(1)}, u32[]{:S(2)}, u32[]{:S(2)}) collective-permute-start(bf16[128,1024]{1,0:T(8,128)(2,1)S(1)} %get-tuple-element.460), channel_id=1, source_target_pairs={{0,2},{1,3},{2,0},{3,1},{4,6},{5,7},{6,4},{7,5},{8,10},{9,11},{10,... | collective-permute-start | bytes 786440 | tf_op jit(solution)/shard_map/ppermute | solution.py:1067
  79.8 19.6 %collective-permute-start.15 = (bf16[128,1024]{1,0:T(8,128)(2,1)S(1)}, bf16[128,1024]{1,0:T(8,128)(2,1)S(1)}, u32[]{:S(2)}, u32[]{:S(2)}) collective-permute-start(bf16[128,1024]{1,0:T(8,128)(2,1)S(1)} %get-tuple-element.461), channel_id=1, source_target_pairs={{0,3},{1,2},{2,1},{3,0},{4,7},{5,6},{6,5},{7,4},{8,11},{9,10},{10,... | collective-permute-start | bytes 786440 | tf_op jit(solution)/shard_map/ppermute | solution.py:1067
  101.4 17.6 %collective-permute-start.21 = (bf16[1024,1408]{1,0:T(8,128)(2,1)S(1)}, bf16[1024,1408]{1,0:T(8,128)(2,1)S(1)}, u32[]{:S(2)}, u32[]{:S(2)}) collective-permute-start(bf16[1024,1408]{1,0:T(8,128)(2,1)S(1)} %assemble.3.refs_4_.refs_9_.refs_6_), channel_id=1, source_target_pairs={{0,16},{16,0},{1,17},{17,1},{2,18},{18,2},{3,19},{19,3},{4,20},{20... | collective-permute-start | bytes 8650760 | tf_op jit(solution)/shard_map/ppermute | solution.py:1067
  140.7 20.0 %collective-permute-start.30 = (bf16[128,1024]{1,0:T(8,128)(2,1)}, bf16[128,1024]{1,0:T(8,128)(2,1)S(1)}, u32[]{:S(2)}, u32[]{:S(2)}) collective-permute-start(bf16[128,1024]{1,0:T(8,128)(2,1)} %collective-permute-done.12.refs_0_.refs_6_), channel_id=1, source_target_pairs={{0,1},{1,0},{2,3},{3,2},{4,5},{5,4},{6,7},{7,6},{8,9},{9,8},{10,11... | collective-permute-start | bytes 786440 | tf_op jit(solution)/shard_map/ppermute | solution.py:1067
  142.2 19.8 %collective-permute-start.29 = (bf16[128,1024]{1,0:T(8,128)(2,1)}, bf16[128,1024]{1,0:T(8,128)(2,1)S(1)}, u32[]{:S(2)}, u32[]{:S(2)}) collective-permute-start(bf16[128,1024]{1,0:T(8,128)(2,1)} %collective-permute-done.12.refs_0_.refs_6_), channel_id=1, source_target_pairs={{0,2},{1,3},{2,0},{3,1},{4,6},{5,7},{6,4},{7,5},{8,10},{9,11},{10,... | collective-permute-start | bytes 786440 | tf_op jit(solution)/shard_map/ppermute | solution.py:1067
  291.9 18.6 %collective-permute-start.64 = (bf16[2176,128]{1,0:T(8,128)(2,1)S(1)}, bf16[2176,128]{1,0:T(8,128)(2,1)S(1)}, u32[]{:S(2)}, u32[]{:S(2)}) collective-permute-start(bf16[2176,128]{1,0:T(8,128)(2,1)S(1)} %fusion.2.refs_4_), channel_id=1, source_target_pairs={{0,4},{12,8},{4,0},{8,12},{1,5},{13,9},{5,1},{9,13},{2,6},{14,10},... | collective-permute-start | bytes 1671176 | tf_op jit(solution)/shard_map/ppermute | solution.py:1200
  311.1 18.7 %collective-permute-start.70 = (bf16[2176,128]{1,0:T(8,128)(2,1)S(1)}, bf16[2176,128]{1,0:T(8,128)(2,1)S(1)}, u32[]{:S(2)}, u32[]{:S(2)}) collective-permute-start(bf16[2176,128]{1,0:T(8,128)(2,1)S(1)} %fusion.3.refs_6_), channel_id=1, source_target_pairs={{0,4},{12,8},{4,0},{8,12},{1,5},{13,9},{5,1},{9,13},{2,6},{14,10},... | collective-permute-start | bytes 1671176 | tf_op jit(solution)/shard_map/ppermute | solution.py:1200
  330.4 22.5 %collective-permute-start.75 = (bf16[2176,128]{1,0:T(8,128)(2,1)S(1)}, bf16[2176,128]{1,0:T(8,128)(2,1)S(1)}, u32[]{:S(2)}, u32[]{:S(2)}) collective-permute-start(bf16[2176,128]{1,0:T(8,128)(2,1)S(1)} %fusion.4.refs_0_), channel_id=1, source_target_pairs={{0,4},{12,8},{4,0},{8,12},{1,5},{13,9},{5,1},{9,13},{2,6},{14,10},... | collective-permute-start | bytes 1671176 | tf_op jit(solution)/shard_map/ppermute | solution.py:1200
  332.8 20.1 %collective-permute-start.76 = (bf16[2176,128]{1,0:T(8,128)(2,1)S(1)}, bf16[2176,128]{1,0:T(8,128)(2,1)S(1)}, u32[]{:S(2)}, u32[]{:S(2)}) collective-permute-start(bf16[2176,128]{1,0:T(8,128)(2,1)S(1)} %add_convert_fusion.16), channel_id=1, source_target_pairs={{4,8},{8,4},{5,9},{9,5},{6,10},{10,6},{7,11},{11,7},{20,24},{24,20... | collective-permute-start | bytes 1671176 | tf_op jit(solution)/shard_map/ppermute | solution.py:1202
  335.5 17.4 %collective-permute-start.73 = (bf16[1472,128]{1,0:T(8,128)(2,1)S(1)}, bf16[1472,128]{1,0:T(8,128)(2,1)S(1)}, u32[]{:S(2)}, u32[]{:S(2)}) collective-permute-start(bf16[1472,128]{1,0:T(8,128)(2,1)S(1)} %get-tuple-element.677), channel_id=1, source_target_pairs={{0,2},{1,3},{2,0},{3,1},{4,6},{5,7},{6,4},{7,5},{8,10},{9,11},{10,... | collective-permute-start | bytes 1130504 | tf_op jit(solution)/shard_map/ppermute | solution.py:1067
  436.8 22.8 %collective-permute-start.105 = (bf16[8464,128]{1,0:T(8,128)(2,1)S(1)}, bf16[8464,128]{1,0:T(8,128)(2,1)S(1)}, u32[]{:S(2)}, u32[]{:S(2)}) collective-permute-start(bf16[8464,128]{1,0:T(8,128)(2,1)S(1)} %collect_feed.3.refs_0_), channel_id=1, source_target_pairs={{16,0},{17,1},{18,2},{19,3},{20,4},{21,5},{22,6},{23,7},{24,8},{25... | collective-permute-start | bytes 6500360 | tf_op jit(solution)/shard_map/ppermute | solution.py:1253
  438.3 21.4 %collective-permute-start.108 = (bf16[4352,128]{1,0:T(8,128)(2,1)S(1)}, bf16[4352,128]{1,0:T(8,128)(2,1)S(1)}, u32[]{:S(2)}, u32[]{:S(2)}) collective-permute-start(bf16[4352,128]{1,0:T(8,128)(2,1)S(1)} %collect_mix.3.refs_4_), channel_id=1, source_target_pairs={{0,16},{1,17},{2,18},{3,19},{4,20},{5,21},{6,22},{7,23},{8,24},{9,... | collective-permute-start | bytes 3342344 | tf_op jit(solution)/shard_map/ppermute | solution.py:1253
  441.6 18.0 %collective-permute-start.109 = (bf16[2176,128]{1,0:T(8,128)(2,1)S(1)}, bf16[2176,128]{1,0:T(8,128)(2,1)S(1)}, u32[]{:S(2)}, u32[]{:S(2)}) collective-permute-start(bf16[2176,128]{1,0:T(8,128)(2,1)S(1)} %add_convert_fusion), channel_id=1, source_target_pairs={{4,0},{8,12},{5,1},{9,13},{6,2},{10,14},{7,3},{11,15},{20,16},{24,... | collective-permute-start | bytes 1671176 | tf_op jit(solution)/shard_map/ppermute | solution.py:1200
  461.1 23.2 %collective-permute-start.110 = (bf16[2,128,1024]{2,1,0:T(8,128)(2,1)S(1)}, bf16[2,128,1024]{2,1,0:T(8,128)(2,1)S(1)}, u32[]{:S(2)}, u32[]{:S(2)}) collective-permute-start(bf16[2,128,1024]{2,1,0:T(8,128)(2,1)S(1)} %pad_maximum_fusion), channel_id=1, source_target_pairs={{0,0},{1,4},{2,8},{3,12},{4,1},{5,5},{6,9},{7,13},{8,2},{9,6},{10,... | collective-permute-start | bytes 1572872 | tf_op jit(solution)/shard_map/ppermute | solution.py:1119
  (166 other events, 2286.5 us)

commit v6 on v5

--- a/solution.py
+++ b/solution.py
@@ -1208,7 +1208,7 @@
     def step(*held, more=None):
         landed, crossed = line["flight"]
         waiting = [v for v in (landed, crossed) if v is not None]
-        held, waiting = tie(held, waiting)
+        waiting, held = tie(waiting, held)
         if landed is not None:
             landed = waiting.pop(0)
         if crossed is not None:

time: 495 us -> 495 us (level)
  no operation moved by 1% of the time
where the time goes in v6:
time: 495 us; the launch traced here: 486 us
  waiting for transfers between devices  215 us (43%)
  starting transfers between devices  146 us (29%)
  Pallas kernels  88.9 us (18%)
  local copies, waits for them, and re-layouts  25.6 us (5%)
  other arithmetic  7.29 us (1%)
    ppermute x78, waiting for transfers between devices, exchange(): return lax.ppermute(value, axis, [(i, i ^ distance) for i in range(count)])  169 us
    ppermute x78, starting transfers between devices, exchange(): return lax.ppermute(value, axis, [(i, i ^ distance) for i in range(count)])  85.8 us
    ppermute x14, starting transfers between devices, go(): flight[0] = lax.ppermute(sent, 'ctx', route)  35 us
    ppermute x14, waiting for transfers between devices, go(): flight[0] = lax.ppermute(sent, 'ctx', route)  29.3 us
    unnamed x158, local copies, waits for them, and re-layouts  21.8 us
    ppermute x3, waiting for transfers between devices, turn_plane(): return lax.ppermute(value, ('section', 'ctx', 'fsdp'), pairs)  16.6 us
    pallas_call x2, Pallas kernels, feed_backward(): call(body, outs, specs, scratch, flops, moved, 'feed_backward')  16 us
    pallas_call x2, Pallas kernels, mix_backward(): call(body, outs, specs, scratch, flops, moved, 'mix_backward')  14.4 us
  transfers between devices with their start and end apart: 112, of which 54 were waited for; matrix products, arithmetic and copies ran while one was open for 1% of the time, Pallas kernels for 15%

profile of v6, /device:TPU:2, one launch (start us, length us, event | category | flops | bytes accessed | tf_op | source)
XLA Modules:
  0.0 486.0 jit_solution(12873952854655287838)
XLA Ops:
  32.8 15.8 %collective-permute-done.2.refs_3_ = bf16[160,1024]{1,0:T(8,128)(2,1)S(1)} collective-permute-done((bf16[160,1024]{1,0:T(8,128)(2,1)S(1)}, bf16[160,1024]{1,0:T(8,128)(2,1)S(1)}, u32[]{:S(2)}, u32[]{:S(2)}) %collective-permute-start.2) | collective-permute-done | bytes 327712 | tf_op jit(solution)/shard_map/ppermute | solution.py:1067
  67.1 6.7 %mix_forward.2 = (f32[128,1024]{1,0:T(8,128)S(1)}, bf16[128,1024]{1,0:T(8,128)(2,1)S(1)}, bf16[128,1024]{1,0:T(8,128)(2,1)S(1)}, bf16[128,1024]{1,0:T(8,128)(2,1...) custom-call(s32[3]{0:T(128)S(1)} %pad_add_fusion.1.place_ref, ...), custom_call_target="tpu_custom_call" | custom-call | flops 1342177280 | bytes 4718592 | tf_op jit(solution)/shard_map/mix_forward/pallas_call | solution.py:260
  81.2 8.0 %collective-permute-done.16.refs_2_ = bf16[256,1408]{1,0:T(8,128)(2,1)} collective-permute-done((bf16[256,1408]{1,0:T(8,128)(2,1)}, bf16[256,1408]{1,0:T(8,128)(2,1)}, u32[]{:S(2)}, u32[]{:S(2)}) %collective-permute-start.16) | collective-permute-done | bytes 720928 | tf_op jit(solution)/shard_map/ppermute | solution.py:1067
  89.2 6.8 %collective-permute-done.13.refs_1_ = bf16[128,1024]{1,0:T(8,128)(2,1)S(1)} collective-permute-done((bf16[128,1024]{1,0:T(8,128)(2,1)S(1)}, bf16[128,1024]{1,0:T(8,128)(2,1)S(1)}, u32[]{:S(2)}, u32[]{:S(2)}) %collective-permute-start.13) | collective-permute-done | bytes 262176 | tf_op jit(solution)/shard_map/ppermute | solution.py:1067
  106.4 5.6 %collective-permute-done.20.refs_1_ = bf16[128,1024]{1,0:T(8,128)(2,1)S(1)} collective-permute-done((bf16[128,1024]{1,0:T(8,128)(2,1)S(1)}, bf16[128,1024]{1,0:T(8,128)(2,1)S(1)}, u32[]{:S(2)}, u32[]{:S(2)}) %collective-permute-start.20) | collective-permute-done | bytes 262176 | tf_op jit(solution)/shard_map/ppermute | solution.py:1067
  112.1 6.9 %collective-permute-done.19.refs_2_ = bf16[128,1024]{1,0:T(8,128)(2,1)S(1)} collective-permute-done((bf16[128,1024]{1,0:T(8,128)(2,1)S(1)}, bf16[128,1024]{1,0:T(8,128)(2,1)S(1)}, u32[]{:S(2)}, u32[]{:S(2)}) %collective-permute-start.19) | collective-permute-done | bytes 262176 | tf_op jit(solution)/shard_map/ppermute | solution.py:1067
  127.1 5.8 %collective-permute-done.22.refs_1_ = bf16[128,1024]{1,0:T(8,128)(2,1)S(1)} collective-permute-done((bf16[128,1024]{1,0:T(8,128)(2,1)S(1)}, bf16[128,1024]{1,0:T(8,128)(2,1)S(1)}, u32[]{:S(2)}, u32[]{:S(2)}) %collective-permute-start.22) | collective-permute-done | bytes 262176 | tf_op jit(solution)/shard_map/ppermute | solution.py:1067
  148.0 5.7 %collective-permute-done.26.refs_2_ = bf16[128,1024]{1,0:T(8,128)(2,1)S(1)} collective-permute-done((bf16[128,1024]{1,0:T(8,128)(2,1)S(1)}, bf16[128,1024]{1,0:T(8,128)(2,1)S(1)}, u32[]{:S(2)}, u32[]{:S(2)}) %collective-permute-start.26) | collective-permute-done | bytes 262176 | tf_op jit(solution)/shard_map/ppermute | solution.py:1067
  153.7 7.0 %mix_forward.3 = (f32[128,1024]{1,0:T(8,128)S(1)}, bf16[128,1024]{1,0:T(8,128)(2,1)S(1)}, bf16[128,1024]{1,0:T(8,128)(2,1)S(1)}, bf16[128,1024]{1,0:T(8,128)(2,1...) custom-call(s32[3]{0:T(128)S(1)} %pad_add_fusion.1.place_ref, ...), custom_call_target="tpu_custom_call" | custom-call | flops 1342177280 | bytes 4718592 | tf_op jit(solution)/shard_map/mix_forward/pallas_call | solution.py:260
  185.3 10.0 %feed_backward.2 = (f32[128,1024]{1,0:T(8,128)}, bf16[128,1024]{1,0:T(8,128)(2,1)}, bf16[128,1024]{1,0:T(8,128)(2,1)}, bf16[128,1024]{1,0:T(8,128)(2,1)}, bf16[5...) custom-call(s32[3]{0:T(128)S(1)} %pad_add_fusion.1.place_ref, ...), custom_call_target="tpu_custom_call" | custom-call | flops 3690987520 | bytes 12779520 | tf_op jit(solution)/shard_map/feed_backward/pallas_call | solution.py:500
  214.2 5.6 %collective-permute-done.42.refs_1_ = bf16[128,1024]{1,0:T(8,128)(2,1)S(1)} collective-permute-done((bf16[128,1024]{1,0:T(8,128)(2,1)S(1)}, bf16[128,1024]{1,0:T(8,128)(2,1)S(1)}, u32[]{:S(2)}, u32[]{:S(2)}) %collective-permute-start.42) | collective-permute-done | bytes 262176 | tf_op jit(solution)/shard_map/ppermute | solution.py:1067
  219.9 5.9 %collective-permute-done.41.refs_2_ = bf16[128,1024]{1,0:T(8,128)(2,1)S(1)} collective-permute-done((bf16[128,1024]{1,0:T(8,128)(2,1)S(1)}, bf16[128,1024]{1,0:T(8,128)(2,1)S(1)}, u32[]{:S(2)}, u32[]{:S(2)}) %collective-permute-start.41) | collective-permute-done | bytes 262176 | tf_op jit(solution)/shard_map/ppermute | solution.py:1067
  233.3 7.1 %mix_backward.2 = (f32[128,1024]{1,0:T(8,128)S(1)}, bf16[128,1024]{1,0:T(8,128)(2,1)S(1)}, bf16[128,1024]{1,0:T(8,128)(2,1)S(1)}, bf16[128,1024]{1,0:T(8,128)(2,...) custom-call(s32[3]{0:T(128)S(1)} %copy-done.63, ...), custom_call_target="tpu_custom_call" | custom-call | flops 1744830464 | bytes 8912896 | tf_op jit(solution)/shard_map/mix_backward/pallas_call | solution.py:353
  266.9 5.0 %collective-permute-done.57.refs_1_ = bf16[128,1024]{1,0:T(8,128)(2,1)S(1)} collective-permute-done((bf16[128,1024]{1,0:T(8,128)(2,1)S(1)}, bf16[128,1024]{1,0:T(8,128)(2,1)S(1)}, u32[]{:S(2)}, u32[]{:S(2)}) %collective-permute-start.57) | collective-permute-done | bytes 262176 | tf_op jit(solution)/shard_map/ppermute | solution.py:1067
  278.9 6.0 %feed_backward.3 = (f32[128,1024]{1,0:T(8,128)S(1)}, bf16[128,1024]{1,0:T(8,128)(2,1)S(1)}, bf16[128,1024]{1,0:T(8,128)(2,1)S(1)}, bf16[128,1024]{1,0:T(8,128)(2...) custom-call(s32[3]{0:T(128)S(1)} %copy-done.63, ...), custom_call_target="tpu_custom_call" | custom-call | flops 3690987520 | bytes 12779520 | tf_op jit(solution)/shard_map/feed_backward/pallas_call | solution.py:500
  285.0 6.5 %collective-permute-done.58.refs_3_ = bf16[2176,128]{1,0:T(8,128)(2,1)S(1)} collective-permute-done((bf16[2176,128]{1,0:T(8,128)(2,1)S(1)}, bf16[2176,128]{1,0:T(8,128)(2,1)S(1)}, u32[]{:S(2)}, u32[]{:S(2)}) %collective-permute-start.58) | collective-permute-done | bytes 557088 | tf_op jit(solution)/shard_map/ppermute | solution.py:1200
  319.0 5.7 %collective-permute-done.71.refs_1_ = bf16[128,1024]{1,0:T(8,128)(2,1)S(1)} collective-permute-done((bf16[128,1024]{1,0:T(8,128)(2,1)S(1)}, bf16[128,1024]{1,0:T(8,128)(2,1)S(1)}, u32[]{:S(2)}, u32[]{:S(2)}) %collective-permute-start.71) | collective-permute-done | bytes 262176 | tf_op jit(solution)/shard_map/ppermute | solution.py:1067
  324.6 5.2 %collective-permute-done.70.refs_2_ = bf16[128,1024]{1,0:T(8,128)(2,1)S(1)} collective-permute-done((bf16[128,1024]{1,0:T(8,128)(2,1)S(1)}, bf16[128,1024]{1,0:T(8,128)(2,1)S(1)}, u32[]{:S(2)}, u32[]{:S(2)}) %collective-permute-start.70) | collective-permute-done | bytes 262176 | tf_op jit(solution)/shard_map/ppermute | solution.py:1067
  337.7 7.3 %mix_backward.3 = (f32[128,1024]{1,0:T(8,128)S(1)}, bf16[128,1024]{1,0:T(8,128)(2,1)S(1)}, bf16[128,1024]{1,0:T(8,128)(2,1)S(1)}, bf16[128,1024]{1,0:T(8,128)(2,...) custom-call(s32[3]{0:T(128)S(1)} %copy-done.63, ...), custom_call_target="tpu_custom_call" | custom-call | flops 1744830464 | bytes 8912896 | tf_op jit(solution)/shard_map/mix_backward/pallas_call | solution.py:353
  345.9 6.9 %collective-permute-done.75.refs_2_ = bf16[1472,128]{1,0:T(8,128)(2,1)S(1)} collective-permute-done((bf16[1472,128]{1,0:T(8,128)(2,1)S(1)}, bf16[1472,128]{1,0:T(8,128)(2,1)S(1)}, u32[]{:S(2)}, u32[]{:S(2)}) %collective-permute-start.75) | collective-permute-done | bytes 376864 | tf_op jit(solution)/shard_map/ppermute | solution.py:1067
  373.6 7.4 %collective-permute-done.82.refs_1_ = bf16[2176,128]{1,0:T(8,128)(2,1)S(1)} collective-permute-done((bf16[2176,128]{1,0:T(8,128)(2,1)S(1)}, bf16[2176,128]{1,0:T(8,128)(2,1)S(1)}, u32[]{:S(2)}, u32[]{:S(2)}) %collective-permute-start.82) | collective-permute-done | bytes 557088 | tf_op jit(solution)/shard_map/ppermute | solution.py:1200
  444.4 15.3 %collective-permute-done.105 = bf16[2176,128]{1,0:T(8,128)(2,1)S(1)} collective-permute-done((bf16[2176,128]{1,0:T(8,128)(2,1)S(1)}, bf16[2176,128]{1,0:T(8,128)(2,1)S(1)}, u32[]{:S(2)}, u32[]{:S(2)}) %collective-permute-start.105) | collective-permute-done | bytes 557088 | tf_op jit(solution)/shard_map/ppermute | solution.py:1200
  463.4 5.1 %unpack_feed.1 = (f32[256,5632]{1,0:T(8,128)}, f32[704,1024]{1,0:T(8,128)}, f32[1,256]{1,0:T(1,128)}) custom-call(s32[4]{0:T(128)S(1)} %pad_add_fusion.2.place_ref, bf16[8464,128]{1,0:T(8,128)(2,1)S(1)} %collect_feed.3.refs_0_, bf16[8464,128]{1,0:T(8,128)(2,1)S(1)} %collective-permute-done.106.refs_1_, bf16[8464,128]{1,0:T(8,128)(2,1)S(1)} %collect_feed.2.refs_2_, ...), custom_call_target="tpu_custom_call" | custom-call | bytes 12985344 | tf_op jit(solution)/shard_map/unpack_feed/pallas_call | solution.py:1002
  471.6 12.7 %collective-permute-done.110 = bf16[2,128,1024]{2,1,0:T(8,128)(2,1)S(1)} collective-permute-done((bf16[2,128,1024]{2,1,0:T(8,128)(2,1)S(1)}, bf16[2,128,1024]{2,1,0:T(8,128)(2,1)S(1)}, u32[]{:S(2)}, u32[]{:S(2)}) %collective-permute-start.110) | collective-permute-done | bytes 524320 | tf_op jit(solution)/shard_map/ppermute | solution.py:1119
  (430 shorter events, 304.0 us)
Async XLA Ops:
  19.1 29.5 %collective-permute-start.6 = (bf16[256,768]{1,0:T(8,128)(2,1)S(1)}, bf16[256,768]{1,0:T(8,128)(2,1)S(1)}, u32[]{:S(2)}, u32[]{:S(2)}) collective-permute-start(bf16[256,768]{1,0:T(8,128)(2,1)S(1)} %get-tuple-element.436), channel_id=1, source_target_pairs={{0,1},{1,0},{2,3},{3,2},{4,5},{5,4},{6,7},{7,6},{8,9},{9,8},{10,11... | collective-permute-start | bytes 1179656 | tf_op jit(solution)/shard_map/ppermute | solution.py:1067
  21.0 27.8 %collective-permute-start.7 = (bf16[256,768]{1,0:T(8,128)(2,1)S(1)}, bf16[256,768]{1,0:T(8,128)(2,1)S(1)}, u32[]{:S(2)}, u32[]{:S(2)}) collective-permute-start(bf16[256,768]{1,0:T(8,128)(2,1)S(1)} %get-tuple-element.437), channel_id=1, source_target_pairs={{0,2},{1,3},{2,0},{3,1},{4,6},{5,7},{6,4},{7,5},{8,10},{9,11},{10,... | collective-permute-start | bytes 1179656 | tf_op jit(solution)/shard_map/ppermute | solution.py:1067
  23.0 25.8 %collective-permute-start.8 = (bf16[256,768]{1,0:T(8,128)(2,1)S(1)}, bf16[256,768]{1,0:T(8,128)(2,1)S(1)}, u32[]{:S(2)}, u32[]{:S(2)}) collective-permute-start(bf16[256,768]{1,0:T(8,128)(2,1)S(1)} %get-tuple-element.438), channel_id=1, source_target_pairs={{0,3},{1,2},{2,1},{3,0},{4,7},{5,6},{6,5},{7,4},{8,11},{9,10},{10,... | collective-permute-start | bytes 1179656 | tf_op jit(solution)/shard_map/ppermute | solution.py:1067
  25.7 22.9 %collective-permute-start.2 = (bf16[160,1024]{1,0:T(8,128)(2,1)S(1)}, bf16[160,1024]{1,0:T(8,128)(2,1)S(1)}, u32[]{:S(2)}, u32[]{:S(2)}) collective-permute-start(bf16[160,1024]{1,0:T(8,128)(2,1)S(1)} %beside.1.refs_0_), channel_id=1, source_target_pairs={{0,3},{1,2},{2,1},{3,0},{4,7},{5,6},{6,5},{7,4},{8,11},{9,10},{10,... | collective-permute-start | bytes 983048 | tf_op jit(solution)/shard_map/ppermute | solution.py:1067
  28.1 28.0 %collective-permute-start.5 = (bf16[704,1024]{1,0:T(8,128)(2,1)}, bf16[704,1024]{1,0:T(8,128)(2,1)S(1)}, u32[]{:S(2)}, u32[]{:S(2)}) collective-permute-start(bf16[704,1024]{1,0:T(8,128)(2,1)} %bitcast.36), channel_id=1, source_target_pairs={{0,16},{16,0},{1,17},{17,1},{2,18},{18,2},{3,19},{19,3},{4,20},{20... | collective-permute-start | bytes 4325384 | tf_op jit(solution)/shard_map/ppermute | solution.py:1067
  50.1 24.9 %collective-permute-start.11 = (bf16[256,1408]{1,0:T(8,128)(2,1)}, bf16[256,1408]{1,0:T(8,128)(2,1)}, u32[]{:S(2)}, u32[]{:S(2)}) collective-permute-start(bf16[256,1408]{1,0:T(8,128)(2,1)} %get-tuple-element.455), channel_id=1, source_target_pairs={{0,1},{1,0},{2,3},{3,2},{4,5},{5,4},{6,7},{7,6},{8,9},{9,8},{10,11... | collective-permute-start | bytes 2162696 | tf_op jit(solution)/shard_map/ppermute | solution.py:1067
  51.6 37.6 %collective-permute-start.16 = (bf16[256,1408]{1,0:T(8,128)(2,1)}, bf16[256,1408]{1,0:T(8,128)(2,1)}, u32[]{:S(2)}, u32[]{:S(2)}) collective-permute-start(bf16[256,1408]{1,0:T(8,128)(2,1)} %get-tuple-element.464), channel_id=1, source_target_pairs={{0,2},{1,3},{2,0},{3,1},{4,6},{5,7},{6,4},{7,5},{8,10},{9,11},{10,... | collective-permute-start | bytes 2162696 | tf_op jit(solution)/shard_map/ppermute | solution.py:1067
  54.5 34.7 %collective-permute-start.17 = (bf16[256,1408]{1,0:T(8,128)(2,1)}, bf16[256,1408]{1,0:T(8,128)(2,1)}, u32[]{:S(2)}, u32[]{:S(2)}) collective-permute-start(bf16[256,1408]{1,0:T(8,128)(2,1)} %get-tuple-element.465), channel_id=1, source_target_pairs={{0,3},{1,2},{2,1},{3,0},{4,7},{5,6},{6,5},{7,4},{8,11},{9,10},{10,... | collective-permute-start | bytes 2162696 | tf_op jit(solution)/shard_map/ppermute | solution.py:1067
  57.2 17.6 %collective-permute-start.12 = (bf16[128,1024]{1,0:T(8,128)(2,1)}, bf16[128,1024]{1,0:T(8,128)(2,1)}, u32[]{:S(2)}, u32[]{:S(2)}) collective-permute-start(bf16[128,1024]{1,0:T(8,128)(2,1)} %dynamic-slice_bitcast_fusion), channel_id=1, source_target_pairs={{0,0},{1,4},{2,8},{3,12},{4,1},{5,5},{6,9},{7,13},{8,2},{9,6},{10,... | collective-permute-start | bytes 786440 | tf_op jit(solution)/shard_map/ppermute | solution.py:1119
  75.0 21.0 %collective-permute-start.13 = (bf16[128,1024]{1,0:T(8,128)(2,1)S(1)}, bf16[128,1024]{1,0:T(8,128)(2,1)S(1)}, u32[]{:S(2)}, u32[]{:S(2)}) collective-permute-start(bf16[128,1024]{1,0:T(8,128)(2,1)S(1)} %get-tuple-element.459), channel_id=1, source_target_pairs={{0,1},{1,0},{2,3},{3,2},{4,5},{5,4},{6,7},{7,6},{8,9},{9,8},{10,11... | collective-permute-start | bytes 786440 | tf_op jit(solution)/shard_map/ppermute | solution.py:1067
  77.2 22.3 %collective-permute-start.14 = (bf16[128,1024]{1,0:T(8,128)(2,1)S(1)}, bf16[128,1024]{1,0:T(8,128)(2,1)S(1)}, u32[]{:S(2)}, u32[]{:S(2)}) collective-permute-start(bf16[128,1024]{1,0:T(8,128)(2,1)S(1)} %get-tuple-element.460), channel_id=1, source_target_pairs={{0,2},{1,3},{2,0},{3,1},{4,6},{5,7},{6,4},{7,5},{8,10},{9,11},{10,... | collective-permute-start | bytes 786440 | tf_op jit(solution)/shard_map/ppermute | solution.py:1067
  79.8 19.6 %collective-permute-start.15 = (bf16[128,1024]{1,0:T(8,128)(2,1)S(1)}, bf16[128,1024]{1,0:T(8,128)(2,1)S(1)}, u32[]{:S(2)}, u32[]{:S(2)}) collective-permute-start(bf16[128,1024]{1,0:T(8,128)(2,1)S(1)} %get-tuple-element.461), channel_id=1, source_target_pairs={{0,3},{1,2},{2,1},{3,0},{4,7},{5,6},{6,5},{7,4},{8,11},{9,10},{10,... | collective-permute-start | bytes 786440 | tf_op jit(solution)/shard_map/ppermute | solution.py:1067
  101.4 17.6 %collective-permute-start.21 = (bf16[1024,1408]{1,0:T(8,128)(2,1)S(1)}, bf16[1024,1408]{1,0:T(8,128)(2,1)S(1)}, u32[]{:S(2)}, u32[]{:S(2)}) collective-permute-start(bf16[1024,1408]{1,0:T(8,128)(2,1)S(1)} %assemble.3.refs_4_.refs_9_.refs_6_), channel_id=1, source_target_pairs={{0,16},{16,0},{1,17},{17,1},{2,18},{18,2},{3,19},{19,3},{4,20},{20... | collective-permute-start | bytes 8650760 | tf_op jit(solution)/shard_map/ppermute | solution.py:1067
  140.7 20.0 %collective-permute-start.30 = (bf16[128,1024]{1,0:T(8,128)(2,1)}, bf16[128,1024]{1,0:T(8,128)(2,1)S(1)}, u32[]{:S(2)}, u32[]{:S(2)}) collective-permute-start(bf16[128,1024]{1,0:T(8,128)(2,1)} %collective-permute-done.12.refs_0_.refs_6_), channel_id=1, source_target_pairs={{0,1},{1,0},{2,3},{3,2},{4,5},{5,4},{6,7},{7,6},{8,9},{9,8},{10,11... | collective-permute-start | bytes 786440 | tf_op jit(solution)/shard_map/ppermute | solution.py:1067
  142.2 19.8 %collective-permute-start.29 = (bf16[128,1024]{1,0:T(8,128)(2,1)}, bf16[128,1024]{1,0:T(8,128)(2,1)S(1)}, u32[]{:S(2)}, u32[]{:S(2)}) collective-permute-start(bf16[128,1024]{1,0:T(8,128)(2,1)} %collective-permute-done.12.refs_0_.refs_6_), channel_id=1, source_target_pairs={{0,2},{1,3},{2,0},{3,1},{4,6},{5,7},{6,4},{7,5},{8,10},{9,11},{10,... | collective-permute-start | bytes 786440 | tf_op jit(solution)/shard_map/ppermute | solution.py:1067
  291.9 18.6 %collective-permute-start.61 = (bf16[2176,128]{1,0:T(8,128)(2,1)S(1)}, bf16[2176,128]{1,0:T(8,128)(2,1)S(1)}, u32[]{:S(2)}, u32[]{:S(2)}) collective-permute-start(bf16[2176,128]{1,0:T(8,128)(2,1)S(1)} %fusion.2.refs_4_), channel_id=1, source_target_pairs={{0,4},{12,8},{4,0},{8,12},{1,5},{13,9},{5,1},{9,13},{2,6},{14,10},... | collective-permute-start | bytes 1671176 | tf_op jit(solution)/shard_map/ppermute | solution.py:1200
  311.1 18.7 %collective-permute-start.66 = (bf16[2176,128]{1,0:T(8,128)(2,1)S(1)}, bf16[2176,128]{1,0:T(8,128)(2,1)S(1)}, u32[]{:S(2)}, u32[]{:S(2)}) collective-permute-start(bf16[2176,128]{1,0:T(8,128)(2,1)S(1)} %fusion.3.refs_6_), channel_id=1, source_target_pairs={{0,4},{12,8},{4,0},{8,12},{1,5},{13,9},{5,1},{9,13},{2,6},{14,10},... | collective-permute-start | bytes 1671176 | tf_op jit(solution)/shard_map/ppermute | solution.py:1200
  330.4 22.5 %collective-permute-start.72 = (bf16[2176,128]{1,0:T(8,128)(2,1)S(1)}, bf16[2176,128]{1,0:T(8,128)(2,1)S(1)}, u32[]{:S(2)}, u32[]{:S(2)}) collective-permute-start(bf16[2176,128]{1,0:T(8,128)(2,1)S(1)} %fusion.4.refs_0_), channel_id=1, source_target_pairs={{0,4},{12,8},{4,0},{8,12},{1,5},{13,9},{5,1},{9,13},{2,6},{14,10},... | collective-permute-start | bytes 1671176 | tf_op jit(solution)/shard_map/ppermute | solution.py:1200
  332.8 20.1 %collective-permute-start.73 = (bf16[2176,128]{1,0:T(8,128)(2,1)S(1)}, bf16[2176,128]{1,0:T(8,128)(2,1)S(1)}, u32[]{:S(2)}, u32[]{:S(2)}) collective-permute-start(bf16[2176,128]{1,0:T(8,128)(2,1)S(1)} %add_convert_fusion.16), channel_id=1, source_target_pairs={{4,8},{8,4},{5,9},{9,5},{6,10},{10,6},{7,11},{11,7},{20,24},{24,20... | collective-permute-start | bytes 1671176 | tf_op jit(solution)/shard_map/ppermute | solution.py:1202
  335.5 17.4 %collective-permute-start.75 = (bf16[1472,128]{1,0:T(8,128)(2,1)S(1)}, bf16[1472,128]{1,0:T(8,128)(2,1)S(1)}, u32[]{:S(2)}, u32[]{:S(2)}) collective-permute-start(bf16[1472,128]{1,0:T(8,128)(2,1)S(1)} %get-tuple-element.679), channel_id=1, source_target_pairs={{0,2},{1,3},{2,0},{3,1},{4,6},{5,7},{6,4},{7,5},{8,10},{9,11},{10,... | collective-permute-start | bytes 1130504 | tf_op jit(solution)/shard_map/ppermute | solution.py:1067
  436.8 22.8 %collective-permute-start.106 = (bf16[8464,128]{1,0:T(8,128)(2,1)S(1)}, bf16[8464,128]{1,0:T(8,128)(2,1)S(1)}, u32[]{:S(2)}, u32[]{:S(2)}) collective-permute-start(bf16[8464,128]{1,0:T(8,128)(2,1)S(1)} %collect_feed.3.refs_0_), channel_id=1, source_target_pairs={{16,0},{17,1},{18,2},{19,3},{20,4},{21,5},{22,6},{23,7},{24,8},{25... | collective-permute-start | bytes 6500360 | tf_op jit(solution)/shard_map/ppermute | solution.py:1253
  438.3 21.4 %collective-permute-start.109 = (bf16[4352,128]{1,0:T(8,128)(2,1)S(1)}, bf16[4352,128]{1,0:T(8,128)(2,1)S(1)}, u32[]{:S(2)}, u32[]{:S(2)}) collective-permute-start(bf16[4352,128]{1,0:T(8,128)(2,1)S(1)} %collect_mix.3.refs_4_), channel_id=1, source_target_pairs={{0,16},{1,17},{2,18},{3,19},{4,20},{5,21},{6,22},{7,23},{8,24},{9,... | collective-permute-start | bytes 3342344 | tf_op jit(solution)/shard_map/ppermute | solution.py:1253
  441.6 18.0 %collective-permute-start.105 = (bf16[2176,128]{1,0:T(8,128)(2,1)S(1)}, bf16[2176,128]{1,0:T(8,128)(2,1)S(1)}, u32[]{:S(2)}, u32[]{:S(2)}) collective-permute-start(bf16[2176,128]{1,0:T(8,128)(2,1)S(1)} %add_convert_fusion), channel_id=1, source_target_pairs={{4,0},{8,12},{5,1},{9,13},{6,2},{10,14},{7,3},{11,15},{20,16},{24,... | collective-permute-start | bytes 1671176 | tf_op jit(solution)/shard_map/ppermute | solution.py:1200
  461.1 23.2 %collective-permute-start.110 = (bf16[2,128,1024]{2,1,0:T(8,128)(2,1)S(1)}, bf16[2,128,1024]{2,1,0:T(8,128)(2,1)S(1)}, u32[]{:S(2)}, u32[]{:S(2)}) collective-permute-start(bf16[2,128,1024]{2,1,0:T(8,128)(2,1)S(1)} %pad_maximum_fusion), channel_id=1, source_target_pairs={{0,0},{1,4},{2,8},{3,12},{4,1},{5,5},{6,9},{7,13},{8,2},{9,6},{10,... | collective-permute-start | bytes 1572872 | tf_op jit(solution)/shard_map/ppermute | solution.py:1119
  (166 other events, 2286.5 us)
